TPU v7x, 32 devices: a whole 2x2x4 slice. The times are simulated.
32 devices in a mesh: dp: 8 (over y, x, core), fsdp: 4 (over z).
Axes of the slice: x: 2, y: 2, z: 4, core: 2. Of those that a mesh axis runs over, the one named last changes fastest.
Arguments:
- tokens: bfloat16 [8, 1536, 960], P('dp', 'fsdp'), may hold values from -6 to 6
- lengths: int32 [8], P('dp'), may hold values from 1153 to 1536, as said below
- cotangent: bfloat16 [8, 1536, 960], P('dp', 'fsdp'), may hold values from -6 to 6
- attention_gain: bfloat16 [960], P('fsdp'), may hold values from 0.5 to 1.5
- feedforward_gain: bfloat16 [960], P('fsdp'), may hold values from 0.5 to 1.5
- query_weight: bfloat16 [960, 960], P('fsdp'), may hold values from -0.1875 to 0.1875
- key_weight: bfloat16 [960, 320], P('fsdp'), may hold values from -0.1875 to 0.1875
- value_weight: bfloat16 [960, 320], P('fsdp'), may hold values from -0.1875 to 0.1875
- out_weight: bfloat16 [960, 960], P('fsdp'), may hold values from -3.5 to 3.5
- gate_weight: bfloat16 [960, 2560], P('fsdp'), may hold values from -0.1875 to 0.1875
- up_weight: bfloat16 [960, 2560], P('fsdp'), may hold values from -0.1875 to 0.1875
- down_weight: bfloat16 [2560, 960], P('fsdp'), may hold values from -0.125 to 0.125
Outputs:
- output: bfloat16 [8, 1536, 960], P('dp', 'fsdp')
- grad_tokens: bfloat16 [8, 1536, 960], P('dp', 'fsdp')
- grad_attention_gain: float32 [960], P('fsdp')
- grad_feedforward_gain: float32 [960], P('fsdp')
- grad_query_weight: float32 [960, 960], P('fsdp')
- grad_key_weight: float32 [960, 320], P('fsdp')
- grad_value_weight: float32 [960, 320], P('fsdp')
- grad_out_weight: float32 [960, 960], P('fsdp')
- grad_gate_weight: float32 [960, 2560], P('fsdp')
- grad_up_weight: float32 [960, 2560], P('fsdp')
- grad_down_weight: float32 [2560, 960], P('fsdp')
Inputs may be any that keep to these rules, and one draw needn't show every extreme that they name: `lengths`: every length exceeds 1536 - 384, and some sequence has all 1536 positions real.
All inputs are finite; a program needn't handle non-finite values.
Results may differ from a plain program's by a relative error of at most 0.028.
Values may be sent and summed in bfloat16 or wider, within the bound.
No kernel may reach another device: no remote copies, remote signals or barrier semaphores. Data moves between devices by JAX's collectives and lax.ppermute only.
A program may use at most 256 MiB of HBM per device.

v0:
```python
import jax
import jax.numpy as jnp
from jax import lax
from jax.experimental import pallas as pl
from jax.experimental.pallas import tpu as pltpu
from jax.sharding import PartitionSpec as P

HEADS = 15
KV_HEADS = 5
HD = 64
GROUP = HEADS // KV_HEADS
KV = KV_HEADS * HD

norm_epsilon = 1e-05
rotary_base = 10000.0

bf16 = jnp.bfloat16
f32 = jnp.float32


def first_hop(i):
    return i ^ (4 if i & 1 else 2)


def second_hop(i):
    return i ^ (2 if i & 1 else 4)


def sibling(i):
    return i ^ 1


def swap(value, hop):
    count = lax.axis_size("dp")
    return lax.ppermute(value, "dp", [(i, hop(i)) for i in range(count)])


def climb(value, step):
    count = lax.axis_size("fsdp")
    return lax.ppermute(value, "fsdp", [(i, i + 1) for i in range(step - 1, count - 1)])


def descend(value, step):
    count = lax.axis_size("fsdp")
    return lax.ppermute(value, "fsdp", [(i, i - 1) for i in range(1, count - step + 1)])


def place():
    low = lax.axis_index("dp") % 8
    core = low % 2
    one = jnp.where(core == 1, 4, 2)
    return low, core, one, 6 - one


def around(value, distance):
    count = lax.axis_size("fsdp")
    return lax.ppermute(value, "fsdp", [(i, (i + distance) % count) for i in range(count)])


def together(*values):
    return lax.optimization_barrier(values)


def call(kernel, operands, wait_for=(), scalars=0, in_specs=(), grid=(), **rest):
    wait_for = jax.tree.leaves(wait_for)
    last = len(operands)

    def waiting(*refs):
        kernel(*refs[:last], *refs[last + len(wait_for) :])

    in_specs = list(in_specs) + [pl.BlockSpec(memory_space=pl.ANY)] * len(wait_for)
    where = dict(in_specs=in_specs, out_specs=rest.pop("out_specs"))
    scratch = rest.pop("scratch_shapes", ())
    if scalars:
        where = dict(
            grid_spec=pltpu.PrefetchScalarGridSpec(
                num_scalar_prefetch=scalars, grid=grid, scratch_shapes=scratch, **where
            )
        )
    else:
        where.update(grid=grid, scratch_shapes=scratch)
    return pl.pallas_call(waiting, **where, **rest)(*operands, *wait_for)


class Gather:
    def __init__(self, blocks):
        self.blocks = blocks

    def hop(self):
        self.mine = jnp.stack(self.blocks)
        self.a = swap(self.mine, first_hop)
        self.b = swap(self.mine, second_hop)

    def hop_on(self):
        self.ab = swap(self.a, second_hop)

    def cross(self):
        mine = [self.mine, self.a, self.b, self.ab]
        return mine + [swap(v, sibling) for v in mine]


def other_blocks(own):
    return [around(own, o) for o in range(1, lax.axis_size("fsdp"))]


def piece_ids(low):
    odd = low % 2
    one = 2 + 2 * odd
    two = 6 - one
    return [low, low ^ one, low ^ two, low ^ 6, low ^ 1, low ^ 1 ^ two, low ^ 1 ^ one, low ^ 7]


def lay_out(low, pieces, own, out_shapes, moves, wait_for=()):
    count = lax.axis_size("fsdp")
    where = jnp.stack([lax.axis_index("fsdp"), low]).astype(jnp.int32)

    def kernel(where_ref, *refs):
        piece_refs, refs = refs[:8], refs[8:]
        own_refs, refs = refs[: len(own)], refs[len(own) :]
        outs = refs
        z, low = where_ref[0], where_ref[1]
        for core in range(2):

            @pl.when(low % 2 == core)
            def _():
                copies = []
                for k, pid in enumerate(piece_ids(low)):
                    own_core = core if k < 4 else 1 - core
                    for o in range(count - 1):
                        block = lax.rem(z + count - 1 - o, count)
                        copies += moves(piece_refs[k].at[o], block, pid // 2, own_core, pid, outs)
                for source, target in copies + own_moves(own_refs, z, outs):
                    target[...] = source[...]

    moves, own_moves = moves
    vmem = pl.BlockSpec(memory_space=pltpu.VMEM)
    return call(
        kernel,
        [where, *pieces, *own],
        wait_for,
        in_specs=[pl.BlockSpec(memory_space=pltpu.SMEM)] + [vmem] * (8 + len(own)),
        out_specs=[vmem] * len(out_shapes),
        out_shape=[jax.ShapeDtypeStruct(shape, bf16) for shape in out_shapes],
        compiler_params=pltpu.CompilerParams(vmem_limit_bytes=26 * 2**20),
        name="lay_out",
        cost_estimate=cost(5),
    )


def rows_at(start, size):
    return pl.ds(pl.multiple_of(start, 16), size)


def lanes_at(start, size):
    return pl.ds(start if isinstance(start, int) else pl.multiple_of(start, 128), size)


def projection_piece(shard, low, core):
    block, width = shard.shape
    rest = block // 2 // 16 * 16
    lanes = width // 4
    return lax.dynamic_slice(shard, (core * rest, low // 2 * lanes), (block - rest, lanes))


def gate_up_piece(gate, up, low, core):
    lanes = gate.shape[1] // 4
    gate, up = (lax.dynamic_slice_in_dim(v, low // 2 * lanes, lanes, 1) for v in (gate, up))
    return jnp.where(core == 1, up, gate)


def down_piece(shard, low):
    rows = shard.shape[0] // 8
    return lax.dynamic_slice_in_dim(shard, low * rows, rows, 0)


def whole_projections(shard, low, pieces, wait_for):
    count = lax.axis_size("fsdp")
    block, width = shard.shape
    lanes = width // 4
    rest = block // 2 // 16 * 16
    held = block - rest

    def moves(src, z, q, c, pid, outs):
        size = held if c else rest
        return [
            (
                src.at[pl.ds(0, size)],
                outs[0].at[rows_at(z * block + c * rest, size), lanes_at(q * lanes, lanes)],
            )
        ]

    def own_moves(refs, z, outs):
        return [(refs[0], outs[0].at[rows_at(z * block, block)])]

    return lay_out(
        low, pieces, [shard], [(count * block, width)], (moves, own_moves), wait_for
    )[0]


def whole_gate_up(gate, up, low, pieces):
    count = lax.axis_size("fsdp")
    block, width = gate.shape
    lanes = width // 4

    def moves(src, z, q, c, pid, outs):
        return [(src, outs[c].at[rows_at(z * block, block), lanes_at(q * lanes, lanes)])]

    def own_moves(refs, z, outs):
        return [(refs[k], outs[k].at[rows_at(z * block, block)]) for k in range(2)]

    return lay_out(low, pieces, [gate, up], [(count * block, width)] * 2, (moves, own_moves))


def whole_down(shard, low, pieces):
    count = lax.axis_size("fsdp")
    block, width = shard.shape
    rows = block // 8

    def moves(src, z, q, c, pid, outs):
        return [(src, outs[0].at[rows_at(z * block + pid * rows, rows)])]

    def own_moves(refs, z, outs):
        return [(refs[0], outs[0].at[rows_at(z * block, block)])]

    return lay_out(low, pieces, [shard], [(count * block, width)], (moves, own_moves))[0]


def all_blocks(others, own):
    count = lax.axis_size("fsdp")
    z = lax.axis_index("fsdp")
    both = jnp.concatenate([own[None], others])
    return jnp.stack(
        [
            lax.dynamic_index_in_dim(both, (k - z + count) % count, 0, keepdims=False)
            for k in range(count)
        ]
    )


def add(*terms):
    return sum(v.astype(f32) for v in terms).astype(bf16)


def cost(us, weight=20):
    return pl.CostEstimate(
        flops=int(us * weight * 1.15e9), bytes_accessed=0, transcendentals=0
    )


HEAVY = 20


class Reduction:
    def __init__(self, send):
        self.got = swap(send, sibling)

    def hop(self, away, near, far):
        self.near, self.far = near, far
        self.came = swap(away, first_hop)

    def hop_on(self):
        self.add_up()
        self.go_on()

    def add_up(self):
        self.far = add(*self.far, self.came[1])
        self.near = add(*self.near, self.came[0])

    def go_on(self):
        self.came = swap(self.far, second_hop)

    def settle(self):
        count, z = lax.axis_size("fsdp"), lax.axis_index("fsdp")
        self.near = add(self.near, self.came)
        self.cuts = [
            lax.dynamic_index_in_dim(self.near, (z + o) % count, 0, keepdims=False)
            for o in range(count)
        ]

    def shift(self):
        count = lax.axis_size("fsdp")
        self.came = [around(self.cuts[o], o) for o in range(1, count)]

    def total(self):
        return over_rest(add(self.cuts[0], *self.came))


def over_rest(mine):
    wide = lax.axis_size("dp")
    if wide > 8:
        groups = [[i + 8 * k for k in range(wide // 8)] for i in range(8)]
        mine = lax.psum(mine, "dp", axis_index_groups=groups)
    return mine


def hand(mine):
    b = swap(mine, second_hop)
    a, ab = swap(mine, first_hop), swap(b, first_hop)
    return [mine, a, b, ab]


def give(handed):
    return handed + [swap(v, sibling) for v in handed]


def ids_of(low):
    one = 2 + 2 * (low % 2)
    return [low ^ one, low ^ 6, low, low ^ 6 ^ one]


def spread(low, pieces, out_shapes, put, wait_for=()):
    def turn_out(shape):
        wide, high = (-(-n // 128) * 128 for n in shape[::-1])
        return shape[0] * wide > shape[1] * high

    def kernel(where_ref, *refs):
        low = where_ref[0]
        outs, rest = list(refs[8 : 8 + len(out_shapes)]), list(refs[8 + len(out_shapes) :])
        targets = [rest.pop(0) if turn_out(s) else v for s, v in zip(out_shapes, outs)]
        for core in range(2):

            @pl.when(low % 2 == core)
            def _():
                for k, pid in enumerate(piece_ids(low)):
                    own_core = core if k < 4 else 1 - core
                    put(targets, pid // 2, own_core, pid, refs[k][...].astype(f32))

        for target, out in zip(targets, outs):
            if target is not out:
                out[...] = target[...].T

    vmem = pl.BlockSpec(memory_space=pltpu.VMEM)
    turned = [turn_out(shape) for shape in out_shapes]
    shapes = [shape[::-1] if t else shape for shape, t in zip(out_shapes, turned)]
    out = call(
        kernel,
        [low[None], *pieces],
        wait_for,
        in_specs=[pl.BlockSpec(memory_space=pltpu.SMEM)] + [vmem] * 8,
        out_specs=[vmem] * len(out_shapes),
        out_shape=[jax.ShapeDtypeStruct(shape, f32) for shape in shapes],
        scratch_shapes=[pltpu.VMEM(s, f32) for s, t in zip(out_shapes, turned) if t],
        compiler_params=pltpu.CompilerParams(vmem_limit_bytes=22 * 2**20),
        name="spread",
        cost_estimate=cost(3),
    )
    return [v.T if t else v for v, t in zip(out, turned)]


def grad_pieces(
    ids, got, operands, in_specs, compute, piece_shape, us, wait_for, vmem=56
):
    block = (1,) + piece_shape
    zeros = (0,) * len(piece_shape)
    in_specs, operands = list(in_specs), list(operands)
    n = len(ids)
    if got is None:
        out_specs = [pl.BlockSpec(block, lambda i, ids: (i,) + zeros)]
        out_shape = [jax.ShapeDtypeStruct((n,) + piece_shape, bf16)]
    else:
        in_specs.append(pl.BlockSpec(block, lambda i, ids: (i,) + zeros))
        operands.append(got)
        half = n // 2
        out_specs = [
            pl.BlockSpec(block, lambda i, ids: (jnp.minimum(i, half - 1),) + zeros),
            pl.BlockSpec(block, lambda i, ids: (jnp.maximum(i - half, 0),) + zeros),
        ]
        out_shape = [jax.ShapeDtypeStruct((half,) + piece_shape, bf16)] * 2

    out_specs.append(pl.BlockSpec((8, 128), lambda i, ids: (0, 0)))
    out_shape.append(jax.ShapeDtypeStruct((8, 128), f32))

    def kernel(ids_ref, *refs):
        step = pl.program_id(0)
        refs[-1][...] = jnp.zeros((8, 128), f32)
        refs = refs[:-1]
        if got is None:

            def put(total):
                refs[-1][...] = total.astype(bf16).reshape(block)

            compute(ids_ref[step], put, *refs[:-1])
        else:

            def put(total):
                total = (total + refs[-3][...].reshape(total.shape).astype(f32)).astype(bf16)

                @pl.when(step < half)
                def _():
                    refs[-2][...] = total.reshape(block)

                @pl.when(step >= half)
                def _():
                    refs[-1][...] = total.reshape(block)

            compute(ids_ref[step], put, *refs[:-3])

    return call(
        kernel,
        [jnp.stack(ids).astype(jnp.int32), *operands],
        wait_for,
        scalars=1,
        grid=(n,),
        in_specs=in_specs,
        out_specs=out_specs,
        out_shape=out_shape,
        compiler_params=pltpu.CompilerParams(vmem_limit_bytes=vmem * 2**20),
        name="weight_grad",
        cost_estimate=cost(us * n, HEAVY),
    )


def flat_product(pid, put, left_ref, right_ref):
    left, right = left_ref[...], right_ref[...]
    put(product(left.reshape(-1, left.shape[-1]), right.reshape(right.shape[-2:]), 1, 0))


def product(a, b, over_a, over_b):
    return lax.dot_general(
        a, b, (((over_a,), (over_b,)), ((), ())), preferred_element_type=f32
    )


def side_by_side(x):
    return jnp.concatenate([x[HD * g : HD * (g + 1)] for g in range(GROUP)], axis=1)


def diagonal_mask(scores, rows, room):
    key = lax.broadcasted_iota(jnp.int32, (rows, rows), 0)
    query = lax.broadcasted_iota(jnp.int32, (rows, rows), 1)
    seen = (key <= query) & (key < room)
    return jnp.where(jnp.concatenate([seen] * GROUP, axis=1), scores, -1e30)


SUMS = 16


def attend_kernel(d, n, place_ref, q_ref, *refs):
    joined = refs[0].shape[0] > KV
    k_ref, v_ref = refs[0], refs[0 if joined else 1]
    refs = refs[1 if joined else 2 :]
    first, last = d == 0, d == n - 1
    m1_ref, a1_ref = (None, None) if first else refs[:2]
    m2_ref, a2_ref = refs[-2:]
    z, room = place_ref[0], place_ref[1]
    rows = q_ref.shape[1]

    @pl.when(z >= d)
    def _():
        ones = jnp.ones((SUMS, rows), bf16)
        for h in range(KV_HEADS):
            q = side_by_side(q_ref[GROUP * HD * h : GROUP * HD * (h + 1), :])
            k = k_ref[HD * h : HD * (h + 1), :]
            start = HD * h + (KV if joined else 0)
            v = v_ref[start : start + HD, :]
            s = product(k, q, 0, 0)
            if first:
                s = diagonal_mask(s, rows, room)
            m = jnp.max(s, axis=0, keepdims=True)
            if not first:
                m = jnp.maximum(m, m1_ref[h])
            p = jnp.exp(s - m).astype(bf16)
            total = product(jnp.concatenate([v, ones], axis=0), p, 1, 0)
            if not first:
                total = total + a1_ref[h] * jnp.exp(m1_ref[h] - m)
            m2_ref[h] = m
            a2_ref[h] = total

    if not first:

        @pl.when(z < d)
        def _():
            m2_ref[...] = m1_ref[...]
            a2_ref[...] = a1_ref[...]

    if last:
        o_ref, lse_ref = refs[2:4]
        for h in range(KV_HEADS):
            l = a2_ref[h, HD : HD + 1, :]
            o = (a2_ref[h, :HD, :] / l).astype(bf16)
            lse = m2_ref[h] + jnp.log(l)
            for g in range(GROUP):
                here = slice(HD * (GROUP * h + g), HD * (GROUP * h + g + 1))
                o_ref[here, :] = o[:, rows * g : rows * (g + 1)]
                lse_ref[h, g : g + 1, :] = lse[:, rows * g : rows * (g + 1)]


def attend(d, n, where, q, kv, state, wait_for):
    rows = q.shape[1]
    state_shapes = [(KV_HEADS, 1, GROUP * rows), (KV_HEADS, HD + SUMS, GROUP * rows)]
    out_shape = [jax.ShapeDtypeStruct(shape, f32) for shape in state_shapes]
    scratch = []
    if d == n - 1:
        scratch = [pltpu.VMEM(shape, f32) for shape in state_shapes]
        out_shape = [
            jax.ShapeDtypeStruct(q.shape, bf16),
            jax.ShapeDtypeStruct((KV_HEADS, GROUP, rows), f32),
        ]
    vmem = pl.BlockSpec(memory_space=pltpu.VMEM)
    return call(
        lambda *refs: attend_kernel(d, n, *refs),
        [where, q, *kv, *state],
        wait_for,
        in_specs=[pl.BlockSpec(memory_space=pltpu.SMEM)] + [vmem] * (1 + len(kv) + len(state)),
        out_specs=[vmem, vmem],
        out_shape=out_shape,
        scratch_shapes=scratch,
        compiler_params=pltpu.CompilerParams(vmem_limit_bytes=24 * 2**20),
        name="attend",
        cost_estimate=cost(4),
    )


def specs(rows):
    return (
        pl.BlockSpec((GROUP * HD, rows), lambda h, s: (h, 0)),
        pl.BlockSpec((2, HD, rows), lambda h, s: (0, h, 0)),
        pl.BlockSpec((1, GROUP, rows), lambda h, s: (h, 0, 0)),
    )


def turn(columns, cosine, sine, heads):
    half = HD // 2
    parts = []
    for h in range(heads):
        a = columns[HD * h : HD * h + half]
        b = columns[HD * h + half : HD * (h + 1)]
        parts += [a * cosine - b * sine, b * cosine + a * sine]
    return jnp.concatenate(parts, axis=0)


def attend_back_kernel(d, place_ref, q_ref, o_ref, do_ref, lse_ref, k_ref, v_ref, *refs):
    dq_ref, dkv_ref = refs[-2:]
    before_ref = None if len(refs) == 2 else refs[-3]
    z, room = place_ref[0], place_ref[1]
    rows = q_ref.shape[1]

    @pl.when(z >= d)
    def _():
        q, do, o = (side_by_side(r[...]) for r in (q_ref, do_ref, o_ref))
        lse = jnp.concatenate([lse_ref[0, g : g + 1, :] for g in range(GROUP)], axis=1)
        delta = jnp.sum(do.astype(f32) * o.astype(f32), axis=0, keepdims=True)
        k, v = k_ref[...], v_ref[...]
        s = product(k, q, 0, 0)
        if d == 0:
            s = diagonal_mask(s, rows, room)
        p = jnp.exp(s - lse)
        dp = product(v, do, 0, 0)
        ds = (p * (dp - delta)).astype(bf16)
        dkv_ref[1] = product(p.astype(bf16), do, 1, 1).T.astype(bf16)
        dkv_ref[0] = product(ds, q, 1, 1).T.astype(bf16)
        dq = product(k, ds, 1, 0) * HD ** (-0.5)
        for g in range(GROUP):
            here = slice(HD * g, HD * (g + 1))
            part = dq[:, rows * g : rows * (g + 1)]
            if before_ref is not None:
                part = part + before_ref[here, :]
            if d == 0:
                part = turn(part, refs[0][...], -refs[1][...], 1).astype(bf16)
            dq_ref[here, :] = part

    if d > 0:

        @pl.when(z < d)
        def _():
            dkv_ref[...] = jnp.zeros(dkv_ref.shape, bf16)
            if before_ref is None:
                dq_ref[...] = jnp.zeros(dq_ref.shape, f32)
            else:
                dq_ref[...] = before_ref[...]


def attend_back(d, where, q, o, do, lse, kv, before, tables, wait_for):
    rows = q.shape[1]
    q_spec, kv_spec, lse_spec = specs(rows)
    k_spec = pl.BlockSpec((HD, rows), lambda h, s: (h, 0))
    skip = 0 if len(kv) > 1 else KV_HEADS
    v_spec = pl.BlockSpec((HD, rows), lambda h, s: (skip + h, 0))
    extra, extra_specs = [], []
    if d == 0:
        extra = list(tables)
        extra_specs = [pl.BlockSpec((HD // 2, rows), lambda h, s: (0, 0))] * 2
    if before is not None:
        extra.append(before)
        extra_specs.append(q_spec)
    return call(
        lambda *refs: attend_back_kernel(d, *refs),
        [where, q, o, do, lse, kv[0], kv[-1], *extra],
        wait_for,
        scalars=1,
        grid=(KV_HEADS,),
        in_specs=[q_spec, q_spec, q_spec, lse_spec, k_spec, v_spec] + extra_specs,
        out_specs=[q_spec, kv_spec],
        out_shape=[
            jax.ShapeDtypeStruct(q.shape, f32 if d else bf16),
            jax.ShapeDtypeStruct((2, KV, rows), bf16),
        ],
        compiler_params=pltpu.CompilerParams(vmem_limit_bytes=32 * 2**20),
        name="attend_back",
        cost_estimate=cost(7, HEAVY),
    )


def gradient_columns(own, got, dq, low, tables, wait_for):
    rows = dq.shape[1]
    lanes = 2 * KV + dq.shape[0] + low.shape[1]

    def kernel(own_ref, got_ref, dq_ref, low_ref, cos_ref, sin_ref, out_ref):
        dkv = own_ref[...].astype(f32) + got_ref[...].astype(f32)
        keys = turn(dkv[0], cos_ref[...], -sin_ref[...], KV_HEADS).astype(bf16)
        sides = jnp.concatenate([keys, dkv[1].astype(bf16), dq_ref[...]], axis=0)
        out_ref[...] = jnp.concatenate([sides.T, low_ref[...]], axis=1)

    vmem = pl.BlockSpec(memory_space=pltpu.VMEM)
    return call(
        kernel,
        [own, got, dq, low, *tables],
        wait_for,
        in_specs=[vmem] * 6,
        out_specs=vmem,
        out_shape=jax.ShapeDtypeStruct((rows, lanes), bf16),
        compiler_params=pltpu.CompilerParams(vmem_limit_bytes=16 * 2**20),
        name="gradient_columns",
        cost_estimate=cost(0.01),
    )


def dot(a, b, pattern):
    return jnp.einsum(pattern, a, b, preferred_element_type=f32)


def normalize(x, gain):
    scale = lax.rsqrt(jnp.mean(x * x, axis=-1, keepdims=True) + norm_epsilon)
    unit = x * scale
    return (unit * gain).astype(bf16), unit, scale


def normalize_back(grad, gain, unit, scale):
    grad_unit = grad * gain
    return scale * (grad_unit - unit * jnp.mean(grad_unit * unit, axis=-1, keepdims=True))


def feed_forward_kernel(x_ref, mix_ref, wo_ref, gain_ref, wg_ref, wu_ref, wd_ref, *refs):
    result_ref, hidden_ref, gate_ref, up_ref, nft_ref, active_ref, nf_ref = refs[-7:]

    @pl.when(pl.program_id(0) == 0)
    def _():
        hidden = x_ref[...] + product(mix_ref[...], wo_ref[...], 0, 0)
        hidden_ref[...] = hidden
        normed, _, _ = normalize(hidden, gain_ref[...])
        nf_ref[...] = normed
        nft_ref[...] = normed.T
        result_ref[...] = hidden

    normed = nf_ref[...]
    gate = product(normed, wg_ref[...], 1, 0)
    up = product(normed, wu_ref[...], 1, 0)
    active = (gate * jax.nn.sigmoid(gate) * up).astype(bf16)
    gate_ref[...] = gate.astype(bf16)
    up_ref[...] = up.astype(bf16)
    active_ref[...] = active.T
    result_ref[...] += product(active, wd_ref[...], 1, 0)


def feed_forward(x, mixture, w_o, gain, w_gate, w_up, w_down, kept):
    rows, model = x.shape
    hidden_units = w_gate.shape[1]
    tile = hidden_units // 5
    half = 0 if kept else 1
    whole = lambda *shape: pl.BlockSpec(shape, lambda i: (0,) * len(shape))
    wide = lambda n: pl.BlockSpec((n, tile), lambda i: (0, i))
    return pl.pallas_call(
        feed_forward_kernel,
        grid=(5,),
        in_specs=[
            whole(rows, model), whole(model, rows), whole(model, model), whole(1, model),
            wide(model), wide(model), pl.BlockSpec((tile, model), lambda i: (i, 0)),
        ]
        + [pl.BlockSpec(memory_space=pl.ANY)] * len(kept),
        out_specs=[
            whole(rows, model), whole(rows, model), wide(rows), wide(rows),
            pl.BlockSpec((model, rows), lambda i: (0, half)),
            pl.BlockSpec((tile, rows), lambda i: (i, half)),
        ],
        out_shape=[
            jax.ShapeDtypeStruct((rows, model), f32),
            jax.ShapeDtypeStruct((rows, model), f32),
            jax.ShapeDtypeStruct((rows, hidden_units), bf16),
            jax.ShapeDtypeStruct((rows, hidden_units), bf16),
            jax.ShapeDtypeStruct((model, 2 * rows), bf16),
            jax.ShapeDtypeStruct((hidden_units, 2 * rows), bf16),
        ],
        scratch_shapes=[pltpu.VMEM((rows, model), bf16)],
        input_output_aliases={7: 4, 8: 5} if kept else {},
        compiler_params=pltpu.CompilerParams(vmem_limit_bytes=48 * 2**20),
        name="feed_forward",
        cost_estimate=cost(12),
    )(x, mixture, w_o, gain[None], w_gate, w_up, w_down, *kept)


def feed_forward_back_kernel(grad_ref, hidden_ref, gain_ref, gate_ref, up_ref, wg_ref, wu_ref,
                             wd_ref, wo_ref, *refs):
    d_gu_ref, d_hidden_ref, low_ref, d_mix_ref, total_ref = refs[-5:]
    step = pl.program_id(0)
    low = grad_ref[...].astype(bf16)
    d_active = product(low, wd_ref[...], 1, 1)
    gate, up = gate_ref[...].astype(f32), up_ref[...].astype(f32)
    sig = jax.nn.sigmoid(gate)
    d_gate = (d_active * up * sig * (1.0 + gate * (1.0 - sig))).astype(bf16)
    d_up = (d_active * gate * sig).astype(bf16)
    d_gu_ref[0] = d_gate
    d_gu_ref[1] = d_up
    term = product(d_gate, wg_ref[...], 1, 1) + product(d_up, wu_ref[...], 1, 1)

    @pl.when(step == 0)
    def _():
        total_ref[...] = term

    @pl.when(step > 0)
    def _():
        total_ref[...] += term

    @pl.when(step == pl.num_programs(0) - 1)
    def _():
        hidden = hidden_ref[...]
        scale = lax.rsqrt(jnp.mean(hidden * hidden, axis=-1, keepdims=True) + norm_epsilon)
        d_norm = normalize_back(total_ref[...], gain_ref[...], hidden * scale, scale)
        d_hidden = grad_ref[...] + d_norm
        d_hidden_ref[...] = d_hidden
        low = d_hidden.astype(bf16)
        low_ref[...] = low
        d_mix_ref[...] = product(wo_ref[...], low, 1, 1).astype(bf16)


def feed_forward_back(
    grad, hidden, gain, gate, up, w_gate, w_up, w_down, w_o, kept, wait_for=()
):
    rows, model = grad.shape
    half = 1 if kept else 0
    hidden_units = gate.shape[1]
    tile = hidden_units // 5
    whole = lambda *shape: pl.BlockSpec(shape, lambda i: (0,) * len(shape))
    wide = lambda n: pl.BlockSpec((n, tile), lambda i: (0, i))
    return call(
        feed_forward_back_kernel,
        [grad, hidden, gain[None], gate, up, w_gate, w_up, w_down, w_o, *kept],
        wait_for,
        grid=(5,),
        in_specs=[
            whole(rows, model), whole(rows, model), whole(1, model), wide(rows), wide(rows),
            wide(model), wide(model), pl.BlockSpec((tile, model), lambda i: (i, 0)),
            whole(model, model),
        ]
        + [pl.BlockSpec(memory_space=pl.ANY)] * len(kept),
        out_specs=[
            pl.BlockSpec((2, rows, tile), lambda i: (0, half, i)),
            whole(rows, model), whole(rows, model), whole(model, rows),
        ],
        out_shape=[
            jax.ShapeDtypeStruct((2, 2 * rows, hidden_units), bf16),
            jax.ShapeDtypeStruct((rows, model), f32),
            jax.ShapeDtypeStruct((rows, model), bf16),
            jax.ShapeDtypeStruct((model, rows), bf16),
        ],
        scratch_shapes=[pltpu.VMEM((rows, model), f32)],
        input_output_aliases={9: 0} if kept else {},
        compiler_params=pltpu.CompilerParams(vmem_limit_bytes=48 * 2**20),
        name="feed_forward_back",
        cost_estimate=cost(18, HEAVY),
    )


def project(normed, w, first, lanes, cosine, sine, heads, scale, name, wait_for=(), split=True):
    rows, model = normed.shape

    cuts = [heads * HD, lanes - heads * HD]
    cuts = [n for n in cuts if n] if split else [lanes]

    def kernel(x_ref, w_ref, cos_ref, sin_ref, out_ref, *rest_ref):
        y = product(x_ref[...], w_ref[:, first : first + lanes], 1, 0).T
        turned = turn(y[: heads * HD], cos_ref[...], sin_ref[...], heads)
        out_ref[: heads * HD, :] = turned.astype(bf16) * bf16(scale)
        if heads * HD < lanes:
            ref, start = (rest_ref[0], 0) if split else (out_ref, heads * HD)
            ref[start:, :] = y[heads * HD :].astype(bf16)

    whole = lambda *shape: pl.BlockSpec(shape, lambda i: (0,) * len(shape))
    width = first + lanes if (first + lanes) % 128 == 0 else w.shape[1]
    return call(
        kernel,
        [normed, w, cosine, sine],
        wait_for,
        grid=(1,),
        in_specs=[
            whole(rows, model), whole(model, width), whole(HD // 2, rows), whole(HD // 2, rows)
        ],
        out_specs=[whole(n, rows) for n in cuts],
        out_shape=[jax.ShapeDtypeStruct((n, rows), bf16) for n in cuts],
        compiler_params=pltpu.CompilerParams(vmem_limit_bytes=24 * 2**20),
        name=name,
        cost_estimate=cost(2),
    )


def projected_kv(normed, projections, tables, split):
    return project(
        normed, projections, 0, 2 * KV, *tables, KV_HEADS, 1.0, "keys_values", (), split
    )


def projected_q(normed, projections, tables, wait_for):
    first, lanes = 2 * KV, HEADS * HD
    return project(
        normed, projections, first, lanes, *tables, HEADS, HD**-0.5, "queries", wait_for
    )[0]


def attention(normed, kv, projections, where, tables, before):
    count = lax.axis_size("fsdp")
    kvs = [kv]
    for step in range(1, count):
        kvs.append([climb(v, step) for v in kvs[-1]])
    q = projected_q(normed, projections, tables, kv[:1])
    state = []
    for d in range(count):
        wait_for = ()
        if d in before:
            wait_for, state = before[d](state)
        state = attend(d, count, where, q, kvs[d], state, wait_for)
    return q, kvs, state


def attention_gradient(d_mixture, low, saved, where, tables, before, at_end):
    q, kvs, (mixture, lse) = saved[1:]
    count = lax.axis_size("fsdp")
    dq = moving = got = None
    for d in reversed(range(count)):
        step = count - 1 - d
        wait_for = []
        if d in before:
            wait_for, dq = before[d](dq)
        if step:
            got = lax.ppermute(
                moving, "fsdp", [(i, i - 1) for i in range(count - step, count)]
            )
        dq, dkv = attend_back(
            d, where, q, mixture, d_mixture, lse, kvs[d], dq, tables, wait_for
        )
        if d:
            moving = add(dkv, got) if step else dkv
    wait_for, dq = at_end(dq)
    return gradient_columns(dkv, got, dq, low, tables, wait_for)


def layer_gradient(d_hidden, columns, norm, gain, w_qkv):
    normed, unit, scale = norm
    d_normed = dot(columns[:, : w_qkv.shape[1]], w_qkv, "tf,df->td")
    return d_hidden + normalize_back(d_normed, gain, unit, scale)


def local(
    tokens,
    lengths,
    cotangent,
    attention_gain,
    feedforward_gain,
    query_weight,
    key_weight,
    value_weight,
    out_weight,
    gate_weight,
    up_weight,
    down_weight,
):
    rows = tokens.shape[1]
    count = lax.axis_size("fsdp")
    z = lax.axis_index("fsdp")
    low, core, one, two = place()
    positions = z * rows + jnp.arange(rows, dtype=jnp.int32)
    length = lengths[0]
    where = jnp.stack([z, length - z * rows]).astype(jnp.int32)
    frequency = rotary_base ** (-jnp.arange(HD // 2, dtype=f32) * 2.0 / HD)
    angles = frequency[:, None] * positions.astype(f32)[None, :]
    tables = (jnp.cos(angles), jnp.sin(angles))
    block = query_weight.shape[0]
    model = block * count
    hidden_units = gate_weight.shape[1]

    projections = jnp.concatenate([key_weight, value_weight, query_weight, out_weight], axis=1)
    lanes = projections.shape[1] // 4
    f_lanes = hidden_units // 4
    down_rows = down_weight.shape[0] // 8
    own_gains = jnp.stack([attention_gain, feedforward_gain])
    piece = projection_piece(projections, low, core)
    held = piece.shape[0]
    own = lax.optimization_barrier(
        (
            jnp.concatenate([piece, jnp.pad(own_gains, ((0, 14), (0, lanes - block)))]),
            gate_up_piece(gate_weight, up_weight, low, core),
            down_piece(down_weight, low),
        )
    )
    blocks = other_blocks(own[0])
    gains = all_blocks(jnp.stack([v[held : held + 2, :block] for v in blocks[::-1]]), own_gains)
    to_proj = Gather([v[:held] for v in blocks])
    to_proj.hop()
    to_proj.hop_on()
    rest = jnp.pad(own[2][:, f_lanes:], ((0, 0), (0, 2 * f_lanes - model)))
    wide = jnp.concatenate([own[1], own[2][:, :f_lanes], rest])
    wide = lax.all_gather(wide, "fsdp")
    wide = [
        lax.dynamic_index_in_dim(wide, (z + count - o) % count, 0, keepdims=False)
        for o in range(1, count)
    ]
    to_gate_up = Gather([v[:block] for v in wide])
    to_down = Gather(
        [
            jnp.concatenate(
                [v[block : block + down_rows], v[block + down_rows :, : model - f_lanes]], axis=1
            )
            for v in wide
        ]
    )
    to_gate_up.hop()
    to_down.hop()
    gains = jnp.moveaxis(gains, 0, 1).reshape(2, model).astype(f32)
    projections = whole_projections(
        projections, low, to_proj.cross(), [to_gate_up.mine, to_down.mine]
    )
    w_qkv = projections[:, : 2 * KV + model]

    start = tokens[0].astype(f32)
    norm_1 = normalize(start, gains[0])
    normed = norm_1[0]
    kv = projected_kv(normed, projections, tables, False)


    def first_arrived(state):
        here = (to_gate_up.a, to_gate_up.b, to_down.a, to_down.b)
        state, here = together(state, here)
        to_gate_up.a, to_gate_up.b, to_down.a, to_down.b = here
        to_gate_up.hop_on()
        to_down.hop_on()
        return (), state

    def second_arrived(state):
        state, here = together(state, (to_gate_up.ab, to_down.ab))
        to_gate_up.ab, to_down.ab = here
        return (), state

    saved_first = (norm_1,) + attention(
        normed, kv, projections, where, tables,
        {2: first_arrived, 3: second_arrived},
    )
    mixture = saved_first[3][0]
    w_o = projections[:, 2 * KV + model :]
    w_down = whole_down(down_weight, low, to_down.cross())
    w_gate, w_up = whole_gate_up(gate_weight, up_weight, low, to_gate_up.cross())
    middle, hidden_1, gate_1, up_1, *kept = feed_forward(
        start, mixture, w_o, gains[1], w_gate, w_up, w_down, []
    )

    norm_2 = normalize(middle, gains[0])
    kv = projected_kv(norm_2[0], projections, tables, True)
    half_rows = block // 2

    def left_of(normed, mixture):
        rows_of = jnp.stack([normed.T, mixture]).reshape(2, count, 2, half_rows, rows)
        return jnp.pad(rows_of, ((0, 0),) * 3 + ((0, held - half_rows), (0, 0)))

    left_1 = left_of(norm_1[0], mixture)
    saved_second = (norm_2,) + attention(
        norm_2[0], kv, projections, where, tables, {1: lambda state: (left_1, state)}
    )
    final, hidden_2, gate_2, up_2, nft, active = feed_forward(
        middle, saved_second[3][0], w_o, gains[1], w_gate, w_up, w_down, kept
    )

    real = (positions < length).astype(f32)
    gradient = cotangent[0].astype(f32) * real[:, None]
    down_back = (gradient.astype(bf16),)
    left = jnp.concatenate([left_of(norm_2[0], saved_second[3][0]), left_1], axis=-1)
    d_gu, d_hidden, low_2, d_mixture = feed_forward_back(
        gradient, hidden_2, gains[1], gate_2, up_2, w_gate, w_up, w_down, w_o, [], [left]
    )
    columns_2 = attention_gradient(
        d_mixture, low_2, saved_second, where, tables, {}, lambda dq: ((), dq)
    )
    gradient = layer_gradient(d_hidden, columns_2, norm_2, gains[0], w_qkv)

    down_back = jnp.concatenate(down_back + (gradient.astype(bf16),))
    active = active.reshape(count, 8, down_rows, 2 * rows)
    theirs, ours = ids_of(low ^ 1), ids_of(low)

    def down_pieces(ids, got, wait_for):
        return grad_pieces(
            ids, got, [active, down_back],
            [
                pl.BlockSpec((count, 1, down_rows, 2 * rows), lambda i, ids: (0, ids[i], 0, 0)),
                pl.BlockSpec((2 * rows, model), lambda i, ids: (0, 0)),
            ],
            flat_product, (count, down_rows, model), 1.4, wait_for,
        )

    send, token = down_pieces(theirs, None, ())
    to_down = Reduction(send)
    away, home, token = down_pieces(ours, to_down.got, [token])
    to_down.hop(away, [home[0]], [home[1]])
    d_gu, d_hidden, low_1, d_mixture = feed_forward_back(
        gradient, hidden_1, gains[1], gate_1, up_1, w_gate, w_up, w_down, w_o, [d_gu], [token]
    )

    def gate_up_pieces(ids, got, wait_for):
        return grad_pieces(
            ids, got, [nft, d_gu],
            [
                pl.BlockSpec((model, 2 * rows), lambda i, ids: (0, 0)),
                pl.BlockSpec(
                    (1, 2 * rows, f_lanes), lambda i, ids: (ids[i] % 2, 0, ids[i] // 2)
                ),
            ],
            flat_product, (count, block, f_lanes), 2.2, wait_for,
        )

    send, token = gate_up_pieces(theirs, None, ())
    to_gate_up = Reduction(send)
    to_down.came, d_hidden = together(to_down.came, d_hidden)
    to_down.hop_on()

    def third(dq):
        return [token], dq

    def second(dq):
        away, home, token = gate_up_pieces(ours, to_gate_up.got, [dq])
        to_gate_up.hop(away, [home[0]], [home[1]])
        dq, to_down.came = together(dq, to_down.came)
        to_down.settle()
        return [token], dq

    def zeroth(dq):
        dq, to_gate_up.came = together(dq, to_gate_up.came)
        to_gate_up.add_up()
        dq, to_gate_up.far, to_down.cuts = together(dq, to_gate_up.far, to_down.cuts)
        to_gate_up.go_on()
        to_down.shift()
        return (), dq

    columns_1 = attention_gradient(
        d_mixture, low_1, saved_first, where, tables,
        {3: third, 2: second, 0: zeroth}, lambda dq: ((), dq),
    )
    columns_1, to_gate_up.came, to_down.came = together(
        columns_1, to_gate_up.came, to_down.came
    )
    to_gate_up.settle()
    to_gate_up.shift()

    def compute_proj(pid, put, a, b, right_2, right_1):
        right = jnp.concatenate([right_2[...], right_1[...]], axis=0)

        def product_of(ref):
            total = product(ref[...].reshape(count * held, 2 * rows), right, 1, 0)
            return total.reshape(count, held, lanes)[:, :half_rows]

        @pl.when(pid // 2 != 2)
        def _():
            put(product_of(a))

        @pl.when(pid // 2 == 2)
        def _():
            lane = lax.broadcasted_iota(jnp.int32, (count, half_rows, lanes), 2)
            put(jnp.where(lane < lanes // 2, product_of(a), product_of(b)))

    def proj_pieces(ids, wait_for, us):
        def left_spec(k):
            return pl.BlockSpec(
                (1, count, 1, held, 2 * rows),
                lambda i, ids: (jnp.where(ids[i] // 2 * 2 + k > 4, 1, 0), 0, ids[i] % 2, 0, 0),
            )

        right_spec = pl.BlockSpec((rows, lanes), lambda i, ids: (0, ids[i] // 2))
        return grad_pieces(
            ids, None, [left, left, columns_2, columns_1],
            [left_spec(0), left_spec(1), right_spec, right_spec],
            compute_proj, (count, half_rows, lanes), us, wait_for, 24,
        )

    send, token = proj_pieces(theirs, to_gate_up.cuts[0], 2)
    to_proj = Reduction(send)
    keep, token = proj_pieces(ours, [token], 0.01)
    down_handed = hand(to_down.total())
    keep, down_handed[1:3] = together(keep, down_handed[1:3])
    down_handed[3] = swap(down_handed[2], first_hop)
    got = to_proj.got
    to_proj.hop(add(keep[:2], got[:2]), [keep[2], got[2]], [keep[3], got[3]])
    (
        to_proj.came, to_gate_up.came[0], to_gate_up.came[2], down_handed[3]
    ) = together(
        to_proj.came, to_gate_up.came[0], to_gate_up.came[2], down_handed[3]
    )
    to_proj.hop_on()
    to_proj.settle()
    to_proj.cuts, to_gate_up.came[1] = together(to_proj.cuts, to_gate_up.came[1])
    gate_up_handed = hand(to_gate_up.total())
    to_proj.shift()
    proj_mine, gate_up_handed[1:] = together(to_proj.total(), gate_up_handed[1:])
    gradient = layer_gradient(d_hidden, columns_1, norm_1, gains[0], w_qkv)
    g_down = give(down_handed)
    proj_handed = hand(proj_mine)
    gate_up_handed[0], proj_handed[2] = together(gate_up_handed[0], proj_handed[2])
    proj_handed[3] = swap(proj_handed[2], first_hop)
    g_gate_up = give(gate_up_handed)

    def put_down(refs, q, c, pid, value):
        refs[0][pl.ds(pl.multiple_of(pid * down_rows, 8), down_rows), :] = value

    def put_gate_up(refs, q, c, pid, value):
        refs[c][:, lanes_at(q * f_lanes, f_lanes)] = value

    widths = [KV, KV, model, model]

    def put_proj(refs, q, c, pid, value):
        here = slice(c * half_rows, (c + 1) * half_rows)
        for quarter in range(4):

            @pl.when(q == quarter)
            def _():
                first = 0
                for ref, width in zip(refs, widths):
                    start = max(first, quarter * lanes)
                    stop = min(first + width, (quarter + 1) * lanes)
                    if start < stop:
                        ref[here, start - first : stop - first] = value[
                            :, start - quarter * lanes : stop - quarter * lanes
                        ]
                    first += width

    g_down = spread(low, g_down, [(8 * down_rows, model)], put_down)[0]
    g_gate, g_up = spread(low, g_gate_up, [(block, hidden_units)] * 2, put_gate_up)
    g_gate, g_up, proj_handed[3] = together(g_gate, g_up, proj_handed[3])
    g_proj = give(proj_handed)
    g_k, g_v, g_q, g_o = spread(
        low, g_proj, [(block, w) for w in widths], put_proj
    )

    def gain_gradient(gain, pairs):
        along = sum(jnp.sum(w.astype(f32) * g, axis=1) for w, g in pairs)
        return along / gain.astype(f32)

    g_attention_gain = gain_gradient(
        attention_gain, [(query_weight, g_q), (key_weight, g_k), (value_weight, g_v)]
    )
    g_feedforward_gain = gain_gradient(
        feedforward_gain, [(gate_weight, g_gate), (up_weight, g_up)]
    )

    return (
        final.astype(bf16)[None],
        gradient.astype(bf16)[None],
        g_attention_gain,
        g_feedforward_gain,
        g_q,
        g_k,
        g_v,
        g_o,
        g_gate,
        g_up,
        g_down,
    )


def solution(mesh):
    rows = P("fsdp", None)
    placed = (P("dp", "fsdp", None), P("dp"), P("dp", "fsdp", None), P("fsdp"), P("fsdp")) + (
        rows,
    ) * 7
    return jax.shard_map(
        local,
        mesh=mesh,
        in_specs=placed,
        out_specs=(P("dp", "fsdp", None), P("dp", "fsdp", None), P("fsdp"), P("fsdp"))
        + (rows,) * 7,
        check_vma=False,
    )
```

profile of v0, /device:TPU:0, one launch (start us, length us, event | category | flops | bytes accessed | tf_op | source)
XLA Modules:
  0.0 556.4 jit_solution(16088161474187479410)
XLA Ops:
  10.8 2.4 concatenate.29.refs_9_
  15.7 3.1 collective-permute-start.2
  18.8 2.6 collective-permute-start.1
  28.5 2.3 copy.33
  31.7 2.8 fusion.35
  42.3 8.8 %collective-permute-done.3.refs_2_ = bf16[3,128,640]{2,1,0:T(8,128)(2,1)} collective-permute-done((bf16[3,128,640]{2,1,0:T(8,128)(2,1)S(1)}, bf16[3,128,640]{2,1,0:T(8,128)(2,1)}, u32[]{:S(2)}, u32[]{:S(2)}) %collective-permute-start.3) | collective-permute-done | bytes 491552 | tf_op jit(solution)/shard_map/ppermute | solution.py:35
  60.3 10.3 %all-gather.3.cloned.1.call-done = bf16[1600,640]{1,0:T(8,128)(2,1)} async-done(((bf16[400,640]{1,0:T(8,128)(2,1)}), bf16[1600,640]{1,0:T(8,128)(2,1)}) %all-gather.3.cloned.1.call-update) | async-done | bytes 2048016 | tf_op jit(solution)/shard_map/all_gather | solution.py:910
  74.8 2.4 lay_out.3.refs_1_
  79.4 6.7 %collective-permute-start.10 = (bf16[640,384]{1,0:T(8,128)(2,1)S(1)}, bf16[640,384]{1,0:T(8,128)(2,1)S(1)}, u32[]{:S(2)}, u32[]{:S(2)}) collective-permute-start(bf16[640,384]{1,0:T(8,128)(2,1)S(1)} %keys_values.2.refs_4_.refs_2_.refs_5_.refs_6_), channel_id=1, source_target_pairs={{0,1},{1,2},{2,3},{4,5},{5,6},{6,7},{8,9},{9,10},{10,11},{12,13},{... | collective-permute-start | bytes 1474568 | tf_op jit(solution)/shard_map/ppermute | solution.py:40
  90.2 3.4 attend.8
  98.6 21.1 %collective-permute-done.15.refs_2_ = bf16[3,80,960]{2,1,0:T(8,128)(2,1)} collective-permute-done((bf16[3,80,960]{2,1,0:T(8,128)(2,1)}, bf16[3,80,960]{2,1,0:T(8,128)(2,1)}, u32[]{:S(2)}, u32[]{:S(2)}) %collective-permute-start.15) | collective-permute-done | bytes 460832 | tf_op jit(solution)/shard_map/ppermute | solution.py:35
  123.6 15.5 %collective-permute-done.18.refs_4_ = bf16[3,80,960]{2,1,0:T(8,128)(2,1)S(1)} collective-permute-done((bf16[3,80,960]{2,1,0:T(8,128)(2,1)}, bf16[3,80,960]{2,1,0:T(8,128)(2,1)S(1)}, u32[]{:S(2)}, u32[]{:S(2)}) %collective-permute-start.18) | collective-permute-done | bytes 460832 | tf_op jit(solution)/shard_map/ppermute | solution.py:35
  147.6 2.9 lay_out.4
  155.0 13.8 %feed_forward.2 = (f32[384,960]{1,0:T(8,128)S(1)}, f32[384,960]{1,0:T(8,128)S(1)}, bf16[384,2560]{1,0:T(8,128)(2,1)}, bf16[384,2560]{1,0:T(8,128)(2,1)}, bf16[96...) custom-call(f32[384,960]{1,0:T(8,128)} %bitcast_convert_fusion.x_ref, bf16[960,384]{1,0:T(8,128)(2,1)S(1)} %copy-done.20, ...), custom_call_target="tpu_custom_call" | custom-call | flops 276000014336 | tf_op jit(solution)/shard_map/feed_forward/pallas_call | solution.py:672
  172.3 2.4 copy-done.18
  181.1 3.2 attend.12
  195.4 4.9 attend.15
  202.7 13.9 %feed_forward.3 = (f32[384,960]{1,0:T(8,128)S(1)}, f32[384,960]{1,0:T(8,128)S(1)}, bf16[384,2560]{1,0:T(8,128)(2,1)}, bf16[384,2560]{1,0:T(8,128)(2,1)}, bf16[96...) custom-call(f32[384,960]{1,0:T(8,128)} %copy-done.1, ...), custom_call_target="tpu_custom_call", output_to_operand_aliasing={{4}: (7, {}), {5}: (8, {})} | custom-call | flops 276000014336 | tf_op jit(solution)/shard_map/feed_forward/pallas_call | solution.py:672
  218.8 16.4 %feed_forward_back.2 = (bf16[2,768,2560]{2,1,0:T(8,128)(2,1)}, f32[384,960]{1,0:T(8,128)S(1)}, bf16[384,960]{1,0:T(8,128)(2,1)S(1)}, bf16[960,384]{1,0:T(8,128)(2,1)S(1)}) custom-call(f32[384,960]{1,0:T(8,128)S(1)} %copy-done.11, f32[384,960]{1,0:T(8,128)} %copy-done.87, f32[1,960]{1,0:T(1,128)S(1)} %copy-done.34, ...), custom_call_target="tpu_custom_call" | custom-call | flops 413999988736 | tf_op jit(solution)/shard_map/feed_forward_back/pallas_call | solution.py:82
  235.3 2.6 attend_back.8
  248.3 7.3 %attend_back.11 = (bf16[960,384]{1,0:T(8,128)(2,1)S(1)}, bf16[2,320,384]{2,1,0:T(8,128)(2,1)S(1)}) custom-call(s32[2]{0:T(128)S(1)} %copy-done.67, bf16[960,384]{1,0:T(8,128)(2,1)S(1)} %copy-done.77, bf16[960,384]{1,0:T(8,128)(2,1)S(1)} %get-tuple-element.168.mix_ref.refs_2_, bf16[960,384]{1,0:T(8,128)(2,1)S(1)} %get-tuple-element.177.refs_3_, ...), custom_call_target="tpu_custom_call" | custom-call | flops 160999997440 | tf_op jit(solution)/shard_map/attend_back/pallas_call | solution.py:82
  255.6 48.2 %collective-permute-done.35.refs_1_ = bf16[2,320,384]{2,1,0:T(8,128)(2,1)} collective-permute-done((bf16[2,320,384]{2,1,0:T(8,128)(2,1)}, bf16[2,320,384]{2,1,0:T(8,128)(2,1)}, u32[]{:S(2)}, u32[]{:S(2)}) %collective-permute-start.35) | collective-permute-done | bytes 491552 | tf_op jit(solution)/shard_map/ppermute | solution.py:843
  305.6 4.3 multiply_reduce_fusion.3
  312.4 6.5 %weight_grad.6 = (bf16[4,4,80,960]{3,2,1,0:T(8,128)(2,1)}, f32[8,128]{1,0:T(8,128)}) custom-call(s32[4]{0:T(128)} %pad_add_fusion.3.refs_0_, bf16[4,8,80,768]{3,2,1,0:T(8,128)(2,1)} %bitcast.134, bf16[768,960]{1,0:T(8,128)(2,1)} %pad_maximum_fusion.1.refs_2_), custom_call_target="tpu_custom_call" | custom-call | flops 128799997952 | tf_op jit(solution)/shard_map/weight_grad/pallas_call | solution.py:82
  319.6 4.6 collective-permute-done.36.refs_3_
  324.2 7.4 %weight_grad.7 = (bf16[2,4,80,960]{3,2,1,0:T(8,128)(2,1)}, bf16[2,4,80,960]{3,2,1,0:T(8,128)(2,1)}, f32[8,128]{1,0:T(8,128)}) custom-call(s32[4]{0:T(128)} %pad_add_fusion.2.refs_0_, bf16[4,8,80,768]{3,2,1,0:T(8,128)(2,1)} %bitcast.135, bf16[768,960]{1,0:T(8,128)(2,1)} %pad_maximum_fusion.1.refs_2_, bf16[4,4,80,960]{3,2,1,0:T(8,128)(2,1)} %collective-permute-done.36.refs_3_, ...), custom_call_target="tpu_custom_call" | custom-call | flops 128799997952 | tf_op jit(solution)/shard_map/weight_grad/pallas_call | solution.py:82
  334.1 16.4 %feed_forward_back.3 = (bf16[2,768,2560]{2,1,0:T(8,128)(2,1)}, f32[384,960]{1,0:T(8,128)S(1)}, bf16[384,960]{1,0:T(8,128)(2,1)S(1)}, bf16[960,384]{1,0:T(8,128)(2,1)S(1)}) custom-call(f32[384,960]{1,0:T(8,128)S(1)} %get-tuple-element.277.refs_0_, f32[384,960]{1,0:T(8,128)} %copy-done.88, f32[1,960]{1,0:T(1,128)S(1)} %copy-done.34, ...), custom_call_target="tpu_custom_call", output_to_operand_aliasing={{0}: (9, {})} | custom-call | flops 413999988736 | tf_op jit(solution)/shard_map/feed_forward_back/pallas_call | solution.py:82
  351.6 9.4 %weight_grad.8 = (bf16[4,4,240,640]{3,2,1,0:T(8,128)(2,1)}, f32[8,128]{1,0:T(8,128)}) custom-call(s32[4]{0:T(128)} %pad_add_fusion.3.refs_0_, bf16[960,768]{1,0:T(8,128)(2,1)} %copy-done.84, bf16[2,768,2560]{2,1,0:T(8,128)(2,1)} %get-tuple-element.201.refs_2_), custom_call_target="tpu_custom_call" | custom-call | flops 202400006144 | tf_op jit(solution)/shard_map/weight_grad/pallas_call | solution.py:82
  366.1 2.6 attend_back.12
  370.3 4.1 collective-permute-done.38
  377.0 11.1 %weight_grad.9 = (bf16[2,4,240,640]{3,2,1,0:T(8,128)(2,1)}, bf16[2,4,240,640]{3,2,1,0:T(8,128)(2,1)}, f32[8,128]{1,0:T(8,128)}) custom-call(s32[4]{0:T(128)} %pad_add_fusion.2.refs_0_, bf16[960,768]{1,0:T(8,128)(2,1)} %copy-done.84, bf16[2,768,2560]{2,1,0:T(8,128)(2,1)} %get-tuple-element.201.refs_2_, ...), custom_call_target="tpu_custom_call" | custom-call | flops 202400006144 | tf_op jit(solution)/shard_map/weight_grad/pallas_call | solution.py:82
  398.8 19.6 %collective-permute-done.40 = bf16[2,4,240,640]{3,2,1,0:T(8,128)(2,1)} collective-permute-done((bf16[2,4,240,640]{3,2,1,0:T(8,128)(2,1)}, bf16[2,4,240,640]{3,2,1,0:T(8,128)(2,1)}, u32[]{:S(2)}, u32[]{:S(2)}) %collective-permute-start.40) | collective-permute-done | bytes 2457632 | tf_op jit(solution)/shard_map/ppermute | solution.py:35
  418.4 3.0 fusion.20
  428.8 7.2 %attend_back.15 = (bf16[960,384]{1,0:T(8,128)(2,1)S(1)}, bf16[2,320,384]{2,1,0:T(8,128)(2,1)S(1)}) custom-call(s32[2]{0:T(128)S(1)} %copy-done.67, bf16[960,384]{1,0:T(8,128)(2,1)S(1)} %copy-done.75, bf16[960,384]{1,0:T(8,128)(2,1)S(1)} %copy-done.22, bf16[960,384]{1,0:T(8,128)(2,1)S(1)} %copy-done.86, f32[5,3,384]{2,1,0:T(4,128)S(1)} %copy-done.91, ...), custom_call_target="tpu_custom_call" | custom-call | flops 160999997440 | tf_op jit(solution)/shard_map/attend_back/pallas_call | solution.py:82
  438.0 5.4 collective-permute-done.46
  447.7 5.7 %weight_grad.10 = (bf16[4,4,120,640]{3,2,1,0:T(8,128)(2,1)S(1)}, f32[8,128]{1,0:T(8,128)S(1)}) custom-call(s32[4]{0:T(128)S(1)} %copy-done.36, bf16[2,4,2,128,768]{4,3,2,1,0:T(8,128)(2,1)S(1)} %copy-done, bf16[2,4,2,128,768]{4,3,2,1,0:T(8,128)(2,1)S(1)} %copy-done, bf16[384,2560]{1,0:T(8,128)(2,1)S(1)} %copy-done.5, ...), custom_call_target="tpu_custom_call" | custom-call | flops 184000004096 | tf_op jit(solution)/shard_map/weight_grad/pallas_call | solution.py:82
  455.5 6.4 %weight_grad.11 = (bf16[4,4,120,640]{3,2,1,0:T(8,128)(2,1)S(1)}, f32[8,128]{1,0:T(8,128)}) custom-call(s32[4]{0:T(128)S(1)} %copy-done.35, bf16[2,4,2,128,768]{4,3,2,1,0:T(8,128)(2,1)S(1)} %copy-done, bf16[2,4,2,128,768]{4,3,2,1,0:T(8,128)(2,1)S(1)} %copy-done, bf16[384,2560]{1,0:T(8,128)(2,1)S(1)} %copy-done.5, ...), custom_call_target="tpu_custom_call" | custom-call | flops 920000000 | tf_op jit(solution)/shard_map/weight_grad/pallas_call | solution.py:82
  463.8 2.3 collective-permute-start.52
  468.4 7.4 %collective-permute-done.52 = bf16[240,640]{1,0:T(8,128)(2,1)S(1)} collective-permute-done((bf16[240,640]{1,0:T(8,128)(2,1)S(1)}, bf16[240,640]{1,0:T(8,128)(2,1)S(1)}, u32[]{:S(2)}, u32[]{:S(2)}) %collective-permute-start.52) | collective-permute-done | bytes 307232 | tf_op jit(solution)/shard_map/ppermute | solution.py:57
  475.8 5.4 collective-permute-done.53
  484.8 2.4 copy.37
  488.5 4.5 collective-permute-done.55
  494.8 9.5 %collective-permute-done.56 = bf16[240,640]{1,0:T(8,128)(2,1)S(1)} collective-permute-done((bf16[240,640]{1,0:T(8,128)(2,1)}, bf16[240,640]{1,0:T(8,128)(2,1)S(1)}, u32[]{:S(2)}, u32[]{:S(2)}) %collective-permute-start.56) | collective-permute-done | bytes 307232 | tf_op jit(solution)/shard_map/ppermute | solution.py:57
  505.3 3.7 multiply_reduce_fusion.2
  515.8 7.4 %collective-permute-done.58 = bf16[120,640]{1,0:T(8,128)(2,1)S(1)} collective-permute-done((bf16[120,640]{1,0:T(8,128)(2,1)S(1)}, bf16[120,640]{1,0:T(8,128)(2,1)S(1)}, u32[]{:S(2)}, u32[]{:S(2)}) %collective-permute-start.58) | collective-permute-done | bytes 153632 | tf_op jit(solution)/shard_map/ppermute | solution.py:57
  531.9 2.4 spread.5
  536.6 2.6 spread.3
  543.8 2.3 spread.4
  (517 shorter events, 178.8 us)
Async XLA Ops:
  7.2 63.4 %all-gather.3.cloned.1.call-start = ((), (), s32[]{:S(2)}) async-start(), calls=%async_computation | async-start | bytes 2560000 | tf_op jit(solution)/shard_map/all_gather | solution.py:910
  15.7 19.8 %collective-permute-start.2 = (bf16[144,640]{1,0:T(8,128)(2,1)S(1)}, bf16[144,640]{1,0:T(8,128)(2,1)S(1)}, u32[]{:S(2)}, u32[]{:S(2)}) collective-permute-start(bf16[144,640]{1,0:T(8,128)(2,1)S(1)} %fusion.31), channel_id=1, source_target_pairs={{0,1},{1,2},{2,3},{3,0},{4,5},{5,6},{6,7},{7,4},{8,9},{9,10},{10,1... | collective-permute-start | bytes 552968 | tf_op jit(solution)/shard_map/ppermute | solution.py:57
  18.8 16.7 %collective-permute-start.1 = (bf16[144,640]{1,0:T(8,128)(2,1)S(1)}, bf16[144,640]{1,0:T(8,128)(2,1)S(1)}, u32[]{:S(2)}, u32[]{:S(2)}) collective-permute-start(bf16[144,640]{1,0:T(8,128)(2,1)S(1)} %fusion.31), channel_id=1, source_target_pairs={{0,2},{1,3},{2,0},{3,1},{4,6},{5,7},{6,4},{7,5},{8,10},{9,11},{10,... | collective-permute-start | bytes 552968 | tf_op jit(solution)/shard_map/ppermute | solution.py:57
  21.3 13.2 %collective-permute-start = (bf16[144,640]{1,0:T(8,128)(2,1)S(1)}, bf16[144,640]{1,0:T(8,128)(2,1)}, u32[]{:S(2)}, u32[]{:S(2)}) collective-permute-start(bf16[144,640]{1,0:T(8,128)(2,1)S(1)} %fusion.31), channel_id=1, source_target_pairs={{0,3},{1,0},{2,1},{3,2},{4,7},{5,4},{6,5},{7,6},{8,11},{9,8},{10,9... | collective-permute-start | bytes 552968 | tf_op jit(solution)/shard_map/ppermute | solution.py:57
  36.9 14.2 %collective-permute-start.3 = (bf16[3,128,640]{2,1,0:T(8,128)(2,1)S(1)}, bf16[3,128,640]{2,1,0:T(8,128)(2,1)}, u32[]{:S(2)}, u32[]{:S(2)}) collective-permute-start(bf16[3,128,640]{2,1,0:T(8,128)(2,1)S(1)} %pad_maximum_fusion.3.refs_1_), channel_id=1, source_target_pairs={{0,8},{4,20},{8,0},{12,28},{16,24},{20,4},{24,16},{28,12},{1,9},{5... | collective-permute-start | bytes 1474568 | tf_op jit(solution)/shard_map/ppermute | solution.py:35
  38.5 19.5 %collective-permute-start.4 = (bf16[3,128,640]{2,1,0:T(8,128)(2,1)S(1)}, bf16[3,128,640]{2,1,0:T(8,128)(2,1)}, u32[]{:S(2)}, u32[]{:S(2)}) collective-permute-start(bf16[3,128,640]{2,1,0:T(8,128)(2,1)S(1)} %pad_maximum_fusion.3.refs_1_), channel_id=1, source_target_pairs={{0,16},{4,12},{8,24},{12,4},{16,0},{20,28},{24,8},{28,20},{1,17},{... | collective-permute-start | bytes 1474568 | tf_op jit(solution)/shard_map/ppermute | solution.py:35
  40.0 34.8 %collective-permute-start.6 = (bf16[3,128,640]{2,1,0:T(8,128)(2,1)S(1)}, bf16[3,128,640]{2,1,0:T(8,128)(2,1)}, u32[]{:S(2)}, u32[]{:S(2)}) collective-permute-start(bf16[3,128,640]{2,1,0:T(8,128)(2,1)S(1)} %pad_maximum_fusion.3.refs_1_), channel_id=1, source_target_pairs={{0,4},{4,0},{8,12},{12,8},{16,20},{20,16},{24,28},{28,24},{1,5},{5... | collective-permute-start | bytes 1474568 | tf_op jit(solution)/shard_map/ppermute | solution.py:35
  51.1 9.1 %collective-permute-start.5 = (bf16[3,128,640]{2,1,0:T(8,128)(2,1)}, bf16[3,128,640]{2,1,0:T(8,128)(2,1)}, u32[]{:S(2)}, u32[]{:S(2)}) collective-permute-start(bf16[3,128,640]{2,1,0:T(8,128)(2,1)} %collective-permute-done.3.refs_2_), channel_id=1, source_target_pairs={{0,16},{4,12},{8,24},{12,4},{16,0},{20,28},{24,8},{28,20},{1,17},{... | collective-permute-start | bytes 1474568 | tf_op jit(solution)/shard_map/ppermute | solution.py:35
  57.9 16.9 %collective-permute-start.7 = (bf16[3,128,640]{2,1,0:T(8,128)(2,1)}, bf16[3,128,640]{2,1,0:T(8,128)(2,1)}, u32[]{:S(2)}, u32[]{:S(2)}) collective-permute-start(bf16[3,128,640]{2,1,0:T(8,128)(2,1)} %collective-permute-done.3.refs_2_), channel_id=1, source_target_pairs={{0,4},{4,0},{8,12},{12,8},{16,20},{20,16},{24,28},{28,24},{1,5},{5... | collective-permute-start | bytes 1474568 | tf_op jit(solution)/shard_map/ppermute | solution.py:35
  57.9 16.8 %collective-permute-start.8 = (bf16[3,128,640]{2,1,0:T(8,128)(2,1)}, bf16[3,128,640]{2,1,0:T(8,128)(2,1)}, u32[]{:S(2)}, u32[]{:S(2)}) collective-permute-start(bf16[3,128,640]{2,1,0:T(8,128)(2,1)} %collective-permute-done.4.refs_3_), channel_id=1, source_target_pairs={{0,4},{4,0},{8,12},{12,8},{16,20},{20,16},{24,28},{28,24},{1,5},{5... | collective-permute-start | bytes 1474568 | tf_op jit(solution)/shard_map/ppermute | solution.py:35
  60.3 14.5 %collective-permute-start.9 = (bf16[3,128,640]{2,1,0:T(8,128)(2,1)}, bf16[3,128,640]{2,1,0:T(8,128)(2,1)}, u32[]{:S(2)}, u32[]{:S(2)}) collective-permute-start(bf16[3,128,640]{2,1,0:T(8,128)(2,1)} %collective-permute-done.5.refs_4_), channel_id=1, source_target_pairs={{0,4},{4,0},{8,12},{12,8},{16,20},{20,16},{24,28},{28,24},{1,5},{5... | collective-permute-start | bytes 1474568 | tf_op jit(solution)/shard_map/ppermute | solution.py:35
  79.4 17.8 %collective-permute-start.10 = (bf16[640,384]{1,0:T(8,128)(2,1)S(1)}, bf16[640,384]{1,0:T(8,128)(2,1)S(1)}, u32[]{:S(2)}, u32[]{:S(2)}) collective-permute-start(bf16[640,384]{1,0:T(8,128)(2,1)S(1)} %keys_values.2.refs_4_.refs_2_.refs_5_.refs_6_), channel_id=1, source_target_pairs={{0,1},{1,2},{2,3},{4,5},{5,6},{6,7},{8,9},{9,10},{10,11},{12,13},{... | collective-permute-start | bytes 1474568 | tf_op jit(solution)/shard_map/ppermute | solution.py:40
  86.1 34.1 %collective-permute-start.13 = (bf16[3,240,640]{2,1,0:T(8,128)(2,1)}, bf16[3,240,640]{2,1,0:T(8,128)(2,1)}, u32[]{:S(2)}, u32[]{:S(2)}) collective-permute-start(bf16[3,240,640]{2,1,0:T(8,128)(2,1)} %pad_maximum_fusion.2.refs_10_.refs_1_), channel_id=1, source_target_pairs={{0,8},{4,20},{8,0},{12,28},{16,24},{20,4},{24,16},{28,12},{1,9},{5... | collective-permute-start | bytes 2764808 | tf_op jit(solution)/shard_map/ppermute | solution.py:35
  86.4 33.8 %collective-permute-start.14 = (bf16[3,240,640]{2,1,0:T(8,128)(2,1)}, bf16[3,240,640]{2,1,0:T(8,128)(2,1)}, u32[]{:S(2)}, u32[]{:S(2)}) collective-permute-start(bf16[3,240,640]{2,1,0:T(8,128)(2,1)} %pad_maximum_fusion.2.refs_10_.refs_1_), channel_id=1, source_target_pairs={{0,16},{4,12},{8,24},{12,4},{16,0},{20,28},{24,8},{28,20},{1,17},{... | collective-permute-start | bytes 2764808 | tf_op jit(solution)/shard_map/ppermute | solution.py:35
  86.8 32.9 %collective-permute-start.15 = (bf16[3,80,960]{2,1,0:T(8,128)(2,1)}, bf16[3,80,960]{2,1,0:T(8,128)(2,1)}, u32[]{:S(2)}, u32[]{:S(2)}) collective-permute-start(bf16[3,80,960]{2,1,0:T(8,128)(2,1)} %pad_maximum_fusion.4.refs_11_.refs_1_), channel_id=1, source_target_pairs={{0,8},{4,20},{8,0},{12,28},{16,24},{20,4},{24,16},{28,12},{1,9},{5... | collective-permute-start | bytes 1382408 | tf_op jit(solution)/shard_map/ppermute | solution.py:35
  88.4 31.2 %collective-permute-start.16 = (bf16[3,80,960]{2,1,0:T(8,128)(2,1)}, bf16[3,80,960]{2,1,0:T(8,128)(2,1)}, u32[]{:S(2)}, u32[]{:S(2)}) collective-permute-start(bf16[3,80,960]{2,1,0:T(8,128)(2,1)} %pad_maximum_fusion.4.refs_11_.refs_1_), channel_id=1, source_target_pairs={{0,16},{4,12},{8,24},{12,4},{16,0},{20,28},{24,8},{28,20},{1,17},{... | collective-permute-start | bytes 1382408 | tf_op jit(solution)/shard_map/ppermute | solution.py:35
  97.2 25.0 %collective-permute-start.11 = (bf16[640,384]{1,0:T(8,128)(2,1)S(1)}, bf16[640,384]{1,0:T(8,128)(2,1)S(1)}, u32[]{:S(2)}, u32[]{:S(2)}) collective-permute-start(bf16[640,384]{1,0:T(8,128)(2,1)S(1)} %collective-permute-done.10.refs_2_.refs_5_.refs_6_), channel_id=1, source_target_pairs={{1,2},{2,3},{5,6},{6,7},{9,10},{10,11},{13,14},{14,15},{17,18},{18... | collective-permute-start | bytes 1474568 | tf_op jit(solution)/shard_map/ppermute | solution.py:40
  119.6 27.9 %collective-permute-start.19 = (bf16[3,240,640]{2,1,0:T(8,128)(2,1)}, bf16[3,240,640]{2,1,0:T(8,128)(2,1)}, u32[]{:S(2)}, u32[]{:S(2)}) collective-permute-start(bf16[3,240,640]{2,1,0:T(8,128)(2,1)} %pad_maximum_fusion.2.refs_10_.refs_1_), channel_id=1, source_target_pairs={{0,4},{4,0},{8,12},{12,8},{16,20},{20,16},{24,28},{28,24},{1,5},{5... | collective-permute-start | bytes 2764808 | tf_op jit(solution)/shard_map/ppermute | solution.py:35
  119.6 22.6 %collective-permute-start.23 = (bf16[3,80,960]{2,1,0:T(8,128)(2,1)}, bf16[3,80,960]{2,1,0:T(8,128)(2,1)}, u32[]{:S(2)}, u32[]{:S(2)}) collective-permute-start(bf16[3,80,960]{2,1,0:T(8,128)(2,1)} %pad_maximum_fusion.4.refs_11_.refs_1_), channel_id=1, source_target_pairs={{0,4},{4,0},{8,12},{12,8},{16,20},{20,16},{24,28},{28,24},{1,5},{5... | collective-permute-start | bytes 1382408 | tf_op jit(solution)/shard_map/ppermute | solution.py:35
  120.2 18.9 %collective-permute-start.17 = (bf16[3,240,640]{2,1,0:T(8,128)(2,1)}, bf16[3,240,640]{2,1,0:T(8,128)(2,1)S(1)}, u32[]{:S(2)}, u32[]{:S(2)}) collective-permute-start(bf16[3,240,640]{2,1,0:T(8,128)(2,1)} %collective-permute-done.13.refs_2_), channel_id=1, source_target_pairs={{0,16},{4,12},{8,24},{12,4},{16,0},{20,28},{24,8},{28,20},{1,17},{... | collective-permute-start | bytes 2764808 | tf_op jit(solution)/shard_map/ppermute | solution.py:35
  120.4 18.6 %collective-permute-start.18 = (bf16[3,80,960]{2,1,0:T(8,128)(2,1)}, bf16[3,80,960]{2,1,0:T(8,128)(2,1)S(1)}, u32[]{:S(2)}, u32[]{:S(2)}) collective-permute-start(bf16[3,80,960]{2,1,0:T(8,128)(2,1)} %collective-permute-done.15.refs_2_), channel_id=1, source_target_pairs={{0,16},{4,12},{8,24},{12,4},{16,0},{20,28},{24,8},{28,20},{1,17},{... | collective-permute-start | bytes 1382408 | tf_op jit(solution)/shard_map/ppermute | solution.py:35
  122.2 17.4 %collective-permute-start.12 = (bf16[640,384]{1,0:T(8,128)(2,1)S(1)}, bf16[640,384]{1,0:T(8,128)(2,1)S(1)}, u32[]{:S(2)}, u32[]{:S(2)}) collective-permute-start(bf16[640,384]{1,0:T(8,128)(2,1)S(1)} %collective-permute-done.11.refs_2_.refs_5_.refs_6_), channel_id=1, source_target_pairs={{2,3},{6,7},{10,11},{14,15},{18,19},{22,23},{26,27},{30,31}} | collective-permute-start | bytes 1474568 | tf_op jit(solution)/shard_map/ppermute | solution.py:40
  176.8 12.2 %collective-permute-start.27 = (bf16[320,384]{1,0:T(8,128)(2,1)S(1)}, bf16[320,384]{1,0:T(8,128)(2,1)S(1)}, u32[]{:S(2)}, u32[]{:S(2)}) collective-permute-start(bf16[320,384]{1,0:T(8,128)(2,1)S(1)} %get-tuple-element.160.refs_4_.refs_2_.refs_5_), channel_id=1, source_target_pairs={{0,1},{1,2},{2,3},{4,5},{5,6},{6,7},{8,9},{9,10},{10,11},{12,13},{... | collective-permute-start | bytes 737288 | tf_op jit(solution)/shard_map/ppermute | solution.py:40
  179.0 10.9 %collective-permute-start.30 = (bf16[320,384]{1,0:T(8,128)(2,1)S(1)}, bf16[320,384]{1,0:T(8,128)(2,1)S(1)}, u32[]{:S(2)}, u32[]{:S(2)}) collective-permute-start(bf16[320,384]{1,0:T(8,128)(2,1)S(1)} %get-tuple-element.161.refs_3_.refs_6_), channel_id=1, source_target_pairs={{0,1},{1,2},{2,3},{4,5},{5,6},{6,7},{8,9},{9,10},{10,11},{12,13},{... | collective-permute-start | bytes 737288 | tf_op jit(solution)/shard_map/ppermute | solution.py:40
  246.6 57.2 %collective-permute-start.35 = (bf16[2,320,384]{2,1,0:T(8,128)(2,1)}, bf16[2,320,384]{2,1,0:T(8,128)(2,1)}, u32[]{:S(2)}, u32[]{:S(2)}) collective-permute-start(bf16[2,320,384]{2,1,0:T(8,128)(2,1)} %add_convert_fusion.10), channel_id=1, source_target_pairs={{1,0},{2,1},{3,2},{5,4},{6,5},{7,6},{9,8},{10,9},{11,10},{13,12},{... | collective-permute-start | bytes 1474568 | tf_op jit(solution)/shard_map/ppermute | solution.py:843
  331.6 29.7 %collective-permute-start.37 = (bf16[2,4,80,960]{3,2,1,0:T(8,128)(2,1)}, bf16[2,4,80,960]{3,2,1,0:T(8,128)(2,1)}, u32[]{:S(2)}, u32[]{:S(2)}) collective-permute-start(bf16[2,4,80,960]{3,2,1,0:T(8,128)(2,1)} %get-tuple-element.190), channel_id=1, source_target_pairs={{0,8},{4,20},{8,0},{12,28},{16,24},{20,4},{24,16},{28,12},{1,9},{5... | collective-permute-start | bytes 3686408 | tf_op jit(solution)/shard_map/ppermute | solution.py:35
  361.0 15.9 %collective-permute-start.39 = (bf16[4,4,240,640]{3,2,1,0:T(8,128)(2,1)}, bf16[4,4,240,640]{3,2,1,0:T(8,128)(2,1)}, u32[]{:S(2)}, u32[]{:S(2)}) collective-permute-start(bf16[4,4,240,640]{3,2,1,0:T(8,128)(2,1)} %get-tuple-element.207), channel_id=1, source_target_pairs={{0,4},{4,0},{8,12},{12,8},{16,20},{20,16},{24,28},{28,24},{1,5},{5... | collective-permute-start | bytes 14745608 | tf_op jit(solution)/shard_map/ppermute | solution.py:35
  363.5 10.9 %collective-permute-start.38 = (bf16[4,80,960]{2,1,0:T(8,128)(2,1)}, bf16[4,80,960]{2,1,0:T(8,128)(2,1)}, u32[]{:S(2)}, u32[]{:S(2)}) collective-permute-start(bf16[4,80,960]{2,1,0:T(8,128)(2,1)} %fusion.25), channel_id=1, source_target_pairs={{0,16},{4,12},{8,24},{12,4},{16,0},{20,28},{24,8},{28,20},{1,17},{... | collective-permute-start | bytes 1843208 | tf_op jit(solution)/shard_map/ppermute | solution.py:35
  368.7 22.5 %collective-permute-start.41 = (bf16[2,320,384]{2,1,0:T(8,128)(2,1)}, bf16[2,320,384]{2,1,0:T(8,128)(2,1)}, u32[]{:S(2)}, u32[]{:S(2)}) collective-permute-start(bf16[2,320,384]{2,1,0:T(8,128)(2,1)} %get-tuple-element.220), channel_id=1, source_target_pairs={{3,2},{7,6},{11,10},{15,14},{19,18},{23,22},{27,26},{31,30}} | collective-permute-start | bytes 1474568 | tf_op jit(solution)/shard_map/ppermute | solution.py:843
  388.1 30.2 %collective-permute-start.40 = (bf16[2,4,240,640]{3,2,1,0:T(8,128)(2,1)}, bf16[2,4,240,640]{3,2,1,0:T(8,128)(2,1)}, u32[]{:S(2)}, u32[]{:S(2)}) collective-permute-start(bf16[2,4,240,640]{3,2,1,0:T(8,128)(2,1)} %get-tuple-element.211), channel_id=1, source_target_pairs={{0,8},{4,20},{8,0},{12,28},{16,24},{20,4},{24,16},{28,12},{1,9},{5... | collective-permute-start | bytes 7372808 | tf_op jit(solution)/shard_map/ppermute | solution.py:35
  397.5 38.5 %collective-permute-start.43 = (bf16[2,320,384]{2,1,0:T(8,128)(2,1)}, bf16[2,320,384]{2,1,0:T(8,128)(2,1)}, u32[]{:S(2)}, u32[]{:S(2)}) collective-permute-start(bf16[2,320,384]{2,1,0:T(8,128)(2,1)} %add_convert_fusion.8), channel_id=1, source_target_pairs={{1,0},{2,1},{3,2},{5,4},{6,5},{7,6},{9,8},{10,9},{11,10},{13,12},{... | collective-permute-start | bytes 1474568 | tf_op jit(solution)/shard_map/ppermute | solution.py:843
  421.4 22.0 %collective-permute-start.44 = (bf16[4,240,640]{2,1,0:T(8,128)(2,1)}, bf16[4,240,640]{2,1,0:T(8,128)(2,1)}, u32[]{:S(2)}, u32[]{:S(2)}) collective-permute-start(bf16[4,240,640]{2,1,0:T(8,128)(2,1)} %fusion.20), channel_id=1, source_target_pairs={{0,16},{4,12},{8,24},{12,4},{16,0},{20,28},{24,8},{28,20},{1,17},{... | collective-permute-start | bytes 3686408 | tf_op jit(solution)/shard_map/ppermute | solution.py:35
  423.2 14.7 %collective-permute-start.45 = (bf16[80,960]{1,0:T(8,128)(2,1)}, bf16[80,960]{1,0:T(8,128)(2,1)}, u32[]{:S(2)}, u32[]{:S(2)}) collective-permute-start(bf16[80,960]{1,0:T(8,128)(2,1)} %get-tuple-element.224), channel_id=1, source_target_pairs={{0,1},{1,2},{2,3},{3,0},{4,5},{5,6},{6,7},{7,4},{8,9},{9,10},{10,1... | collective-permute-start | bytes 460808 | tf_op jit(solution)/shard_map/ppermute | solution.py:57
  425.0 18.4 %collective-permute-start.46 = (bf16[80,960]{1,0:T(8,128)(2,1)}, bf16[80,960]{1,0:T(8,128)(2,1)}, u32[]{:S(2)}, u32[]{:S(2)}) collective-permute-start(bf16[80,960]{1,0:T(8,128)(2,1)} %get-tuple-element.225), channel_id=1, source_target_pairs={{0,2},{1,3},{2,0},{3,1},{4,6},{5,7},{6,4},{7,5},{8,10},{9,11},{10,... | collective-permute-start | bytes 460808 | tf_op jit(solution)/shard_map/ppermute | solution.py:57
  426.7 16.7 %collective-permute-start.47 = (bf16[80,960]{1,0:T(8,128)(2,1)}, bf16[80,960]{1,0:T(8,128)(2,1)}, u32[]{:S(2)}, u32[]{:S(2)}) collective-permute-start(bf16[80,960]{1,0:T(8,128)(2,1)} %get-tuple-element.226), channel_id=1, source_target_pairs={{0,3},{1,0},{2,1},{3,2},{4,7},{5,4},{6,5},{7,6},{8,11},{9,8},{10,9... | collective-permute-start | bytes 460808 | tf_op jit(solution)/shard_map/ppermute | solution.py:57
  453.4 8.5 %collective-permute-start.50 = (bf16[4,4,120,640]{3,2,1,0:T(8,128)(2,1)S(1)}, bf16[4,4,120,640]{3,2,1,0:T(8,128)(2,1)S(1)}, u32[]{:S(2)}, u32[]{:S(2)}) collective-permute-start(bf16[4,4,120,640]{3,2,1,0:T(8,128)(2,1)S(1)} %get-tuple-element.236), channel_id=1, source_target_pairs={{0,4},{4,0},{8,12},{12,8},{16,20},{20,16},{24,28},{28,24},{1,5},{5... | collective-permute-start | bytes 7372808 | tf_op jit(solution)/shard_map/ppermute | solution.py:35
  462.6 18.6 %collective-permute-start.51 = (bf16[2,4,120,640]{3,2,1,0:T(8,128)(2,1)S(1)}, bf16[2,4,120,640]{3,2,1,0:T(8,128)(2,1)S(1)}, u32[]{:S(2)}, u32[]{:S(2)}) collective-permute-start(bf16[2,4,120,640]{3,2,1,0:T(8,128)(2,1)S(1)} %add_convert_fusion), channel_id=1, source_target_pairs={{0,8},{4,20},{8,0},{12,28},{16,24},{20,4},{24,16},{28,12},{1,9},{5... | collective-permute-start | bytes 3686408 | tf_op jit(solution)/shard_map/ppermute | solution.py:35
  463.8 12.0 %collective-permute-start.52 = (bf16[240,640]{1,0:T(8,128)(2,1)S(1)}, bf16[240,640]{1,0:T(8,128)(2,1)S(1)}, u32[]{:S(2)}, u32[]{:S(2)}) collective-permute-start(bf16[240,640]{1,0:T(8,128)(2,1)S(1)} %copy-done.119), channel_id=1, source_target_pairs={{0,1},{1,2},{2,3},{3,0},{4,5},{5,6},{6,7},{7,4},{8,9},{9,10},{10,1... | collective-permute-start | bytes 921608 | tf_op jit(solution)/shard_map/ppermute | solution.py:57
  466.1 15.1 %collective-permute-start.53 = (bf16[240,640]{1,0:T(8,128)(2,1)S(1)}, bf16[240,640]{1,0:T(8,128)(2,1)S(1)}, u32[]{:S(2)}, u32[]{:S(2)}) collective-permute-start(bf16[240,640]{1,0:T(8,128)(2,1)S(1)} %copy-done.118), channel_id=1, source_target_pairs={{0,3},{1,0},{2,1},{3,2},{4,7},{5,4},{6,5},{7,6},{8,11},{9,8},{10,9... | collective-permute-start | bytes 921608 | tf_op jit(solution)/shard_map/ppermute | solution.py:57
  467.7 13.6 %collective-permute-start.54 = (bf16[80,960]{1,0:T(8,128)(2,1)S(1)}, bf16[80,960]{1,0:T(8,128)(2,1)S(1)}, u32[]{:S(2)}, u32[]{:S(2)}) collective-permute-start(bf16[80,960]{1,0:T(8,128)(2,1)S(1)} %collective-permute-done.49.refs_3_), channel_id=1, source_target_pairs={{0,8},{4,20},{8,0},{12,28},{16,24},{20,4},{24,16},{28,12},{1,9},{5... | collective-permute-start | bytes 460808 | tf_op jit(solution)/shard_map/ppermute | solution.py:35
  482.5 10.5 %collective-permute-start.55 = (bf16[4,120,640]{2,1,0:T(8,128)(2,1)}, bf16[4,120,640]{2,1,0:T(8,128)(2,1)}, u32[]{:S(2)}, u32[]{:S(2)}) collective-permute-start(bf16[4,120,640]{2,1,0:T(8,128)(2,1)} %fusion.28), channel_id=1, source_target_pairs={{0,16},{4,12},{8,24},{12,4},{16,0},{20,28},{24,8},{28,20},{1,17},{... | collective-permute-start | bytes 1843208 | tf_op jit(solution)/shard_map/ppermute | solution.py:35
  487.2 17.1 %collective-permute-start.56 = (bf16[240,640]{1,0:T(8,128)(2,1)}, bf16[240,640]{1,0:T(8,128)(2,1)S(1)}, u32[]{:S(2)}, u32[]{:S(2)}) collective-permute-start(bf16[240,640]{1,0:T(8,128)(2,1)} %get-tuple-element.287), channel_id=1, source_target_pairs={{0,2},{1,3},{2,0},{3,1},{4,6},{5,7},{6,4},{7,5},{8,10},{9,11},{10,... | collective-permute-start | bytes 921608 | tf_op jit(solution)/shard_map/ppermute | solution.py:57
  509.1 14.8 %collective-permute-start.60 = (bf16[240,640]{1,0:T(8,128)(2,1)S(1)}, bf16[240,640]{1,0:T(8,128)(2,1)S(1)}, u32[]{:S(2)}, u32[]{:S(2)}) collective-permute-start(bf16[240,640]{1,0:T(8,128)(2,1)S(1)} %add_convert_fusion.12.refs_1_), channel_id=1, source_target_pairs={{0,8},{4,20},{8,0},{12,28},{16,24},{20,4},{24,16},{28,12},{1,9},{5... | collective-permute-start | bytes 921608 | tf_op jit(solution)/shard_map/ppermute | solution.py:35
  511.1 12.2 %collective-permute-start.58 = (bf16[120,640]{1,0:T(8,128)(2,1)S(1)}, bf16[120,640]{1,0:T(8,128)(2,1)S(1)}, u32[]{:S(2)}, u32[]{:S(2)}) collective-permute-start(bf16[120,640]{1,0:T(8,128)(2,1)S(1)} %get-tuple-element.241), channel_id=1, source_target_pairs={{0,2},{1,3},{2,0},{3,1},{4,6},{5,7},{6,4},{7,5},{8,10},{9,11},{10,... | collective-permute-start | bytes 460808 | tf_op jit(solution)/shard_map/ppermute | solution.py:57
  511.1 12.2 %collective-permute-start.57 = (bf16[120,640]{1,0:T(8,128)(2,1)S(1)}, bf16[120,640]{1,0:T(8,128)(2,1)S(1)}, u32[]{:S(2)}, u32[]{:S(2)}) collective-permute-start(bf16[120,640]{1,0:T(8,128)(2,1)S(1)} %get-tuple-element.240), channel_id=1, source_target_pairs={{0,1},{1,2},{2,3},{3,0},{4,5},{5,6},{6,7},{7,4},{8,9},{9,10},{10,1... | collective-permute-start | bytes 460808 | tf_op jit(solution)/shard_map/ppermute | solution.py:57
  512.0 12.1 %collective-permute-start.62 = (bf16[240,640]{1,0:T(8,128)(2,1)S(1)}, bf16[240,640]{1,0:T(8,128)(2,1)S(1)}, u32[]{:S(2)}, u32[]{:S(2)}) collective-permute-start(bf16[240,640]{1,0:T(8,128)(2,1)S(1)} %collective-permute-done.61.refs_3_), channel_id=1, source_target_pairs={{0,8},{4,20},{8,0},{12,28},{16,24},{20,4},{24,16},{28,12},{1,9},{5... | collective-permute-start | bytes 921608 | tf_op jit(solution)/shard_map/ppermute | solution.py:35
  515.8 15.1 %collective-permute-start.74 = (bf16[80,960]{1,0:T(8,128)(2,1)S(1)}, bf16[80,960]{1,0:T(8,128)(2,1)S(1)}, u32[]{:S(2)}, u32[]{:S(2)}) collective-permute-start(bf16[80,960]{1,0:T(8,128)(2,1)S(1)} %copy-done.32), channel_id=1, source_target_pairs={{0,4},{4,0},{8,12},{12,8},{16,20},{20,16},{24,28},{28,24},{1,5},{5... | collective-permute-start | bytes 460808 | tf_op jit(solution)/shard_map/ppermute | solution.py:35
  534.5 9.3 %collective-permute-start.70 = (bf16[120,640]{1,0:T(8,128)(2,1)S(1)}, bf16[120,640]{1,0:T(8,128)(2,1)S(1)}, u32[]{:S(2)}, u32[]{:S(2)}) collective-permute-start(bf16[120,640]{1,0:T(8,128)(2,1)S(1)} %add_convert_fusion.14.refs_1_), channel_id=1, source_target_pairs={{0,4},{4,0},{8,12},{12,8},{16,20},{20,16},{24,28},{28,24},{1,5},{5... | collective-permute-start | bytes 460808 | tf_op jit(solution)/shard_map/ppermute | solution.py:35
  (165 other events, 1392.2 us)
Sparse Core Ops, SparseCore 0:
  23.9 46.6 all-gather.2
where the time goes:
time: 567 us; the launch traced here: 556 us
  waiting for transfers between devices  179 us (32%)
  Pallas kernels  168 us (30%)
  starting transfers between devices  76.8 us (14%)
  local copies, waits for them, and re-layouts  56.8 us (10%)
  other arithmetic  50.9 us (9%)
  between operations  16.8 us (3%)
  matrix products  8.09 us (1%)
    pallas_call x36, Pallas kernels, call(): return pl.pallas_call(waiting, **where, **rest)(*operands, *wait_for)  140 us
    ppermute x51, waiting for transfers between devices, swap(): return lax.ppermute(value, 'dp', [(i, hop(i)) for i in range(count)])  81.1 us
    ppermute x6, waiting for transfers between devices, attention_gradient(): lax.ppermute(moving, 'fsdp', [(i, i - 1) for i in range(count - step, cou...  48.2 us
    unnamed x276, local copies, waits for them, and re-layouts  38.1 us
    ppermute x12, waiting for transfers between devices, around(): lax.ppermute(value, 'fsdp', [(i, (i + distance) % count) for i in range(c...  37.5 us
    ppermute x51, starting transfers between devices, swap(): return lax.ppermute(value, 'dp', [(i, hop(i)) for i in range(count)])  32.9 us
    pallas_call x2, Pallas kernels, feed_forward(): pl.pallas_call(feed_forward_kernel, grid=(5,), in_specs=[whole(rows, mode...  27.7 us
    convert_element_type x14, other arithmetic, add(): return sum((v.astype(f32) for v in terms)).astype(bf16)  21.7 us
  transfers between devices with their start and end apart: 79, of which 24 were waited for; matrix products, arithmetic and copies ran while one was open for 11% of the time, Pallas kernels for 15%

commit v1 on v0

--- a/solution.py
+++ b/solution.py
@@ -241,13 +241,13 @@
     return sum(v.astype(f32) for v in terms).astype(bf16)
 
 
-def cost(us, weight=20):
+def cost(us, weight=6):
     return pl.CostEstimate(
         flops=int(us * weight * 1.15e9), bytes_accessed=0, transcendentals=0
     )
 
 
-HEAVY = 20
+HEAVY = 6
 
 
 class Reduction:

time: 567 us -> 544 us (0.959)
  other arithmetic: 50.9 us -> 36.3 us
  Pallas kernels: 168 us -> 159 us
    convert_element_type x14, other arithmetic: 21.7 us -> 8.79 us  [add(): return sum((v.astype(f32) for v in terms)).astype(bf16)]
    pallas_call x36, Pallas kernels: 140 us -> 132 us  [call(): return pl.pallas_call(waiting, **where, **rest)(*operands, *wait_for)]
    unnamed x276 -> x274, local copies, waits for them, and re-layouts: 38.1 us -> 39.3 us
  transfers between devices with their start and end apart: 79 -> 79, of which waited for: 24 -> 24; matrix products, arithmetic and copies ran while one was open for 11% -> 10% of each run, Pallas kernels for 15% -> 15%
where the time goes in v1:
time: 544 us; the launch traced here: 534 us
  waiting for transfers between devices  183 us (34%)
  Pallas kernels  159 us (29%)
  starting transfers between devices  73.9 us (14%)
  local copies, waits for them, and re-layouts  58.8 us (11%)
  other arithmetic  36.3 us (7%)
  between operations  17 us (3%)
  matrix products  5.47 us (1%)
    pallas_call x36, Pallas kernels, call(): return pl.pallas_call(waiting, **where, **rest)(*operands, *wait_for)  132 us
    ppermute x51, waiting for transfers between devices, swap(): return lax.ppermute(value, 'dp', [(i, hop(i)) for i in range(count)])  86.6 us
    ppermute x6, waiting for transfers between devices, attention_gradient(): lax.ppermute(moving, 'fsdp', [(i, i - 1) for i in range(count - step, cou...  45 us
    ppermute x12, waiting for transfers between devices, around(): lax.ppermute(value, 'fsdp', [(i, (i + distance) % count) for i in range(c...  39.5 us
    unnamed x274, local copies, waits for them, and re-layouts  39.3 us
    ppermute x51, starting transfers between devices, swap(): return lax.ppermute(value, 'dp', [(i, hop(i)) for i in range(count)])  31.4 us
    pallas_call x2, Pallas kernels, feed_forward(): pl.pallas_call(feed_forward_kernel, grid=(5,), in_specs=[whole(rows, mode...  27.8 us
    ppermute x12, starting transfers between devices, around(): lax.ppermute(value, 'fsdp', [(i, (i + distance) % count) for i in range(c...  20.3 us
  transfers between devices with their start and end apart: 79, of which 24 were waited for; matrix products, arithmetic and copies ran while one was open for 10% of the time, Pallas kernels for 15%

profile of v1, /device:TPU:0, one launch (start us, length us, event | category | flops | bytes accessed | tf_op | source)
XLA Modules:
  0.0 533.7 jit_solution(5331123858380774912)
XLA Ops:
  10.8 2.4 concatenate.29.refs_9_
  15.7 3.1 collective-permute-start.2
  18.8 2.6 collective-permute-start.1
  28.5 2.3 copy.33
  31.7 2.8 fusion.35
  42.6 8.8 %collective-permute-done.3.refs_2_ = bf16[3,128,640]{2,1,0:T(8,128)(2,1)} collective-permute-done((bf16[3,128,640]{2,1,0:T(8,128)(2,1)S(1)}, bf16[3,128,640]{2,1,0:T(8,128)(2,1)}, u32[]{:S(2)}, u32[]{:S(2)}) %collective-permute-start.3) | collective-permute-done | bytes 491552 | tf_op jit(solution)/shard_map/ppermute | solution.py:35
  51.4 2.3 fusion.38
  53.7 2.3 copy.32
  60.6 10.0 %all-gather.3.cloned.1.call-done = bf16[1600,640]{1,0:T(8,128)(2,1)} async-done(((bf16[400,640]{1,0:T(8,128)(2,1)}), bf16[1600,640]{1,0:T(8,128)(2,1)}) %all-gather.3.cloned.1.call-update) | async-done | bytes 2048016 | tf_op jit(solution)/shard_map/all_gather | solution.py:910
  73.2 2.4 lay_out.3.refs_1_
  77.7 7.0 %collective-permute-start.10 = (bf16[640,384]{1,0:T(8,128)(2,1)S(1)}, bf16[640,384]{1,0:T(8,128)(2,1)S(1)}, u32[]{:S(2)}, u32[]{:S(2)}) collective-permute-start(bf16[640,384]{1,0:T(8,128)(2,1)S(1)} %keys_values.2.refs_4_.refs_2_.refs_5_.refs_6_), channel_id=1, source_target_pairs={{0,1},{1,2},{2,3},{4,5},{5,6},{6,7},{8,9},{9,10},{10,11},{12,13},{... | collective-permute-start | bytes 1474568 | tf_op jit(solution)/shard_map/ppermute | solution.py:40
  88.8 3.4 attend.8
  97.2 20.8 %collective-permute-done.15.refs_2_ = bf16[3,80,960]{2,1,0:T(8,128)(2,1)S(1)} collective-permute-done((bf16[3,80,960]{2,1,0:T(8,128)(2,1)S(1)}, bf16[3,80,960]{2,1,0:T(8,128)(2,1)S(1)}, u32[]{:S(2)}, u32[]{:S(2)}) %collective-permute-start.15) | collective-permute-done | bytes 460832 | tf_op jit(solution)/shard_map/ppermute | solution.py:35
  121.9 15.3 %collective-permute-done.18.refs_4_ = bf16[3,80,960]{2,1,0:T(8,128)(2,1)S(1)} collective-permute-done((bf16[3,80,960]{2,1,0:T(8,128)(2,1)S(1)}, bf16[3,80,960]{2,1,0:T(8,128)(2,1)S(1)}, u32[]{:S(2)}, u32[]{:S(2)}) %collective-permute-start.18) | collective-permute-done | bytes 460832 | tf_op jit(solution)/shard_map/ppermute | solution.py:35
  148.0 2.3 copy-done.70
  150.3 13.9 %feed_forward.2 = (f32[384,960]{1,0:T(8,128)S(1)}, f32[384,960]{1,0:T(8,128)S(1)}, bf16[384,2560]{1,0:T(8,128)(2,1)}, bf16[384,2560]{1,0:T(8,128)(2,1)}, bf16[96...) custom-call(f32[384,960]{1,0:T(8,128)} %bitcast_convert_fusion.x_ref, ...), custom_call_target="tpu_custom_call" | custom-call | flops 82800001024 | tf_op jit(solution)/shard_map/feed_forward/pallas_call | solution.py:672
  175.5 3.2 attend.12
  181.1 2.3 copy.34
  191.1 4.6 attend.15
  198.1 13.9 %feed_forward.3 = (f32[384,960]{1,0:T(8,128)S(1)}, f32[384,960]{1,0:T(8,128)S(1)}, bf16[384,2560]{1,0:T(8,128)(2,1)}, bf16[384,2560]{1,0:T(8,128)(2,1)}, bf16[96...) custom-call(f32[384,960]{1,0:T(8,128)} %copy-done.1, ...), custom_call_target="tpu_custom_call", output_to_operand_aliasing={{4}: (7, {}), {5}: (8, {})} | custom-call | flops 82800001024 | tf_op jit(solution)/shard_map/feed_forward/pallas_call | solution.py:672
  213.1 16.9 %feed_forward_back.2 = (bf16[2,768,2560]{2,1,0:T(8,128)(2,1)}, f32[384,960]{1,0:T(8,128)S(1)}, bf16[384,960]{1,0:T(8,128)(2,1)S(1)}, bf16[960,384]{1,0:T(8,128)(2,1)S(1)}) custom-call(f32[384,960]{1,0:T(8,128)S(1)} %copy-done.10, f32[384,960]{1,0:T(8,128)} %copy-done.84, f32[1,960]{1,0:T(1,128)S(1)} %slice.162.gain_ref.refs_2_, ...), custom_call_target="tpu_custom_call" | custom-call | flops 124200001536 | tf_op jit(solution)/shard_map/feed_forward_back/pallas_call | solution.py:82
  238.4 7.2 %attend_back.11 = (bf16[960,384]{1,0:T(8,128)(2,1)S(1)}, bf16[2,320,384]{2,1,0:T(8,128)(2,1)S(1)}) custom-call(s32[2]{0:T(128)S(1)} %copy-done.61, bf16[960,384]{1,0:T(8,128)(2,1)S(1)} %copy-done.68, bf16[960,384]{1,0:T(8,128)(2,1)S(1)} %get-tuple-element.168.mix_ref.refs_2_, bf16[960,384]{1,0:T(8,128)(2,1)S(1)} %copy-done.83, f32[5,3,384]{2,1,0:T(4,128)S(1)} %copy-done.89, ...), custom_call_target="tpu_custom_call" | custom-call | flops 48299999232 | tf_op jit(solution)/shard_map/attend_back/pallas_call | solution.py:82
  245.6 44.9 %collective-permute-done.35.refs_1_ = bf16[2,320,384]{2,1,0:T(8,128)(2,1)S(1)} collective-permute-done((bf16[2,320,384]{2,1,0:T(8,128)(2,1)S(1)}, bf16[2,320,384]{2,1,0:T(8,128)(2,1)S(1)}, u32[]{:S(2)}, u32[]{:S(2)}) %collective-permute-start.35) | collective-permute-done | bytes 491552 | tf_op jit(solution)/shard_map/ppermute | solution.py:843
  296.2 6.5 %weight_grad.6 = (bf16[4,4,80,960]{3,2,1,0:T(8,128)(2,1)}, f32[8,128]{1,0:T(8,128)}) custom-call(s32[4]{0:T(128)} %pad_add_fusion.3.refs_0_, bf16[4,8,80,768]{3,2,1,0:T(8,128)(2,1)} %bitcast.138, bf16[768,960]{1,0:T(8,128)(2,1)} %pad_maximum_fusion.1.refs_2_), custom_call_target="tpu_custom_call" | custom-call | flops 38640001024 | tf_op jit(solution)/shard_map/weight_grad/pallas_call | solution.py:82
  303.3 4.7 collective-permute-done.36.refs_3_
  307.9 7.3 %weight_grad.7 = (bf16[2,4,80,960]{3,2,1,0:T(8,128)(2,1)}, bf16[2,4,80,960]{3,2,1,0:T(8,128)(2,1)}, f32[8,128]{1,0:T(8,128)}) custom-call(s32[4]{0:T(128)} %pad_add_fusion.2.refs_0_, bf16[4,8,80,768]{3,2,1,0:T(8,128)(2,1)} %bitcast.139, bf16[768,960]{1,0:T(8,128)(2,1)} %pad_maximum_fusion.1.refs_2_, bf16[4,4,80,960]{3,2,1,0:T(8,128)(2,1)} %collective-permute-done.36.refs_3_, ...), custom_call_target="tpu_custom_call" | custom-call | flops 38640001024 | tf_op jit(solution)/shard_map/weight_grad/pallas_call | solution.py:82
  318.1 16.3 %feed_forward_back.3 = (bf16[2,768,2560]{2,1,0:T(8,128)(2,1)}, f32[384,960]{1,0:T(8,128)S(1)}, bf16[384,960]{1,0:T(8,128)(2,1)S(1)}, bf16[960,384]{1,0:T(8,128)(2,1)S(1)}) custom-call(f32[384,960]{1,0:T(8,128)S(1)} %get-tuple-element.277.refs_0_, f32[384,960]{1,0:T(8,128)} %copy-done.85, ...), custom_call_target="tpu_custom_call", output_to_operand_aliasing={{0}: (9, {})} | custom-call | flops 124200001536 | tf_op jit(solution)/shard_map/feed_forward_back/pallas_call | solution.py:82
  335.6 9.4 %weight_grad.8 = (bf16[4,4,240,640]{3,2,1,0:T(8,128)(2,1)}, f32[8,128]{1,0:T(8,128)}) custom-call(s32[4]{0:T(128)} %pad_add_fusion.3.refs_0_, bf16[960,768]{1,0:T(8,128)(2,1)} %copy-done.77, bf16[2,768,2560]{2,1,0:T(8,128)(2,1)} %get-tuple-element.201.refs_2_), custom_call_target="tpu_custom_call" | custom-call | flops 60720001024 | tf_op jit(solution)/shard_map/weight_grad/pallas_call | solution.py:82
  350.6 6.5 %collective-permute-done.38 = bf16[4,80,960]{2,1,0:T(8,128)(2,1)S(1)} collective-permute-done((bf16[4,80,960]{2,1,0:T(8,128)(2,1)S(1)}, bf16[4,80,960]{2,1,0:T(8,128)(2,1)S(1)}, u32[]{:S(2)}, u32[]{:S(2)}) %collective-permute-start.38) | collective-permute-done | bytes 614432 | tf_op jit(solution)/shard_map/ppermute | solution.py:35
  359.5 10.8 %weight_grad.9 = (bf16[2,4,240,640]{3,2,1,0:T(8,128)(2,1)}, bf16[2,4,240,640]{3,2,1,0:T(8,128)(2,1)}, f32[8,128]{1,0:T(8,128)}) custom-call(s32[4]{0:T(128)} %pad_add_fusion.2.refs_0_, bf16[960,768]{1,0:T(8,128)(2,1)} %copy-done.77, bf16[2,768,2560]{2,1,0:T(8,128)(2,1)} %get-tuple-element.201.refs_2_, ...), custom_call_target="tpu_custom_call" | custom-call | flops 60720001024 | tf_op jit(solution)/shard_map/weight_grad/pallas_call | solution.py:82
  378.4 22.0 %collective-permute-done.40 = bf16[2,4,240,640]{3,2,1,0:T(8,128)(2,1)S(1)} collective-permute-done((bf16[2,4,240,640]{3,2,1,0:T(8,128)(2,1)}, bf16[2,4,240,640]{3,2,1,0:T(8,128)(2,1)S(1)}, u32[]{:S(2)}, u32[]{:S(2)}) %collective-permute-start.40) | collective-permute-done | bytes 2457632 | tf_op jit(solution)/shard_map/ppermute | solution.py:35
  405.3 2.6 collective-permute-start.47
  407.9 7.2 %attend_back.15 = (bf16[960,384]{1,0:T(8,128)(2,1)S(1)}, bf16[2,320,384]{2,1,0:T(8,128)(2,1)S(1)}) custom-call(s32[2]{0:T(128)S(1)} %copy-done.61, bf16[960,384]{1,0:T(8,128)(2,1)S(1)} %copy-done.64, bf16[960,384]{1,0:T(8,128)(2,1)S(1)} %copy-done.19, bf16[960,384]{1,0:T(8,128)(2,1)S(1)} %copy-done.80, f32[5,3,384]{2,1,0:T(4,128)S(1)} %copy-done.87, ...), custom_call_target="tpu_custom_call" | custom-call | flops 48299999232 | tf_op jit(solution)/shard_map/attend_back/pallas_call | solution.py:82
  417.7 5.4 %collective-permute-done.46 = bf16[80,960]{1,0:T(8,128)(2,1)S(1)} collective-permute-done((bf16[80,960]{1,0:T(8,128)(2,1)S(1)}, bf16[80,960]{1,0:T(8,128)(2,1)S(1)}, u32[]{:S(2)}, u32[]{:S(2)}) %collective-permute-start.46) | collective-permute-done | bytes 153632 | tf_op jit(solution)/shard_map/ppermute | solution.py:57
  426.0 5.7 %weight_grad.10 = (bf16[4,4,120,640]{3,2,1,0:T(8,128)(2,1)S(1)}, f32[8,128]{1,0:T(8,128)S(1)}) custom-call(s32[4]{0:T(128)S(1)} %copy-done.31, bf16[2,4,2,128,768]{4,3,2,1,0:T(8,128)(2,1)S(1)} %copy-done, bf16[2,4,2,128,768]{4,3,2,1,0:T(8,128)(2,1)S(1)} %copy-done, bf16[384,2560]{1,0:T(8,128)(2,1)S(1)} %copy-done.4, ...), custom_call_target="tpu_custom_call" | custom-call | flops 55199997952 | tf_op jit(solution)/shard_map/weight_grad/pallas_call | solution.py:82
  432.7 6.4 %weight_grad.11 = (bf16[4,4,120,640]{3,2,1,0:T(8,128)(2,1)S(1)}, f32[8,128]{1,0:T(8,128)}) custom-call(s32[4]{0:T(128)S(1)} %copy-done.30, bf16[2,4,2,128,768]{4,3,2,1,0:T(8,128)(2,1)S(1)} %copy-done, bf16[2,4,2,128,768]{4,3,2,1,0:T(8,128)(2,1)S(1)} %copy-done, bf16[384,2560]{1,0:T(8,128)(2,1)S(1)} %copy-done.4, ...), custom_call_target="tpu_custom_call" | custom-call | flops 276000000 | tf_op jit(solution)/shard_map/weight_grad/pallas_call | solution.py:82
  441.4 2.3 collective-permute-start.52
  445.6 7.8 %collective-permute-done.52 = bf16[240,640]{1,0:T(8,128)(2,1)S(1)} collective-permute-done((bf16[240,640]{1,0:T(8,128)(2,1)S(1)}, bf16[240,640]{1,0:T(8,128)(2,1)S(1)}, u32[]{:S(2)}, u32[]{:S(2)}) %collective-permute-start.52) | collective-permute-done | bytes 307232 | tf_op jit(solution)/shard_map/ppermute | solution.py:57
  453.4 5.1 collective-permute-done.53
  461.9 2.4 copy.37
  465.6 4.7 collective-permute-done.55
  472.2 9.6 %collective-permute-done.56 = bf16[240,640]{1,0:T(8,128)(2,1)S(1)} collective-permute-done((bf16[240,640]{1,0:T(8,128)(2,1)}, bf16[240,640]{1,0:T(8,128)(2,1)S(1)}, u32[]{:S(2)}, u32[]{:S(2)}) %collective-permute-start.56) | collective-permute-done | bytes 307232 | tf_op jit(solution)/shard_map/ppermute | solution.py:57
  482.2 3.7 multiply_reduce_fusion.2
  492.8 7.8 %collective-permute-done.58 = bf16[120,640]{1,0:T(8,128)(2,1)S(1)} collective-permute-done((bf16[120,640]{1,0:T(8,128)(2,1)S(1)}, bf16[120,640]{1,0:T(8,128)(2,1)S(1)}, u32[]{:S(2)}, u32[]{:S(2)}) %collective-permute-start.58) | collective-permute-done | bytes 153632 | tf_op jit(solution)/shard_map/ppermute | solution.py:57
  504.3 2.3 copy.38
  509.3 2.4 spread.5
  514.0 2.6 spread.3
  521.1 2.3 spread.4
  (517 shorter events, 158.1 us)
Async XLA Ops:
  7.2 63.4 %all-gather.3.cloned.1.call-start = ((), (), s32[]{:S(2)}) async-start(), calls=%async_computation | async-start | bytes 2560000 | tf_op jit(solution)/shard_map/all_gather | solution.py:910
  15.7 20.7 %collective-permute-start.2 = (bf16[144,640]{1,0:T(8,128)(2,1)S(1)}, bf16[144,640]{1,0:T(8,128)(2,1)S(1)}, u32[]{:S(2)}, u32[]{:S(2)}) collective-permute-start(bf16[144,640]{1,0:T(8,128)(2,1)S(1)} %fusion.31), channel_id=1, source_target_pairs={{0,1},{1,2},{2,3},{3,0},{4,5},{5,6},{6,7},{7,4},{8,9},{9,10},{10,1... | collective-permute-start | bytes 552968 | tf_op jit(solution)/shard_map/ppermute | solution.py:57
  18.8 16.7 %collective-permute-start.1 = (bf16[144,640]{1,0:T(8,128)(2,1)S(1)}, bf16[144,640]{1,0:T(8,128)(2,1)}, u32[]{:S(2)}, u32[]{:S(2)}) collective-permute-start(bf16[144,640]{1,0:T(8,128)(2,1)S(1)} %fusion.31), channel_id=1, source_target_pairs={{0,2},{1,3},{2,0},{3,1},{4,6},{5,7},{6,4},{7,5},{8,10},{9,11},{10,... | collective-permute-start | bytes 552968 | tf_op jit(solution)/shard_map/ppermute | solution.py:57
  21.3 13.2 %collective-permute-start = (bf16[144,640]{1,0:T(8,128)(2,1)S(1)}, bf16[144,640]{1,0:T(8,128)(2,1)}, u32[]{:S(2)}, u32[]{:S(2)}) collective-permute-start(bf16[144,640]{1,0:T(8,128)(2,1)S(1)} %fusion.31), channel_id=1, source_target_pairs={{0,3},{1,0},{2,1},{3,2},{4,7},{5,4},{6,5},{7,6},{8,11},{9,8},{10,9... | collective-permute-start | bytes 552968 | tf_op jit(solution)/shard_map/ppermute | solution.py:57
  37.2 14.2 %collective-permute-start.3 = (bf16[3,128,640]{2,1,0:T(8,128)(2,1)S(1)}, bf16[3,128,640]{2,1,0:T(8,128)(2,1)}, u32[]{:S(2)}, u32[]{:S(2)}) collective-permute-start(bf16[3,128,640]{2,1,0:T(8,128)(2,1)S(1)} %pad_maximum_fusion.3.refs_1_), channel_id=1, source_target_pairs={{0,8},{4,20},{8,0},{12,28},{16,24},{20,4},{24,16},{28,12},{1,9},{5... | collective-permute-start | bytes 1474568 | tf_op jit(solution)/shard_map/ppermute | solution.py:35
  38.8 19.5 %collective-permute-start.4 = (bf16[3,128,640]{2,1,0:T(8,128)(2,1)S(1)}, bf16[3,128,640]{2,1,0:T(8,128)(2,1)}, u32[]{:S(2)}, u32[]{:S(2)}) collective-permute-start(bf16[3,128,640]{2,1,0:T(8,128)(2,1)S(1)} %pad_maximum_fusion.3.refs_1_), channel_id=1, source_target_pairs={{0,16},{4,12},{8,24},{12,4},{16,0},{20,28},{24,8},{28,20},{1,17},{... | collective-permute-start | bytes 1474568 | tf_op jit(solution)/shard_map/ppermute | solution.py:35
  40.3 32.8 %collective-permute-start.6 = (bf16[3,128,640]{2,1,0:T(8,128)(2,1)S(1)}, bf16[3,128,640]{2,1,0:T(8,128)(2,1)}, u32[]{:S(2)}, u32[]{:S(2)}) collective-permute-start(bf16[3,128,640]{2,1,0:T(8,128)(2,1)S(1)} %pad_maximum_fusion.3.refs_1_), channel_id=1, source_target_pairs={{0,4},{4,0},{8,12},{12,8},{16,20},{20,16},{24,28},{28,24},{1,5},{5... | collective-permute-start | bytes 1474568 | tf_op jit(solution)/shard_map/ppermute | solution.py:35
  51.4 9.1 %collective-permute-start.5 = (bf16[3,128,640]{2,1,0:T(8,128)(2,1)}, bf16[3,128,640]{2,1,0:T(8,128)(2,1)}, u32[]{:S(2)}, u32[]{:S(2)}) collective-permute-start(bf16[3,128,640]{2,1,0:T(8,128)(2,1)} %collective-permute-done.3.refs_2_), channel_id=1, source_target_pairs={{0,16},{4,12},{8,24},{12,4},{16,0},{20,28},{24,8},{28,20},{1,17},{... | collective-permute-start | bytes 1474568 | tf_op jit(solution)/shard_map/ppermute | solution.py:35
  58.2 14.9 %collective-permute-start.7 = (bf16[3,128,640]{2,1,0:T(8,128)(2,1)}, bf16[3,128,640]{2,1,0:T(8,128)(2,1)}, u32[]{:S(2)}, u32[]{:S(2)}) collective-permute-start(bf16[3,128,640]{2,1,0:T(8,128)(2,1)} %collective-permute-done.3.refs_2_), channel_id=1, source_target_pairs={{0,4},{4,0},{8,12},{12,8},{16,20},{20,16},{24,28},{28,24},{1,5},{5... | collective-permute-start | bytes 1474568 | tf_op jit(solution)/shard_map/ppermute | solution.py:35
  58.3 14.9 %collective-permute-start.8 = (bf16[3,128,640]{2,1,0:T(8,128)(2,1)}, bf16[3,128,640]{2,1,0:T(8,128)(2,1)}, u32[]{:S(2)}, u32[]{:S(2)}) collective-permute-start(bf16[3,128,640]{2,1,0:T(8,128)(2,1)} %collective-permute-done.4.refs_3_), channel_id=1, source_target_pairs={{0,4},{4,0},{8,12},{12,8},{16,20},{20,16},{24,28},{28,24},{1,5},{5... | collective-permute-start | bytes 1474568 | tf_op jit(solution)/shard_map/ppermute | solution.py:35
  60.6 12.6 %collective-permute-start.9 = (bf16[3,128,640]{2,1,0:T(8,128)(2,1)}, bf16[3,128,640]{2,1,0:T(8,128)(2,1)}, u32[]{:S(2)}, u32[]{:S(2)}) collective-permute-start(bf16[3,128,640]{2,1,0:T(8,128)(2,1)} %collective-permute-done.5.refs_4_), channel_id=1, source_target_pairs={{0,4},{4,0},{8,12},{12,8},{16,20},{20,16},{24,28},{28,24},{1,5},{5... | collective-permute-start | bytes 1474568 | tf_op jit(solution)/shard_map/ppermute | solution.py:35
  77.7 18.1 %collective-permute-start.10 = (bf16[640,384]{1,0:T(8,128)(2,1)S(1)}, bf16[640,384]{1,0:T(8,128)(2,1)S(1)}, u32[]{:S(2)}, u32[]{:S(2)}) collective-permute-start(bf16[640,384]{1,0:T(8,128)(2,1)S(1)} %keys_values.2.refs_4_.refs_2_.refs_5_.refs_6_), channel_id=1, source_target_pairs={{0,1},{1,2},{2,3},{4,5},{5,6},{6,7},{8,9},{9,10},{10,11},{12,13},{... | collective-permute-start | bytes 1474568 | tf_op jit(solution)/shard_map/ppermute | solution.py:40
  84.7 33.8 %collective-permute-start.13 = (bf16[3,240,640]{2,1,0:T(8,128)(2,1)S(1)}, bf16[3,240,640]{2,1,0:T(8,128)(2,1)S(1)}, u32[]{:S(2)}, u32[]{:S(2)}) collective-permute-start(bf16[3,240,640]{2,1,0:T(8,128)(2,1)S(1)} %pad_maximum_fusion.2.refs_10_.refs_1_), channel_id=1, source_target_pairs={{0,8},{4,20},{8,0},{12,28},{16,24},{20,4},{24,16},{28,12},{1,9},{5... | collective-permute-start | bytes 2764808 | tf_op jit(solution)/shard_map/ppermute | solution.py:35
  85.0 33.5 %collective-permute-start.14 = (bf16[3,240,640]{2,1,0:T(8,128)(2,1)S(1)}, bf16[3,240,640]{2,1,0:T(8,128)(2,1)S(1)}, u32[]{:S(2)}, u32[]{:S(2)}) collective-permute-start(bf16[3,240,640]{2,1,0:T(8,128)(2,1)S(1)} %pad_maximum_fusion.2.refs_10_.refs_1_), channel_id=1, source_target_pairs={{0,16},{4,12},{8,24},{12,4},{16,0},{20,28},{24,8},{28,20},{1,17},{... | collective-permute-start | bytes 2764808 | tf_op jit(solution)/shard_map/ppermute | solution.py:35
  85.6 32.3 %collective-permute-start.15 = (bf16[3,80,960]{2,1,0:T(8,128)(2,1)S(1)}, bf16[3,80,960]{2,1,0:T(8,128)(2,1)S(1)}, u32[]{:S(2)}, u32[]{:S(2)}) collective-permute-start(bf16[3,80,960]{2,1,0:T(8,128)(2,1)S(1)} %pad_maximum_fusion.4.refs_11_.refs_1_), channel_id=1, source_target_pairs={{0,8},{4,20},{8,0},{12,28},{16,24},{20,4},{24,16},{28,12},{1,9},{5... | collective-permute-start | bytes 1382408 | tf_op jit(solution)/shard_map/ppermute | solution.py:35
  87.5 30.5 %collective-permute-start.16 = (bf16[3,80,960]{2,1,0:T(8,128)(2,1)S(1)}, bf16[3,80,960]{2,1,0:T(8,128)(2,1)S(1)}, u32[]{:S(2)}, u32[]{:S(2)}) collective-permute-start(bf16[3,80,960]{2,1,0:T(8,128)(2,1)S(1)} %pad_maximum_fusion.4.refs_11_.refs_1_), channel_id=1, source_target_pairs={{0,16},{4,12},{8,24},{12,4},{16,0},{20,28},{24,8},{28,20},{1,17},{... | collective-permute-start | bytes 1382408 | tf_op jit(solution)/shard_map/ppermute | solution.py:35
  95.8 24.7 %collective-permute-start.11 = (bf16[640,384]{1,0:T(8,128)(2,1)S(1)}, bf16[640,384]{1,0:T(8,128)(2,1)S(1)}, u32[]{:S(2)}, u32[]{:S(2)}) collective-permute-start(bf16[640,384]{1,0:T(8,128)(2,1)S(1)} %collective-permute-done.10.refs_2_.refs_5_.refs_6_), channel_id=1, source_target_pairs={{1,2},{2,3},{5,6},{6,7},{9,10},{10,11},{13,14},{14,15},{17,18},{18... | collective-permute-start | bytes 1474568 | tf_op jit(solution)/shard_map/ppermute | solution.py:40
  117.9 25.9 %collective-permute-start.19 = (bf16[3,240,640]{2,1,0:T(8,128)(2,1)S(1)}, bf16[3,240,640]{2,1,0:T(8,128)(2,1)S(1)}, u32[]{:S(2)}, u32[]{:S(2)}) collective-permute-start(bf16[3,240,640]{2,1,0:T(8,128)(2,1)S(1)} %pad_maximum_fusion.2.refs_10_.refs_1_), channel_id=1, source_target_pairs={{0,4},{4,0},{8,12},{12,8},{16,20},{20,16},{24,28},{28,24},{1,5},{5... | collective-permute-start | bytes 2764808 | tf_op jit(solution)/shard_map/ppermute | solution.py:35
  117.9 21.3 %collective-permute-start.23 = (bf16[3,80,960]{2,1,0:T(8,128)(2,1)S(1)}, bf16[3,80,960]{2,1,0:T(8,128)(2,1)S(1)}, u32[]{:S(2)}, u32[]{:S(2)}) collective-permute-start(bf16[3,80,960]{2,1,0:T(8,128)(2,1)S(1)} %pad_maximum_fusion.4.refs_11_.refs_1_), channel_id=1, source_target_pairs={{0,4},{4,0},{8,12},{12,8},{16,20},{20,16},{24,28},{28,24},{1,5},{5... | collective-permute-start | bytes 1382408 | tf_op jit(solution)/shard_map/ppermute | solution.py:35
  118.4 18.7 %collective-permute-start.17 = (bf16[3,240,640]{2,1,0:T(8,128)(2,1)S(1)}, bf16[3,240,640]{2,1,0:T(8,128)(2,1)S(1)}, u32[]{:S(2)}, u32[]{:S(2)}) collective-permute-start(bf16[3,240,640]{2,1,0:T(8,128)(2,1)S(1)} %collective-permute-done.13.refs_2_), channel_id=1, source_target_pairs={{0,16},{4,12},{8,24},{12,4},{16,0},{20,28},{24,8},{28,20},{1,17},{... | collective-permute-start | bytes 2764808 | tf_op jit(solution)/shard_map/ppermute | solution.py:35
  119.5 17.7 %collective-permute-start.18 = (bf16[3,80,960]{2,1,0:T(8,128)(2,1)S(1)}, bf16[3,80,960]{2,1,0:T(8,128)(2,1)S(1)}, u32[]{:S(2)}, u32[]{:S(2)}) collective-permute-start(bf16[3,80,960]{2,1,0:T(8,128)(2,1)S(1)} %collective-permute-done.15.refs_2_), channel_id=1, source_target_pairs={{0,16},{4,12},{8,24},{12,4},{16,0},{20,28},{24,8},{28,20},{1,17},{... | collective-permute-start | bytes 1382408 | tf_op jit(solution)/shard_map/ppermute | solution.py:35
  120.5 17.2 %collective-permute-start.12 = (bf16[640,384]{1,0:T(8,128)(2,1)S(1)}, bf16[640,384]{1,0:T(8,128)(2,1)S(1)}, u32[]{:S(2)}, u32[]{:S(2)}) collective-permute-start(bf16[640,384]{1,0:T(8,128)(2,1)S(1)} %collective-permute-done.11.refs_2_.refs_5_.refs_6_), channel_id=1, source_target_pairs={{2,3},{6,7},{10,11},{14,15},{18,19},{22,23},{26,27},{30,31}} | collective-permute-start | bytes 1474568 | tf_op jit(solution)/shard_map/ppermute | solution.py:40
  171.2 12.3 %collective-permute-start.27 = (bf16[320,384]{1,0:T(8,128)(2,1)S(1)}, bf16[320,384]{1,0:T(8,128)(2,1)S(1)}, u32[]{:S(2)}, u32[]{:S(2)}) collective-permute-start(bf16[320,384]{1,0:T(8,128)(2,1)S(1)} %get-tuple-element.160.refs_4_.refs_2_.refs_5_), channel_id=1, source_target_pairs={{0,1},{1,2},{2,3},{4,5},{5,6},{6,7},{8,9},{9,10},{10,11},{12,13},{... | collective-permute-start | bytes 737288 | tf_op jit(solution)/shard_map/ppermute | solution.py:40
  173.4 10.8 %collective-permute-start.30 = (bf16[320,384]{1,0:T(8,128)(2,1)S(1)}, bf16[320,384]{1,0:T(8,128)(2,1)S(1)}, u32[]{:S(2)}, u32[]{:S(2)}) collective-permute-start(bf16[320,384]{1,0:T(8,128)(2,1)S(1)} %get-tuple-element.161.refs_3_.refs_6_), channel_id=1, source_target_pairs={{0,1},{1,2},{2,3},{4,5},{5,6},{6,7},{8,9},{9,10},{10,11},{12,13},{... | collective-permute-start | bytes 737288 | tf_op jit(solution)/shard_map/ppermute | solution.py:40
  235.7 54.8 %collective-permute-start.35 = (bf16[2,320,384]{2,1,0:T(8,128)(2,1)S(1)}, bf16[2,320,384]{2,1,0:T(8,128)(2,1)S(1)}, u32[]{:S(2)}, u32[]{:S(2)}) collective-permute-start(bf16[2,320,384]{2,1,0:T(8,128)(2,1)S(1)} %add_convert_fusion.10), channel_id=1, source_target_pairs={{1,0},{2,1},{3,2},{5,4},{6,5},{7,6},{9,8},{10,9},{11,10},{13,12},{... | collective-permute-start | bytes 1474568 | tf_op jit(solution)/shard_map/ppermute | solution.py:843
  315.2 29.8 %collective-permute-start.37 = (bf16[2,4,80,960]{3,2,1,0:T(8,128)(2,1)}, bf16[2,4,80,960]{3,2,1,0:T(8,128)(2,1)}, u32[]{:S(2)}, u32[]{:S(2)}) collective-permute-start(bf16[2,4,80,960]{3,2,1,0:T(8,128)(2,1)} %get-tuple-element.190), channel_id=1, source_target_pairs={{0,8},{4,20},{8,0},{12,28},{16,24},{20,4},{24,16},{28,12},{1,9},{5... | collective-permute-start | bytes 3686408 | tf_op jit(solution)/shard_map/ppermute | solution.py:35
  344.9 14.5 %collective-permute-start.39 = (bf16[4,4,240,640]{3,2,1,0:T(8,128)(2,1)}, bf16[4,4,240,640]{3,2,1,0:T(8,128)(2,1)}, u32[]{:S(2)}, u32[]{:S(2)}) collective-permute-start(bf16[4,4,240,640]{3,2,1,0:T(8,128)(2,1)} %get-tuple-element.207), channel_id=1, source_target_pairs={{0,4},{4,0},{8,12},{12,8},{16,20},{20,16},{24,28},{28,24},{1,5},{5... | collective-permute-start | bytes 14745608 | tf_op jit(solution)/shard_map/ppermute | solution.py:35
  346.5 10.7 %collective-permute-start.38 = (bf16[4,80,960]{2,1,0:T(8,128)(2,1)S(1)}, bf16[4,80,960]{2,1,0:T(8,128)(2,1)S(1)}, u32[]{:S(2)}, u32[]{:S(2)}) collective-permute-start(bf16[4,80,960]{2,1,0:T(8,128)(2,1)S(1)} %fusion.25), channel_id=1, source_target_pairs={{0,16},{4,12},{8,24},{12,4},{16,0},{20,28},{24,8},{28,20},{1,17},{... | collective-permute-start | bytes 1843208 | tf_op jit(solution)/shard_map/ppermute | solution.py:35
  349.0 25.2 %collective-permute-start.41 = (bf16[2,320,384]{2,1,0:T(8,128)(2,1)S(1)}, bf16[2,320,384]{2,1,0:T(8,128)(2,1)}, u32[]{:S(2)}, u32[]{:S(2)}) collective-permute-start(bf16[2,320,384]{2,1,0:T(8,128)(2,1)S(1)} %get-tuple-element.220), channel_id=1, source_target_pairs={{3,2},{7,6},{11,10},{15,14},{19,18},{23,22},{27,26},{31,30}} | collective-permute-start | bytes 1474568 | tf_op jit(solution)/shard_map/ppermute | solution.py:843
  370.3 30.1 %collective-permute-start.40 = (bf16[2,4,240,640]{3,2,1,0:T(8,128)(2,1)}, bf16[2,4,240,640]{3,2,1,0:T(8,128)(2,1)S(1)}, u32[]{:S(2)}, u32[]{:S(2)}) collective-permute-start(bf16[2,4,240,640]{3,2,1,0:T(8,128)(2,1)} %get-tuple-element.211), channel_id=1, source_target_pairs={{0,8},{4,20},{8,0},{12,28},{16,24},{20,4},{24,16},{28,12},{1,9},{5... | collective-permute-start | bytes 7372808 | tf_op jit(solution)/shard_map/ppermute | solution.py:35
  377.1 38.1 %collective-permute-start.43 = (bf16[2,320,384]{2,1,0:T(8,128)(2,1)S(1)}, bf16[2,320,384]{2,1,0:T(8,128)(2,1)S(1)}, u32[]{:S(2)}, u32[]{:S(2)}) collective-permute-start(bf16[2,320,384]{2,1,0:T(8,128)(2,1)S(1)} %add_convert_fusion.8), channel_id=1, source_target_pairs={{1,0},{2,1},{3,2},{5,4},{6,5},{7,6},{9,8},{10,9},{11,10},{13,12},{... | collective-permute-start | bytes 1474568 | tf_op jit(solution)/shard_map/ppermute | solution.py:843
  400.8 22.4 %collective-permute-start.44 = (bf16[4,240,640]{2,1,0:T(8,128)(2,1)S(1)}, bf16[4,240,640]{2,1,0:T(8,128)(2,1)S(1)}, u32[]{:S(2)}, u32[]{:S(2)}) collective-permute-start(bf16[4,240,640]{2,1,0:T(8,128)(2,1)S(1)} %fusion.20), channel_id=1, source_target_pairs={{0,16},{4,12},{8,24},{12,4},{16,0},{20,28},{24,8},{28,20},{1,17},{... | collective-permute-start | bytes 3686408 | tf_op jit(solution)/shard_map/ppermute | solution.py:35
  402.3 15.4 %collective-permute-start.45 = (bf16[80,960]{1,0:T(8,128)(2,1)S(1)}, bf16[80,960]{1,0:T(8,128)(2,1)S(1)}, u32[]{:S(2)}, u32[]{:S(2)}) collective-permute-start(bf16[80,960]{1,0:T(8,128)(2,1)S(1)} %copy-done.117), channel_id=1, source_target_pairs={{0,1},{1,2},{2,3},{3,0},{4,5},{5,6},{6,7},{7,4},{8,9},{9,10},{10,1... | collective-permute-start | bytes 460808 | tf_op jit(solution)/shard_map/ppermute | solution.py:57
  404.1 19.1 %collective-permute-start.46 = (bf16[80,960]{1,0:T(8,128)(2,1)S(1)}, bf16[80,960]{1,0:T(8,128)(2,1)S(1)}, u32[]{:S(2)}, u32[]{:S(2)}) collective-permute-start(bf16[80,960]{1,0:T(8,128)(2,1)S(1)} %copy-done.116), channel_id=1, source_target_pairs={{0,2},{1,3},{2,0},{3,1},{4,6},{5,7},{6,4},{7,5},{8,10},{9,11},{10,... | collective-permute-start | bytes 460808 | tf_op jit(solution)/shard_map/ppermute | solution.py:57
  405.3 17.9 %collective-permute-start.47 = (bf16[80,960]{1,0:T(8,128)(2,1)S(1)}, bf16[80,960]{1,0:T(8,128)(2,1)S(1)}, u32[]{:S(2)}, u32[]{:S(2)}) collective-permute-start(bf16[80,960]{1,0:T(8,128)(2,1)S(1)} %copy-done.115), channel_id=1, source_target_pairs={{0,3},{1,0},{2,1},{3,2},{4,7},{5,4},{6,5},{7,6},{8,11},{9,8},{10,9... | collective-permute-start | bytes 460808 | tf_op jit(solution)/shard_map/ppermute | solution.py:57
  439.8 18.8 %collective-permute-start.51 = (bf16[2,4,120,640]{3,2,1,0:T(8,128)(2,1)S(1)}, bf16[2,4,120,640]{3,2,1,0:T(8,128)(2,1)S(1)}, u32[]{:S(2)}, u32[]{:S(2)}) collective-permute-start(bf16[2,4,120,640]{3,2,1,0:T(8,128)(2,1)S(1)} %add_convert_fusion), channel_id=1, source_target_pairs={{0,8},{4,20},{8,0},{12,28},{16,24},{20,4},{24,16},{28,12},{1,9},{5... | collective-permute-start | bytes 3686408 | tf_op jit(solution)/shard_map/ppermute | solution.py:35
  441.4 12.0 %collective-permute-start.52 = (bf16[240,640]{1,0:T(8,128)(2,1)S(1)}, bf16[240,640]{1,0:T(8,128)(2,1)S(1)}, u32[]{:S(2)}, u32[]{:S(2)}) collective-permute-start(bf16[240,640]{1,0:T(8,128)(2,1)S(1)} %get-tuple-element.289), channel_id=1, source_target_pairs={{0,1},{1,2},{2,3},{3,0},{4,5},{5,6},{6,7},{7,4},{8,9},{9,10},{10,1... | collective-permute-start | bytes 921608 | tf_op jit(solution)/shard_map/ppermute | solution.py:57
  443.7 14.9 %collective-permute-start.53 = (bf16[240,640]{1,0:T(8,128)(2,1)S(1)}, bf16[240,640]{1,0:T(8,128)(2,1)S(1)}, u32[]{:S(2)}, u32[]{:S(2)}) collective-permute-start(bf16[240,640]{1,0:T(8,128)(2,1)S(1)} %get-tuple-element.288), channel_id=1, source_target_pairs={{0,3},{1,0},{2,1},{3,2},{4,7},{5,4},{6,5},{7,6},{8,11},{9,8},{10,9... | collective-permute-start | bytes 921608 | tf_op jit(solution)/shard_map/ppermute | solution.py:57
  445.2 13.3 %collective-permute-start.54 = (bf16[80,960]{1,0:T(8,128)(2,1)S(1)}, bf16[80,960]{1,0:T(8,128)(2,1)S(1)}, u32[]{:S(2)}, u32[]{:S(2)}) collective-permute-start(bf16[80,960]{1,0:T(8,128)(2,1)S(1)} %collective-permute-done.49.refs_3_), channel_id=1, source_target_pairs={{0,8},{4,20},{8,0},{12,28},{16,24},{20,4},{24,16},{28,12},{1,9},{5... | collective-permute-start | bytes 460808 | tf_op jit(solution)/shard_map/ppermute | solution.py:35
  459.8 10.5 %collective-permute-start.55 = (bf16[4,120,640]{2,1,0:T(8,128)(2,1)}, bf16[4,120,640]{2,1,0:T(8,128)(2,1)}, u32[]{:S(2)}, u32[]{:S(2)}) collective-permute-start(bf16[4,120,640]{2,1,0:T(8,128)(2,1)} %fusion.28), channel_id=1, source_target_pairs={{0,16},{4,12},{8,24},{12,4},{16,0},{20,28},{24,8},{28,20},{1,17},{... | collective-permute-start | bytes 1843208 | tf_op jit(solution)/shard_map/ppermute | solution.py:35
  464.3 17.4 %collective-permute-start.56 = (bf16[240,640]{1,0:T(8,128)(2,1)}, bf16[240,640]{1,0:T(8,128)(2,1)S(1)}, u32[]{:S(2)}, u32[]{:S(2)}) collective-permute-start(bf16[240,640]{1,0:T(8,128)(2,1)} %get-tuple-element.287), channel_id=1, source_target_pairs={{0,2},{1,3},{2,0},{3,1},{4,6},{5,7},{6,4},{7,5},{8,10},{9,11},{10,... | collective-permute-start | bytes 921608 | tf_op jit(solution)/shard_map/ppermute | solution.py:57
  486.0 15.2 %collective-permute-start.60 = (bf16[240,640]{1,0:T(8,128)(2,1)S(1)}, bf16[240,640]{1,0:T(8,128)(2,1)S(1)}, u32[]{:S(2)}, u32[]{:S(2)}) collective-permute-start(bf16[240,640]{1,0:T(8,128)(2,1)S(1)} %add_convert_fusion.12.refs_1_), channel_id=1, source_target_pairs={{0,8},{4,20},{8,0},{12,28},{16,24},{20,4},{24,16},{28,12},{1,9},{5... | collective-permute-start | bytes 921608 | tf_op jit(solution)/shard_map/ppermute | solution.py:35
  488.3 12.3 %collective-permute-start.58 = (bf16[120,640]{1,0:T(8,128)(2,1)S(1)}, bf16[120,640]{1,0:T(8,128)(2,1)S(1)}, u32[]{:S(2)}, u32[]{:S(2)}) collective-permute-start(bf16[120,640]{1,0:T(8,128)(2,1)S(1)} %get-tuple-element.241), channel_id=1, source_target_pairs={{0,2},{1,3},{2,0},{3,1},{4,6},{5,7},{6,4},{7,5},{8,10},{9,11},{10,... | collective-permute-start | bytes 460808 | tf_op jit(solution)/shard_map/ppermute | solution.py:57
  488.3 12.3 %collective-permute-start.57 = (bf16[120,640]{1,0:T(8,128)(2,1)S(1)}, bf16[120,640]{1,0:T(8,128)(2,1)S(1)}, u32[]{:S(2)}, u32[]{:S(2)}) collective-permute-start(bf16[120,640]{1,0:T(8,128)(2,1)S(1)} %get-tuple-element.240), channel_id=1, source_target_pairs={{0,1},{1,2},{2,3},{3,0},{4,5},{5,6},{6,7},{7,4},{8,9},{9,10},{10,1... | collective-permute-start | bytes 460808 | tf_op jit(solution)/shard_map/ppermute | solution.py:57
  489.3 12.1 %collective-permute-start.62 = (bf16[240,640]{1,0:T(8,128)(2,1)S(1)}, bf16[240,640]{1,0:T(8,128)(2,1)S(1)}, u32[]{:S(2)}, u32[]{:S(2)}) collective-permute-start(bf16[240,640]{1,0:T(8,128)(2,1)S(1)} %collective-permute-done.61.refs_3_), channel_id=1, source_target_pairs={{0,8},{4,20},{8,0},{12,28},{16,24},{20,4},{24,16},{28,12},{1,9},{5... | collective-permute-start | bytes 921608 | tf_op jit(solution)/shard_map/ppermute | solution.py:35
  492.8 15.5 %collective-permute-start.74 = (bf16[80,960]{1,0:T(8,128)(2,1)S(1)}, bf16[80,960]{1,0:T(8,128)(2,1)S(1)}, u32[]{:S(2)}, u32[]{:S(2)}) collective-permute-start(bf16[80,960]{1,0:T(8,128)(2,1)S(1)} %copy-done.29), channel_id=1, source_target_pairs={{0,4},{4,0},{8,12},{12,8},{16,20},{20,16},{24,28},{28,24},{1,5},{5... | collective-permute-start | bytes 460808 | tf_op jit(solution)/shard_map/ppermute | solution.py:35
  500.6 8.2 %collective-permute-start.76 = (bf16[80,960]{1,0:T(8,128)(2,1)S(1)}, bf16[80,960]{1,0:T(8,128)(2,1)S(1)}, u32[]{:S(2)}, u32[]{:S(2)}) collective-permute-start(bf16[80,960]{1,0:T(8,128)(2,1)S(1)} %copy-done.57), channel_id=1, source_target_pairs={{0,4},{4,0},{8,12},{12,8},{16,20},{20,16},{24,28},{28,24},{1,5},{5... | collective-permute-start | bytes 460808 | tf_op jit(solution)/shard_map/ppermute | solution.py:35
  511.8 9.3 %collective-permute-start.70 = (bf16[120,640]{1,0:T(8,128)(2,1)S(1)}, bf16[120,640]{1,0:T(8,128)(2,1)S(1)}, u32[]{:S(2)}, u32[]{:S(2)}) collective-permute-start(bf16[120,640]{1,0:T(8,128)(2,1)S(1)} %add_convert_fusion.14.refs_1_), channel_id=1, source_target_pairs={{0,4},{4,0},{8,12},{12,8},{16,20},{20,16},{24,28},{28,24},{1,5},{5... | collective-permute-start | bytes 460808 | tf_op jit(solution)/shard_map/ppermute | solution.py:35
  (164 other events, 1416.4 us)
Sparse Core Ops, SparseCore 0:
  23.9 46.6 all-gather.2

commit v2 on v1

--- a/solution.py
+++ b/solution.py
@@ -530,8 +530,8 @@
 
 
 def attend_back_kernel(d, place_ref, q_ref, o_ref, do_ref, lse_ref, k_ref, v_ref, *refs):
-    dq_ref, dkv_ref = refs[-2:]
-    before_ref = None if len(refs) == 2 else refs[-3]
+    dq_ref, dk_ref, dv_ref = refs[-3:]
+    before_ref = None if len(refs) == 3 else refs[-4]
     z, room = place_ref[0], place_ref[1]
     rows = q_ref.shape[1]
 
@@ -547,8 +547,8 @@
         p = jnp.exp(s - lse)
         dp = product(v, do, 0, 0)
         ds = (p * (dp - delta)).astype(bf16)
-        dkv_ref[1] = product(p.astype(bf16), do, 1, 1).T.astype(bf16)
-        dkv_ref[0] = product(ds, q, 1, 1).T.astype(bf16)
+        dv_ref[...] = product(p.astype(bf16), do, 1, 1).T.astype(bf16)
+        dk_ref[...] = product(ds, q, 1, 1).T.astype(bf16)
         dq = product(k, ds, 1, 0) * HD ** (-0.5)
         for g in range(GROUP):
             here = slice(HD * g, HD * (g + 1))
@@ -563,7 +563,8 @@
 
         @pl.when(z < d)
         def _():
-            dkv_ref[...] = jnp.zeros(dkv_ref.shape, bf16)
+            dk_ref[...] = jnp.zeros(dk_ref.shape, bf16)
+            dv_ref[...] = jnp.zeros(dv_ref.shape, bf16)
             if before_ref is None:
                 dq_ref[...] = jnp.zeros(dq_ref.shape, f32)
             else:
@@ -590,10 +591,11 @@
         scalars=1,
         grid=(KV_HEADS,),
         in_specs=[q_spec, q_spec, q_spec, lse_spec, k_spec, v_spec] + extra_specs,
-        out_specs=[q_spec, kv_spec],
+        out_specs=[q_spec, k_spec, k_spec],
         out_shape=[
             jax.ShapeDtypeStruct(q.shape, f32 if d else bf16),
-            jax.ShapeDtypeStruct((2, KV, rows), bf16),
+            jax.ShapeDtypeStruct((KV, rows), bf16),
+            jax.ShapeDtypeStruct((KV, rows), bf16),
         ],
         compiler_params=pltpu.CompilerParams(vmem_limit_bytes=32 * 2**20),
         name="attend_back",
@@ -605,18 +607,21 @@
     rows = dq.shape[1]
     lanes = 2 * KV + dq.shape[0] + low.shape[1]
 
-    def kernel(own_ref, got_ref, dq_ref, low_ref, cos_ref, sin_ref, out_ref):
-        dkv = own_ref[...].astype(f32) + got_ref[...].astype(f32)
-        keys = turn(dkv[0], cos_ref[...], -sin_ref[...], KV_HEADS).astype(bf16)
-        sides = jnp.concatenate([keys, dkv[1].astype(bf16), dq_ref[...]], axis=0)
+    def kernel(
+        dk_ref, dv_ref, got_k_ref, got_v_ref, dq_ref, low_ref, cos_ref, sin_ref, out_ref
+    ):
+        dk = dk_ref[...].astype(f32) + got_k_ref[...].astype(f32)
+        dv = dv_ref[...].astype(f32) + got_v_ref[...].astype(f32)
+        keys = turn(dk, cos_ref[...], -sin_ref[...], KV_HEADS).astype(bf16)
+        sides = jnp.concatenate([keys, dv.astype(bf16), dq_ref[...]], axis=0)
         out_ref[...] = jnp.concatenate([sides.T, low_ref[...]], axis=1)
 
     vmem = pl.BlockSpec(memory_space=pltpu.VMEM)
     return call(
         kernel,
-        [own, got, dq, low, *tables],
+        [*own, *got, dq, low, *tables],
         wait_for,
-        in_specs=[vmem] * 6,
+        in_specs=[vmem] * 8,
         out_specs=vmem,
         out_shape=jax.ShapeDtypeStruct((rows, lanes), bf16),
         compiler_params=pltpu.CompilerParams(vmem_limit_bytes=16 * 2**20),
@@ -840,14 +845,13 @@
         if d in before:
             wait_for, dq = before[d](dq)
         if step:
-            got = lax.ppermute(
-                moving, "fsdp", [(i, i - 1) for i in range(count - step, count)]
-            )
-        dq, dkv = attend_back(
+            pairs = [(i, i - 1) for i in range(count - step, count)]
+            got = [lax.ppermute(v, "fsdp", pairs) for v in moving]
+        dq, *dkv = attend_back(
             d, where, q, mixture, d_mixture, lse, kvs[d], dq, tables, wait_for
         )
         if d:
-            moving = add(dkv, got) if step else dkv
+            moving = [add(a, b) for a, b in zip(dkv, got)] if step else dkv
     wait_for, dq = at_end(dq)
     return gradient_columns(dkv, got, dq, low, tables, wait_for)
 

time: 544 us -> 539 us (level)
  waiting for transfers between devices: 183 us -> 167 us
  starting transfers between devices: 73.9 us -> 84.9 us
    ppermute x6 -> x12, waiting for transfers between devices: 45 us -> 36.8 us  [attention_gradient(): got = [lax.ppermute(v, 'fsdp', pairs) for v in moving]]
    ppermute x6 -> x12, starting transfers between devices: 6.81 us -> 12 us  [attention_gradient(): got = [lax.ppermute(v, 'fsdp', pairs) for v in moving]]
    unnamed x274 -> x272, local copies, waits for them, and re-layouts: 39.3 us -> 39.3 us
  transfers between devices with their start and end apart: 79 -> 85, of which waited for: 24 -> 23; matrix products, arithmetic and copies ran while one was open for 10% -> 10% of each run, Pallas kernels for 15% -> 15%
where the time goes in v2:
time: 539 us; the launch traced here: 528 us
  waiting for transfers between devices  167 us (31%)
  Pallas kernels  159 us (29%)
  starting transfers between devices  84.9 us (16%)
  local copies, waits for them, and re-layouts  58.8 us (11%)
  other arithmetic  36.1 us (7%)
  between operations  17.1 us (3%)
  matrix products  5.47 us (1%)
    pallas_call x36, Pallas kernels, call(): return pl.pallas_call(waiting, **where, **rest)(*operands, *wait_for)  131 us
    ppermute x51, waiting for transfers between devices, swap(): return lax.ppermute(value, 'dp', [(i, hop(i)) for i in range(count)])  84.3 us
    unnamed x272, local copies, waits for them, and re-layouts  39.3 us
    ppermute x12, waiting for transfers between devices, attention_gradient(): got = [lax.ppermute(v, 'fsdp', pairs) for v in moving]  36.8 us
    ppermute x12, waiting for transfers between devices, around(): lax.ppermute(value, 'fsdp', [(i, (i + distance) % count) for i in range(c...  34.4 us
    ppermute x51, starting transfers between devices, swap(): return lax.ppermute(value, 'dp', [(i, hop(i)) for i in range(count)])  34 us
    pallas_call x2, Pallas kernels, feed_forward(): pl.pallas_call(feed_forward_kernel, grid=(5,), in_specs=[whole(rows, mode...  27.7 us
    ppermute x12, starting transfers between devices, around(): lax.ppermute(value, 'fsdp', [(i, (i + distance) % count) for i in range(c...  23.4 us
  transfers between devices with their start and end apart: 85, of which 23 were waited for; matrix products, arithmetic and copies ran while one was open for 10% of the time, Pallas kernels for 15%

profile of v2, /device:TPU:0, one launch (start us, length us, event | category | flops | bytes accessed | tf_op | source)
XLA Modules:
  0.0 528.3 jit_solution(8279982478172398247)
XLA Ops:
  10.8 2.4 concatenate.29.refs_9_
  15.7 3.1 collective-permute-start.2
  18.8 2.6 collective-permute-start.1
  28.5 2.3 copy.33
  31.7 2.8 fusion.35
  42.5 8.8 %collective-permute-done.3.refs_2_ = bf16[3,128,640]{2,1,0:T(8,128)(2,1)} collective-permute-done((bf16[3,128,640]{2,1,0:T(8,128)(2,1)S(1)}, bf16[3,128,640]{2,1,0:T(8,128)(2,1)}, u32[]{:S(2)}, u32[]{:S(2)}) %collective-permute-start.3) | collective-permute-done | bytes 491552 | tf_op jit(solution)/shard_map/ppermute | solution.py:35
  53.7 2.3 copy.32
  60.5 10.1 %all-gather.3.cloned.1.call-done = bf16[1600,640]{1,0:T(8,128)(2,1)} async-done(((bf16[400,640]{1,0:T(8,128)(2,1)}), bf16[1600,640]{1,0:T(8,128)(2,1)}) %all-gather.3.cloned.1.call-update) | async-done | bytes 2048016 | tf_op jit(solution)/shard_map/all_gather | solution.py:914
  73.2 2.4 lay_out.3.refs_1_
  77.7 6.9 %collective-permute-start.10 = (bf16[640,384]{1,0:T(8,128)(2,1)S(1)}, bf16[640,384]{1,0:T(8,128)(2,1)S(1)}, u32[]{:S(2)}, u32[]{:S(2)}) collective-permute-start(bf16[640,384]{1,0:T(8,128)(2,1)S(1)} %keys_values.2.refs_4_.refs_2_.refs_5_.refs_6_), channel_id=1, source_target_pairs={{0,1},{1,2},{2,3},{4,5},{5,6},{6,7},{8,9},{9,10},{10,11},{12,13},{... | collective-permute-start | bytes 1474568 | tf_op jit(solution)/shard_map/ppermute | solution.py:40
  88.7 3.4 attend.8
  97.1 20.8 %collective-permute-done.15.refs_2_ = bf16[3,80,960]{2,1,0:T(8,128)(2,1)S(1)} collective-permute-done((bf16[3,80,960]{2,1,0:T(8,128)(2,1)S(1)}, bf16[3,80,960]{2,1,0:T(8,128)(2,1)S(1)}, u32[]{:S(2)}, u32[]{:S(2)}) %collective-permute-start.15) | collective-permute-done | bytes 460832 | tf_op jit(solution)/shard_map/ppermute | solution.py:35
  121.8 15.3 %collective-permute-done.18.refs_4_ = bf16[3,80,960]{2,1,0:T(8,128)(2,1)S(1)} collective-permute-done((bf16[3,80,960]{2,1,0:T(8,128)(2,1)S(1)}, bf16[3,80,960]{2,1,0:T(8,128)(2,1)S(1)}, u32[]{:S(2)}, u32[]{:S(2)}) %collective-permute-start.18) | collective-permute-done | bytes 460832 | tf_op jit(solution)/shard_map/ppermute | solution.py:35
  150.2 13.8 %feed_forward.2 = (f32[384,960]{1,0:T(8,128)S(1)}, f32[384,960]{1,0:T(8,128)S(1)}, bf16[384,2560]{1,0:T(8,128)(2,1)}, bf16[384,2560]{1,0:T(8,128)(2,1)}, bf16[96...) custom-call(f32[384,960]{1,0:T(8,128)} %bitcast_convert_fusion.x_ref, ...), custom_call_target="tpu_custom_call" | custom-call | flops 82800001024 | tf_op jit(solution)/shard_map/feed_forward/pallas_call | solution.py:677
  175.6 3.2 attend.12
  181.2 2.3 copy.34
  191.1 4.7 attend.15
  198.2 13.9 %feed_forward.3 = (f32[384,960]{1,0:T(8,128)S(1)}, f32[384,960]{1,0:T(8,128)S(1)}, bf16[384,2560]{1,0:T(8,128)(2,1)}, bf16[384,2560]{1,0:T(8,128)(2,1)}, bf16[96...) custom-call(f32[384,960]{1,0:T(8,128)} %copy-done.1, ...), custom_call_target="tpu_custom_call", output_to_operand_aliasing={{4}: (7, {}), {5}: (8, {})} | custom-call | flops 82800001024 | tf_op jit(solution)/shard_map/feed_forward/pallas_call | solution.py:677
  213.3 16.9 %feed_forward_back.2 = (bf16[2,768,2560]{2,1,0:T(8,128)(2,1)}, f32[384,960]{1,0:T(8,128)S(1)}, bf16[384,960]{1,0:T(8,128)(2,1)S(1)}, bf16[960,384]{1,0:T(8,128)(2,1)S(1)}) custom-call(f32[384,960]{1,0:T(8,128)S(1)} %copy-done.10, f32[384,960]{1,0:T(8,128)} %copy-done.83, f32[1,960]{1,0:T(1,128)S(1)} %slice.162.gain_ref.refs_2_, ...), custom_call_target="tpu_custom_call" | custom-call | flops 124200001536 | tf_op jit(solution)/shard_map/feed_forward_back/pallas_call | solution.py:82
  240.9 7.1 %attend_back.11 = (bf16[960,384]{1,0:T(8,128)(2,1)S(1)}, bf16[320,384]{1,0:T(8,128)(2,1)S(1)}, bf16[320,384]{1,0:T(8,128)(2,1)S(1)}) custom-call(s32[2]{0:T(128)S(1)} %copy-done.61, bf16[960,384]{1,0:T(8,128)(2,1)S(1)} %copy-done.68, bf16[960,384]{1,0:T(8,128)(2,1)S(1)} %get-tuple-element.176.mix_ref.refs_2_, bf16[960,384]{1,0:T(8,128)(2,1)S(1)} %copy-done.82, ...), custom_call_target="tpu_custom_call" | custom-call | flops 48299999232 | tf_op jit(solution)/shard_map/attend_back/pallas_call | solution.py:82
  248.0 33.9 %collective-permute-done.35.refs_2_ = bf16[320,384]{1,0:T(8,128)(2,1)S(1)} collective-permute-done((bf16[320,384]{1,0:T(8,128)(2,1)S(1)}, bf16[320,384]{1,0:T(8,128)(2,1)S(1)}, u32[]{:S(2)}, u32[]{:S(2)}) %collective-permute-start.35) | collective-permute-done | bytes 245792 | tf_op jit(solution)/shard_map/ppermute | solution.py:849
  281.9 2.9 collective-permute-done.38.refs_3_
  290.4 6.5 %weight_grad.6 = (bf16[4,4,80,960]{3,2,1,0:T(8,128)(2,1)}, f32[8,128]{1,0:T(8,128)}) custom-call(s32[4]{0:T(128)} %pad_add_fusion.3.refs_0_, bf16[4,8,80,768]{3,2,1,0:T(8,128)(2,1)} %bitcast.138, bf16[768,960]{1,0:T(8,128)(2,1)} %pad_maximum_fusion.1.refs_2_), custom_call_target="tpu_custom_call" | custom-call | flops 38640001024 | tf_op jit(solution)/shard_map/weight_grad/pallas_call | solution.py:82
  297.5 4.7 collective-permute-done.39.refs_3_
  302.2 7.3 %weight_grad.7 = (bf16[2,4,80,960]{3,2,1,0:T(8,128)(2,1)}, bf16[2,4,80,960]{3,2,1,0:T(8,128)(2,1)}, f32[8,128]{1,0:T(8,128)}) custom-call(s32[4]{0:T(128)} %pad_add_fusion.2.refs_0_, bf16[4,8,80,768]{3,2,1,0:T(8,128)(2,1)} %bitcast.139, bf16[768,960]{1,0:T(8,128)(2,1)} %pad_maximum_fusion.1.refs_2_, bf16[4,4,80,960]{3,2,1,0:T(8,128)(2,1)} %collective-permute-done.39.refs_3_, ...), custom_call_target="tpu_custom_call" | custom-call | flops 38640001024 | tf_op jit(solution)/shard_map/weight_grad/pallas_call | solution.py:82
  312.3 16.3 %feed_forward_back.3 = (bf16[2,768,2560]{2,1,0:T(8,128)(2,1)}, f32[384,960]{1,0:T(8,128)S(1)}, bf16[384,960]{1,0:T(8,128)(2,1)S(1)}, bf16[960,384]{1,0:T(8,128)(2,1)S(1)}) custom-call(f32[384,960]{1,0:T(8,128)S(1)} %get-tuple-element.293.refs_0_, f32[384,960]{1,0:T(8,128)} %copy-done.84, ...), custom_call_target="tpu_custom_call", output_to_operand_aliasing={{0}: (9, {})} | custom-call | flops 124200001536 | tf_op jit(solution)/shard_map/feed_forward_back/pallas_call | solution.py:82
  329.8 9.4 %weight_grad.8 = (bf16[4,4,240,640]{3,2,1,0:T(8,128)(2,1)}, f32[8,128]{1,0:T(8,128)}) custom-call(s32[4]{0:T(128)} %pad_add_fusion.3.refs_0_, bf16[960,768]{1,0:T(8,128)(2,1)} %copy-done.77, bf16[2,768,2560]{2,1,0:T(8,128)(2,1)} %get-tuple-element.213.refs_2_), custom_call_target="tpu_custom_call" | custom-call | flops 60720001024 | tf_op jit(solution)/shard_map/weight_grad/pallas_call | solution.py:82
  345.4 6.0 %collective-permute-done.41 = bf16[4,80,960]{2,1,0:T(8,128)(2,1)S(1)} collective-permute-done((bf16[4,80,960]{2,1,0:T(8,128)(2,1)S(1)}, bf16[4,80,960]{2,1,0:T(8,128)(2,1)S(1)}, u32[]{:S(2)}, u32[]{:S(2)}) %collective-permute-start.41) | collective-permute-done | bytes 614432 | tf_op jit(solution)/shard_map/ppermute | solution.py:35
  353.7 10.8 %weight_grad.9 = (bf16[2,4,240,640]{3,2,1,0:T(8,128)(2,1)}, bf16[2,4,240,640]{3,2,1,0:T(8,128)(2,1)}, f32[8,128]{1,0:T(8,128)}) custom-call(s32[4]{0:T(128)} %pad_add_fusion.2.refs_0_, bf16[960,768]{1,0:T(8,128)(2,1)} %copy-done.77, bf16[2,768,2560]{2,1,0:T(8,128)(2,1)} %get-tuple-element.213.refs_2_, ...), custom_call_target="tpu_custom_call" | custom-call | flops 60720001024 | tf_op jit(solution)/shard_map/weight_grad/pallas_call | solution.py:82
  374.5 20.2 %collective-permute-done.43 = bf16[2,4,240,640]{3,2,1,0:T(8,128)(2,1)S(1)} collective-permute-done((bf16[2,4,240,640]{3,2,1,0:T(8,128)(2,1)}, bf16[2,4,240,640]{3,2,1,0:T(8,128)(2,1)S(1)}, u32[]{:S(2)}, u32[]{:S(2)}) %collective-permute-start.43) | collective-permute-done | bytes 2457632 | tf_op jit(solution)/shard_map/ppermute | solution.py:35
  396.6 4.8 collective-permute-start.51
  401.4 3.6 collective-permute-start.52
  405.7 7.2 %attend_back.15 = (bf16[960,384]{1,0:T(8,128)(2,1)S(1)}, bf16[320,384]{1,0:T(8,128)(2,1)S(1)}, bf16[320,384]{1,0:T(8,128)(2,1)S(1)}) custom-call(s32[2]{0:T(128)S(1)} %copy-done.61, bf16[960,384]{1,0:T(8,128)(2,1)S(1)} %copy-done.64, bf16[960,384]{1,0:T(8,128)(2,1)S(1)} %copy-done.19, bf16[960,384]{1,0:T(8,128)(2,1)S(1)} %copy-done.80, ...), custom_call_target="tpu_custom_call" | custom-call | flops 48299999232 | tf_op jit(solution)/shard_map/attend_back/pallas_call | solution.py:82
  413.5 2.9 collective-permute-done.52
  419.2 5.7 %weight_grad.10 = (bf16[4,4,120,640]{3,2,1,0:T(8,128)(2,1)S(1)}, f32[8,128]{1,0:T(8,128)S(1)}) custom-call(s32[4]{0:T(128)S(1)} %copy-done.31, bf16[2,4,2,128,768]{4,3,2,1,0:T(8,128)(2,1)S(1)} %copy-done, bf16[2,4,2,128,768]{4,3,2,1,0:T(8,128)(2,1)S(1)} %copy-done, bf16[384,2560]{1,0:T(8,128)(2,1)S(1)} %copy-done.4, ...), custom_call_target="tpu_custom_call" | custom-call | flops 55199997952 | tf_op jit(solution)/shard_map/weight_grad/pallas_call | solution.py:82
  427.1 6.4 %weight_grad.11 = (bf16[4,4,120,640]{3,2,1,0:T(8,128)(2,1)S(1)}, f32[8,128]{1,0:T(8,128)}) custom-call(s32[4]{0:T(128)S(1)} %copy-done.30, bf16[2,4,2,128,768]{4,3,2,1,0:T(8,128)(2,1)S(1)} %copy-done, bf16[2,4,2,128,768]{4,3,2,1,0:T(8,128)(2,1)S(1)} %copy-done, bf16[384,2560]{1,0:T(8,128)(2,1)S(1)} %copy-done.4, ...), custom_call_target="tpu_custom_call" | custom-call | flops 276000000 | tf_op jit(solution)/shard_map/weight_grad/pallas_call | solution.py:82
  435.6 3.0 collective-permute-start.58
  440.3 7.3 %collective-permute-done.58 = bf16[240,640]{1,0:T(8,128)(2,1)S(1)} collective-permute-done((bf16[240,640]{1,0:T(8,128)(2,1)S(1)}, bf16[240,640]{1,0:T(8,128)(2,1)S(1)}, u32[]{:S(2)}, u32[]{:S(2)}) %collective-permute-start.58) | collective-permute-done | bytes 307232 | tf_op jit(solution)/shard_map/ppermute | solution.py:57
  447.6 5.3 collective-permute-done.59
  456.5 2.4 copy.37
  460.2 4.4 collective-permute-done.61
  466.5 9.0 %collective-permute-done.62 = bf16[240,640]{1,0:T(8,128)(2,1)S(1)} collective-permute-done((bf16[240,640]{1,0:T(8,128)(2,1)}, bf16[240,640]{1,0:T(8,128)(2,1)S(1)}, u32[]{:S(2)}, u32[]{:S(2)}) %collective-permute-start.62) | collective-permute-done | bytes 307232 | tf_op jit(solution)/shard_map/ppermute | solution.py:57
  476.3 3.7 multiply_reduce_fusion.2
  487.5 7.8 %collective-permute-done.64 = bf16[120,640]{1,0:T(8,128)(2,1)S(1)} collective-permute-done((bf16[120,640]{1,0:T(8,128)(2,1)S(1)}, bf16[120,640]{1,0:T(8,128)(2,1)S(1)}, u32[]{:S(2)}, u32[]{:S(2)}) %collective-permute-start.64) | collective-permute-done | bytes 153632 | tf_op jit(solution)/shard_map/ppermute | solution.py:57
  498.6 2.3 copy.38
  503.9 2.4 spread.5
  508.6 2.6 spread.3
  515.8 2.3 spread.4
  (531 shorter events, 165.3 us)
Async XLA Ops:
  7.2 63.4 %all-gather.3.cloned.1.call-start = ((), (), s32[]{:S(2)}) async-start(), calls=%async_computation | async-start | bytes 2560000 | tf_op jit(solution)/shard_map/all_gather | solution.py:914
  15.7 20.7 %collective-permute-start.2 = (bf16[144,640]{1,0:T(8,128)(2,1)S(1)}, bf16[144,640]{1,0:T(8,128)(2,1)S(1)}, u32[]{:S(2)}, u32[]{:S(2)}) collective-permute-start(bf16[144,640]{1,0:T(8,128)(2,1)S(1)} %fusion.31), channel_id=1, source_target_pairs={{0,1},{1,2},{2,3},{3,0},{4,5},{5,6},{6,7},{7,4},{8,9},{9,10},{10,1... | collective-permute-start | bytes 552968 | tf_op jit(solution)/shard_map/ppermute | solution.py:57
  18.8 16.7 %collective-permute-start.1 = (bf16[144,640]{1,0:T(8,128)(2,1)S(1)}, bf16[144,640]{1,0:T(8,128)(2,1)}, u32[]{:S(2)}, u32[]{:S(2)}) collective-permute-start(bf16[144,640]{1,0:T(8,128)(2,1)S(1)} %fusion.31), channel_id=1, source_target_pairs={{0,2},{1,3},{2,0},{3,1},{4,6},{5,7},{6,4},{7,5},{8,10},{9,11},{10,... | collective-permute-start | bytes 552968 | tf_op jit(solution)/shard_map/ppermute | solution.py:57
  21.3 13.1 %collective-permute-start = (bf16[144,640]{1,0:T(8,128)(2,1)S(1)}, bf16[144,640]{1,0:T(8,128)(2,1)}, u32[]{:S(2)}, u32[]{:S(2)}) collective-permute-start(bf16[144,640]{1,0:T(8,128)(2,1)S(1)} %fusion.31), channel_id=1, source_target_pairs={{0,3},{1,0},{2,1},{3,2},{4,7},{5,4},{6,5},{7,6},{8,11},{9,8},{10,9... | collective-permute-start | bytes 552968 | tf_op jit(solution)/shard_map/ppermute | solution.py:57
  37.1 14.2 %collective-permute-start.3 = (bf16[3,128,640]{2,1,0:T(8,128)(2,1)S(1)}, bf16[3,128,640]{2,1,0:T(8,128)(2,1)}, u32[]{:S(2)}, u32[]{:S(2)}) collective-permute-start(bf16[3,128,640]{2,1,0:T(8,128)(2,1)S(1)} %pad_maximum_fusion.3.refs_1_), channel_id=1, source_target_pairs={{0,8},{4,20},{8,0},{12,28},{16,24},{20,4},{24,16},{28,12},{1,9},{5... | collective-permute-start | bytes 1474568 | tf_op jit(solution)/shard_map/ppermute | solution.py:35
  38.7 19.5 %collective-permute-start.4 = (bf16[3,128,640]{2,1,0:T(8,128)(2,1)S(1)}, bf16[3,128,640]{2,1,0:T(8,128)(2,1)}, u32[]{:S(2)}, u32[]{:S(2)}) collective-permute-start(bf16[3,128,640]{2,1,0:T(8,128)(2,1)S(1)} %pad_maximum_fusion.3.refs_1_), channel_id=1, source_target_pairs={{0,16},{4,12},{8,24},{12,4},{16,0},{20,28},{24,8},{28,20},{1,17},{... | collective-permute-start | bytes 1474568 | tf_op jit(solution)/shard_map/ppermute | solution.py:35
  40.2 32.9 %collective-permute-start.6 = (bf16[3,128,640]{2,1,0:T(8,128)(2,1)S(1)}, bf16[3,128,640]{2,1,0:T(8,128)(2,1)}, u32[]{:S(2)}, u32[]{:S(2)}) collective-permute-start(bf16[3,128,640]{2,1,0:T(8,128)(2,1)S(1)} %pad_maximum_fusion.3.refs_1_), channel_id=1, source_target_pairs={{0,4},{4,0},{8,12},{12,8},{16,20},{20,16},{24,28},{28,24},{1,5},{5... | collective-permute-start | bytes 1474568 | tf_op jit(solution)/shard_map/ppermute | solution.py:35
  58.2 14.9 %collective-permute-start.7 = (bf16[3,128,640]{2,1,0:T(8,128)(2,1)}, bf16[3,128,640]{2,1,0:T(8,128)(2,1)}, u32[]{:S(2)}, u32[]{:S(2)}) collective-permute-start(bf16[3,128,640]{2,1,0:T(8,128)(2,1)} %collective-permute-done.3.refs_2_), channel_id=1, source_target_pairs={{0,4},{4,0},{8,12},{12,8},{16,20},{20,16},{24,28},{28,24},{1,5},{5... | collective-permute-start | bytes 1474568 | tf_op jit(solution)/shard_map/ppermute | solution.py:35
  58.2 14.9 %collective-permute-start.8 = (bf16[3,128,640]{2,1,0:T(8,128)(2,1)}, bf16[3,128,640]{2,1,0:T(8,128)(2,1)}, u32[]{:S(2)}, u32[]{:S(2)}) collective-permute-start(bf16[3,128,640]{2,1,0:T(8,128)(2,1)} %collective-permute-done.4.refs_3_), channel_id=1, source_target_pairs={{0,4},{4,0},{8,12},{12,8},{16,20},{20,16},{24,28},{28,24},{1,5},{5... | collective-permute-start | bytes 1474568 | tf_op jit(solution)/shard_map/ppermute | solution.py:35
  60.5 12.6 %collective-permute-start.9 = (bf16[3,128,640]{2,1,0:T(8,128)(2,1)}, bf16[3,128,640]{2,1,0:T(8,128)(2,1)}, u32[]{:S(2)}, u32[]{:S(2)}) collective-permute-start(bf16[3,128,640]{2,1,0:T(8,128)(2,1)} %collective-permute-done.5.refs_4_), channel_id=1, source_target_pairs={{0,4},{4,0},{8,12},{12,8},{16,20},{20,16},{24,28},{28,24},{1,5},{5... | collective-permute-start | bytes 1474568 | tf_op jit(solution)/shard_map/ppermute | solution.py:35
  77.7 18.0 %collective-permute-start.10 = (bf16[640,384]{1,0:T(8,128)(2,1)S(1)}, bf16[640,384]{1,0:T(8,128)(2,1)S(1)}, u32[]{:S(2)}, u32[]{:S(2)}) collective-permute-start(bf16[640,384]{1,0:T(8,128)(2,1)S(1)} %keys_values.2.refs_4_.refs_2_.refs_5_.refs_6_), channel_id=1, source_target_pairs={{0,1},{1,2},{2,3},{4,5},{5,6},{6,7},{8,9},{9,10},{10,11},{12,13},{... | collective-permute-start | bytes 1474568 | tf_op jit(solution)/shard_map/ppermute | solution.py:40
  84.6 33.8 %collective-permute-start.13 = (bf16[3,240,640]{2,1,0:T(8,128)(2,1)S(1)}, bf16[3,240,640]{2,1,0:T(8,128)(2,1)S(1)}, u32[]{:S(2)}, u32[]{:S(2)}) collective-permute-start(bf16[3,240,640]{2,1,0:T(8,128)(2,1)S(1)} %pad_maximum_fusion.2.refs_10_.refs_1_), channel_id=1, source_target_pairs={{0,8},{4,20},{8,0},{12,28},{16,24},{20,4},{24,16},{28,12},{1,9},{5... | collective-permute-start | bytes 2764808 | tf_op jit(solution)/shard_map/ppermute | solution.py:35
  85.0 33.4 %collective-permute-start.14 = (bf16[3,240,640]{2,1,0:T(8,128)(2,1)S(1)}, bf16[3,240,640]{2,1,0:T(8,128)(2,1)S(1)}, u32[]{:S(2)}, u32[]{:S(2)}) collective-permute-start(bf16[3,240,640]{2,1,0:T(8,128)(2,1)S(1)} %pad_maximum_fusion.2.refs_10_.refs_1_), channel_id=1, source_target_pairs={{0,16},{4,12},{8,24},{12,4},{16,0},{20,28},{24,8},{28,20},{1,17},{... | collective-permute-start | bytes 2764808 | tf_op jit(solution)/shard_map/ppermute | solution.py:35
  85.6 32.2 %collective-permute-start.15 = (bf16[3,80,960]{2,1,0:T(8,128)(2,1)S(1)}, bf16[3,80,960]{2,1,0:T(8,128)(2,1)S(1)}, u32[]{:S(2)}, u32[]{:S(2)}) collective-permute-start(bf16[3,80,960]{2,1,0:T(8,128)(2,1)S(1)} %pad_maximum_fusion.4.refs_11_.refs_1_), channel_id=1, source_target_pairs={{0,8},{4,20},{8,0},{12,28},{16,24},{20,4},{24,16},{28,12},{1,9},{5... | collective-permute-start | bytes 1382408 | tf_op jit(solution)/shard_map/ppermute | solution.py:35
  87.4 30.5 %collective-permute-start.16 = (bf16[3,80,960]{2,1,0:T(8,128)(2,1)S(1)}, bf16[3,80,960]{2,1,0:T(8,128)(2,1)S(1)}, u32[]{:S(2)}, u32[]{:S(2)}) collective-permute-start(bf16[3,80,960]{2,1,0:T(8,128)(2,1)S(1)} %pad_maximum_fusion.4.refs_11_.refs_1_), channel_id=1, source_target_pairs={{0,16},{4,12},{8,24},{12,4},{16,0},{20,28},{24,8},{28,20},{1,17},{... | collective-permute-start | bytes 1382408 | tf_op jit(solution)/shard_map/ppermute | solution.py:35
  95.7 24.7 %collective-permute-start.11 = (bf16[640,384]{1,0:T(8,128)(2,1)S(1)}, bf16[640,384]{1,0:T(8,128)(2,1)S(1)}, u32[]{:S(2)}, u32[]{:S(2)}) collective-permute-start(bf16[640,384]{1,0:T(8,128)(2,1)S(1)} %collective-permute-done.10.refs_2_.refs_5_.refs_6_), channel_id=1, source_target_pairs={{1,2},{2,3},{5,6},{6,7},{9,10},{10,11},{13,14},{14,15},{17,18},{18... | collective-permute-start | bytes 1474568 | tf_op jit(solution)/shard_map/ppermute | solution.py:40
  117.8 25.9 %collective-permute-start.19 = (bf16[3,240,640]{2,1,0:T(8,128)(2,1)S(1)}, bf16[3,240,640]{2,1,0:T(8,128)(2,1)S(1)}, u32[]{:S(2)}, u32[]{:S(2)}) collective-permute-start(bf16[3,240,640]{2,1,0:T(8,128)(2,1)S(1)} %pad_maximum_fusion.2.refs_10_.refs_1_), channel_id=1, source_target_pairs={{0,4},{4,0},{8,12},{12,8},{16,20},{20,16},{24,28},{28,24},{1,5},{5... | collective-permute-start | bytes 2764808 | tf_op jit(solution)/shard_map/ppermute | solution.py:35
  117.9 21.3 %collective-permute-start.23 = (bf16[3,80,960]{2,1,0:T(8,128)(2,1)S(1)}, bf16[3,80,960]{2,1,0:T(8,128)(2,1)S(1)}, u32[]{:S(2)}, u32[]{:S(2)}) collective-permute-start(bf16[3,80,960]{2,1,0:T(8,128)(2,1)S(1)} %pad_maximum_fusion.4.refs_11_.refs_1_), channel_id=1, source_target_pairs={{0,4},{4,0},{8,12},{12,8},{16,20},{20,16},{24,28},{28,24},{1,5},{5... | collective-permute-start | bytes 1382408 | tf_op jit(solution)/shard_map/ppermute | solution.py:35
  118.4 18.7 %collective-permute-start.17 = (bf16[3,240,640]{2,1,0:T(8,128)(2,1)S(1)}, bf16[3,240,640]{2,1,0:T(8,128)(2,1)S(1)}, u32[]{:S(2)}, u32[]{:S(2)}) collective-permute-start(bf16[3,240,640]{2,1,0:T(8,128)(2,1)S(1)} %collective-permute-done.13.refs_2_), channel_id=1, source_target_pairs={{0,16},{4,12},{8,24},{12,4},{16,0},{20,28},{24,8},{28,20},{1,17},{... | collective-permute-start | bytes 2764808 | tf_op jit(solution)/shard_map/ppermute | solution.py:35
  119.4 17.7 %collective-permute-start.18 = (bf16[3,80,960]{2,1,0:T(8,128)(2,1)S(1)}, bf16[3,80,960]{2,1,0:T(8,128)(2,1)S(1)}, u32[]{:S(2)}, u32[]{:S(2)}) collective-permute-start(bf16[3,80,960]{2,1,0:T(8,128)(2,1)S(1)} %collective-permute-done.15.refs_2_), channel_id=1, source_target_pairs={{0,16},{4,12},{8,24},{12,4},{16,0},{20,28},{24,8},{28,20},{1,17},{... | collective-permute-start | bytes 1382408 | tf_op jit(solution)/shard_map/ppermute | solution.py:35
  120.4 17.2 %collective-permute-start.12 = (bf16[640,384]{1,0:T(8,128)(2,1)S(1)}, bf16[640,384]{1,0:T(8,128)(2,1)S(1)}, u32[]{:S(2)}, u32[]{:S(2)}) collective-permute-start(bf16[640,384]{1,0:T(8,128)(2,1)S(1)} %collective-permute-done.11.refs_2_.refs_5_.refs_6_), channel_id=1, source_target_pairs={{2,3},{6,7},{10,11},{14,15},{18,19},{22,23},{26,27},{30,31}} | collective-permute-start | bytes 1474568 | tf_op jit(solution)/shard_map/ppermute | solution.py:40
  171.1 12.4 %collective-permute-start.27 = (bf16[320,384]{1,0:T(8,128)(2,1)S(1)}, bf16[320,384]{1,0:T(8,128)(2,1)S(1)}, u32[]{:S(2)}, u32[]{:S(2)}) collective-permute-start(bf16[320,384]{1,0:T(8,128)(2,1)S(1)} %get-tuple-element.168.refs_4_.refs_2_.refs_5_), channel_id=1, source_target_pairs={{0,1},{1,2},{2,3},{4,5},{5,6},{6,7},{8,9},{9,10},{10,11},{12,13},{... | collective-permute-start | bytes 737288 | tf_op jit(solution)/shard_map/ppermute | solution.py:40
  173.3 10.9 %collective-permute-start.30 = (bf16[320,384]{1,0:T(8,128)(2,1)S(1)}, bf16[320,384]{1,0:T(8,128)(2,1)S(1)}, u32[]{:S(2)}, u32[]{:S(2)}) collective-permute-start(bf16[320,384]{1,0:T(8,128)(2,1)S(1)} %get-tuple-element.169.refs_3_.refs_6_), channel_id=1, source_target_pairs={{0,1},{1,2},{2,3},{4,5},{5,6},{6,7},{8,9},{9,10},{10,11},{12,13},{... | collective-permute-start | bytes 737288 | tf_op jit(solution)/shard_map/ppermute | solution.py:40
  236.9 45.0 %collective-permute-start.35 = (bf16[320,384]{1,0:T(8,128)(2,1)S(1)}, bf16[320,384]{1,0:T(8,128)(2,1)S(1)}, u32[]{:S(2)}, u32[]{:S(2)}) collective-permute-start(bf16[320,384]{1,0:T(8,128)(2,1)S(1)} %add_convert_fusion.15), channel_id=1, source_target_pairs={{1,0},{2,1},{3,2},{5,4},{6,5},{7,6},{9,8},{10,9},{11,10},{13,12},{... | collective-permute-start | bytes 737288 | tf_op jit(solution)/shard_map/ppermute | solution.py:849
  238.4 46.4 %collective-permute-start.38 = (bf16[320,384]{1,0:T(8,128)(2,1)S(1)}, bf16[320,384]{1,0:T(8,128)(2,1)S(1)}, u32[]{:S(2)}, u32[]{:S(2)}) collective-permute-start(bf16[320,384]{1,0:T(8,128)(2,1)S(1)} %add_convert_fusion.13), channel_id=1, source_target_pairs={{1,0},{2,1},{3,2},{5,4},{6,5},{7,6},{9,8},{10,9},{11,10},{13,12},{... | collective-permute-start | bytes 737288 | tf_op jit(solution)/shard_map/ppermute | solution.py:849
  309.5 29.8 %collective-permute-start.40 = (bf16[2,4,80,960]{3,2,1,0:T(8,128)(2,1)}, bf16[2,4,80,960]{3,2,1,0:T(8,128)(2,1)}, u32[]{:S(2)}, u32[]{:S(2)}) collective-permute-start(bf16[2,4,80,960]{3,2,1,0:T(8,128)(2,1)} %get-tuple-element.202), channel_id=1, source_target_pairs={{0,8},{4,20},{8,0},{12,28},{16,24},{20,4},{24,16},{28,12},{1,9},{5... | collective-permute-start | bytes 3686408 | tf_op jit(solution)/shard_map/ppermute | solution.py:35
  339.2 14.5 %collective-permute-start.42 = (bf16[4,4,240,640]{3,2,1,0:T(8,128)(2,1)}, bf16[4,4,240,640]{3,2,1,0:T(8,128)(2,1)}, u32[]{:S(2)}, u32[]{:S(2)}) collective-permute-start(bf16[4,4,240,640]{3,2,1,0:T(8,128)(2,1)} %get-tuple-element.219), channel_id=1, source_target_pairs={{0,4},{4,0},{8,12},{12,8},{16,20},{20,16},{24,28},{28,24},{1,5},{5... | collective-permute-start | bytes 14745608 | tf_op jit(solution)/shard_map/ppermute | solution.py:35
  340.8 10.7 %collective-permute-start.41 = (bf16[4,80,960]{2,1,0:T(8,128)(2,1)S(1)}, bf16[4,80,960]{2,1,0:T(8,128)(2,1)S(1)}, u32[]{:S(2)}, u32[]{:S(2)}) collective-permute-start(bf16[4,80,960]{2,1,0:T(8,128)(2,1)S(1)} %fusion.25), channel_id=1, source_target_pairs={{0,16},{4,12},{8,24},{12,4},{16,0},{20,28},{24,8},{28,20},{1,17},{... | collective-permute-start | bytes 1843208 | tf_op jit(solution)/shard_map/ppermute | solution.py:35
  343.2 25.2 %collective-permute-start.44 = (bf16[320,384]{1,0:T(8,128)(2,1)S(1)}, bf16[320,384]{1,0:T(8,128)(2,1)}, u32[]{:S(2)}, u32[]{:S(2)}) collective-permute-start(bf16[320,384]{1,0:T(8,128)(2,1)S(1)} %get-tuple-element.233), channel_id=1, source_target_pairs={{3,2},{7,6},{11,10},{15,14},{19,18},{23,22},{27,26},{31,30}} | collective-permute-start | bytes 737288 | tf_op jit(solution)/shard_map/ppermute | solution.py:849
  344.6 25.5 %collective-permute-start.47 = (bf16[320,384]{1,0:T(8,128)(2,1)S(1)}, bf16[320,384]{1,0:T(8,128)(2,1)S(1)}, u32[]{:S(2)}, u32[]{:S(2)}) collective-permute-start(bf16[320,384]{1,0:T(8,128)(2,1)S(1)} %get-tuple-element.236), channel_id=1, source_target_pairs={{3,2},{7,6},{11,10},{15,14},{19,18},{23,22},{27,26},{31,30}} | collective-permute-start | bytes 737288 | tf_op jit(solution)/shard_map/ppermute | solution.py:849
  364.5 30.1 %collective-permute-start.43 = (bf16[2,4,240,640]{3,2,1,0:T(8,128)(2,1)}, bf16[2,4,240,640]{3,2,1,0:T(8,128)(2,1)S(1)}, u32[]{:S(2)}, u32[]{:S(2)}) collective-permute-start(bf16[2,4,240,640]{3,2,1,0:T(8,128)(2,1)} %get-tuple-element.223), channel_id=1, source_target_pairs={{0,8},{4,20},{8,0},{12,28},{16,24},{20,4},{24,16},{28,12},{1,9},{5... | collective-permute-start | bytes 7372808 | tf_op jit(solution)/shard_map/ppermute | solution.py:35
  371.8 33.2 %collective-permute-start.46 = (bf16[320,384]{1,0:T(8,128)(2,1)S(1)}, bf16[320,384]{1,0:T(8,128)(2,1)S(1)}, u32[]{:S(2)}, u32[]{:S(2)}) collective-permute-start(bf16[320,384]{1,0:T(8,128)(2,1)S(1)} %add_convert_fusion.11), channel_id=1, source_target_pairs={{1,0},{2,1},{3,2},{5,4},{6,5},{7,6},{9,8},{10,9},{11,10},{13,12},{... | collective-permute-start | bytes 737288 | tf_op jit(solution)/shard_map/ppermute | solution.py:849
  373.2 39.6 %collective-permute-start.49 = (bf16[320,384]{1,0:T(8,128)(2,1)S(1)}, bf16[320,384]{1,0:T(8,128)(2,1)S(1)}, u32[]{:S(2)}, u32[]{:S(2)}) collective-permute-start(bf16[320,384]{1,0:T(8,128)(2,1)S(1)} %add_convert_fusion.9), channel_id=1, source_target_pairs={{1,0},{2,1},{3,2},{5,4},{6,5},{7,6},{9,8},{10,9},{11,10},{13,12},{... | collective-permute-start | bytes 737288 | tf_op jit(solution)/shard_map/ppermute | solution.py:849
  395.0 21.4 %collective-permute-start.50 = (bf16[4,240,640]{2,1,0:T(8,128)(2,1)S(1)}, bf16[4,240,640]{2,1,0:T(8,128)(2,1)S(1)}, u32[]{:S(2)}, u32[]{:S(2)}) collective-permute-start(bf16[4,240,640]{2,1,0:T(8,128)(2,1)S(1)} %fusion.20), channel_id=1, source_target_pairs={{0,16},{4,12},{8,24},{12,4},{16,0},{20,28},{24,8},{28,20},{1,17},{... | collective-permute-start | bytes 3686408 | tf_op jit(solution)/shard_map/ppermute | solution.py:35
  396.6 16.9 %collective-permute-start.51 = (bf16[80,960]{1,0:T(8,128)(2,1)S(1)}, bf16[80,960]{1,0:T(8,128)(2,1)S(1)}, u32[]{:S(2)}, u32[]{:S(2)}) collective-permute-start(bf16[80,960]{1,0:T(8,128)(2,1)S(1)} %copy-done.116), channel_id=1, source_target_pairs={{0,1},{1,2},{2,3},{3,0},{4,5},{5,6},{6,7},{7,4},{8,9},{9,10},{10,1... | collective-permute-start | bytes 460808 | tf_op jit(solution)/shard_map/ppermute | solution.py:57
  401.4 15.0 %collective-permute-start.52 = (bf16[80,960]{1,0:T(8,128)(2,1)S(1)}, bf16[80,960]{1,0:T(8,128)(2,1)S(1)}, u32[]{:S(2)}, u32[]{:S(2)}) collective-permute-start(bf16[80,960]{1,0:T(8,128)(2,1)S(1)} %copy-done.115), channel_id=1, source_target_pairs={{0,2},{1,3},{2,0},{3,1},{4,6},{5,7},{6,4},{7,5},{8,10},{9,11},{10,... | collective-permute-start | bytes 460808 | tf_op jit(solution)/shard_map/ppermute | solution.py:57
  405.0 11.4 %collective-permute-start.53 = (bf16[80,960]{1,0:T(8,128)(2,1)S(1)}, bf16[80,960]{1,0:T(8,128)(2,1)S(1)}, u32[]{:S(2)}, u32[]{:S(2)}) collective-permute-start(bf16[80,960]{1,0:T(8,128)(2,1)S(1)} %copy-done.114), channel_id=1, source_target_pairs={{0,3},{1,0},{2,1},{3,2},{4,7},{5,4},{6,5},{7,6},{8,11},{9,8},{10,9... | collective-permute-start | bytes 460808 | tf_op jit(solution)/shard_map/ppermute | solution.py:57
  434.2 18.7 %collective-permute-start.57 = (bf16[2,4,120,640]{3,2,1,0:T(8,128)(2,1)S(1)}, bf16[2,4,120,640]{3,2,1,0:T(8,128)(2,1)S(1)}, u32[]{:S(2)}, u32[]{:S(2)}) collective-permute-start(bf16[2,4,120,640]{3,2,1,0:T(8,128)(2,1)S(1)} %add_convert_fusion), channel_id=1, source_target_pairs={{0,8},{4,20},{8,0},{12,28},{16,24},{20,4},{24,16},{28,12},{1,9},{5... | collective-permute-start | bytes 3686408 | tf_op jit(solution)/shard_map/ppermute | solution.py:35
  435.6 12.0 %collective-permute-start.58 = (bf16[240,640]{1,0:T(8,128)(2,1)S(1)}, bf16[240,640]{1,0:T(8,128)(2,1)S(1)}, u32[]{:S(2)}, u32[]{:S(2)}) collective-permute-start(bf16[240,640]{1,0:T(8,128)(2,1)S(1)} %get-tuple-element.305), channel_id=1, source_target_pairs={{0,1},{1,2},{2,3},{3,0},{4,5},{5,6},{6,7},{7,4},{8,9},{9,10},{10,1... | collective-permute-start | bytes 921608 | tf_op jit(solution)/shard_map/ppermute | solution.py:57
  438.5 14.3 %collective-permute-start.59 = (bf16[240,640]{1,0:T(8,128)(2,1)S(1)}, bf16[240,640]{1,0:T(8,128)(2,1)S(1)}, u32[]{:S(2)}, u32[]{:S(2)}) collective-permute-start(bf16[240,640]{1,0:T(8,128)(2,1)S(1)} %get-tuple-element.304), channel_id=1, source_target_pairs={{0,3},{1,0},{2,1},{3,2},{4,7},{5,4},{6,5},{7,6},{8,11},{9,8},{10,9... | collective-permute-start | bytes 921608 | tf_op jit(solution)/shard_map/ppermute | solution.py:57
  439.4 13.5 %collective-permute-start.60 = (bf16[80,960]{1,0:T(8,128)(2,1)S(1)}, bf16[80,960]{1,0:T(8,128)(2,1)S(1)}, u32[]{:S(2)}, u32[]{:S(2)}) collective-permute-start(bf16[80,960]{1,0:T(8,128)(2,1)S(1)} %collective-permute-done.55.refs_3_), channel_id=1, source_target_pairs={{0,8},{4,20},{8,0},{12,28},{16,24},{20,4},{24,16},{28,12},{1,9},{5... | collective-permute-start | bytes 460808 | tf_op jit(solution)/shard_map/ppermute | solution.py:35
  454.2 10.5 %collective-permute-start.61 = (bf16[4,120,640]{2,1,0:T(8,128)(2,1)}, bf16[4,120,640]{2,1,0:T(8,128)(2,1)}, u32[]{:S(2)}, u32[]{:S(2)}) collective-permute-start(bf16[4,120,640]{2,1,0:T(8,128)(2,1)} %fusion.28), channel_id=1, source_target_pairs={{0,16},{4,12},{8,24},{12,4},{16,0},{20,28},{24,8},{28,20},{1,17},{... | collective-permute-start | bytes 1843208 | tf_op jit(solution)/shard_map/ppermute | solution.py:35
  458.9 16.6 %collective-permute-start.62 = (bf16[240,640]{1,0:T(8,128)(2,1)}, bf16[240,640]{1,0:T(8,128)(2,1)S(1)}, u32[]{:S(2)}, u32[]{:S(2)}) collective-permute-start(bf16[240,640]{1,0:T(8,128)(2,1)} %get-tuple-element.303), channel_id=1, source_target_pairs={{0,2},{1,3},{2,0},{3,1},{4,6},{5,7},{6,4},{7,5},{8,10},{9,11},{10,... | collective-permute-start | bytes 921608 | tf_op jit(solution)/shard_map/ppermute | solution.py:57
  480.0 15.9 %collective-permute-start.66 = (bf16[240,640]{1,0:T(8,128)(2,1)S(1)}, bf16[240,640]{1,0:T(8,128)(2,1)S(1)}, u32[]{:S(2)}, u32[]{:S(2)}) collective-permute-start(bf16[240,640]{1,0:T(8,128)(2,1)S(1)} %add_convert_fusion.8.refs_1_), channel_id=1, source_target_pairs={{0,8},{4,20},{8,0},{12,28},{16,24},{20,4},{24,16},{28,12},{1,9},{5... | collective-permute-start | bytes 921608 | tf_op jit(solution)/shard_map/ppermute | solution.py:35
  482.8 12.5 %collective-permute-start.64 = (bf16[120,640]{1,0:T(8,128)(2,1)S(1)}, bf16[120,640]{1,0:T(8,128)(2,1)S(1)}, u32[]{:S(2)}, u32[]{:S(2)}) collective-permute-start(bf16[120,640]{1,0:T(8,128)(2,1)S(1)} %get-tuple-element.257), channel_id=1, source_target_pairs={{0,2},{1,3},{2,0},{3,1},{4,6},{5,7},{6,4},{7,5},{8,10},{9,11},{10,... | collective-permute-start | bytes 460808 | tf_op jit(solution)/shard_map/ppermute | solution.py:57
  482.8 12.5 %collective-permute-start.63 = (bf16[120,640]{1,0:T(8,128)(2,1)S(1)}, bf16[120,640]{1,0:T(8,128)(2,1)S(1)}, u32[]{:S(2)}, u32[]{:S(2)}) collective-permute-start(bf16[120,640]{1,0:T(8,128)(2,1)S(1)} %get-tuple-element.256), channel_id=1, source_target_pairs={{0,1},{1,2},{2,3},{3,0},{4,5},{5,6},{6,7},{7,4},{8,9},{9,10},{10,1... | collective-permute-start | bytes 460808 | tf_op jit(solution)/shard_map/ppermute | solution.py:57
  483.6 12.5 %collective-permute-start.68 = (bf16[240,640]{1,0:T(8,128)(2,1)S(1)}, bf16[240,640]{1,0:T(8,128)(2,1)S(1)}, u32[]{:S(2)}, u32[]{:S(2)}) collective-permute-start(bf16[240,640]{1,0:T(8,128)(2,1)S(1)} %collective-permute-done.67.refs_3_), channel_id=1, source_target_pairs={{0,8},{4,20},{8,0},{12,28},{16,24},{20,4},{24,16},{28,12},{1,9},{5... | collective-permute-start | bytes 921608 | tf_op jit(solution)/shard_map/ppermute | solution.py:35
  487.5 15.4 %collective-permute-start.80 = (bf16[80,960]{1,0:T(8,128)(2,1)S(1)}, bf16[80,960]{1,0:T(8,128)(2,1)S(1)}, u32[]{:S(2)}, u32[]{:S(2)}) collective-permute-start(bf16[80,960]{1,0:T(8,128)(2,1)S(1)} %copy-done.29), channel_id=1, source_target_pairs={{0,4},{4,0},{8,12},{12,8},{16,20},{20,16},{24,28},{28,24},{1,5},{5... | collective-permute-start | bytes 460808 | tf_op jit(solution)/shard_map/ppermute | solution.py:35
  (169 other events, 1474.0 us)
Sparse Core Ops, SparseCore 0:
  23.9 46.6 all-gather.2

commit v3 on v2

--- a/solution.py
+++ b/solution.py
@@ -241,13 +241,13 @@
     return sum(v.astype(f32) for v in terms).astype(bf16)
 
 
-def cost(us, weight=6):
+def cost(us, weight=8):
     return pl.CostEstimate(
         flops=int(us * weight * 1.15e9), bytes_accessed=0, transcendentals=0
     )
 
 
-HEAVY = 6
+HEAVY = 8
 
 
 class Reduction:

time: 539 us -> 540 us (level)
    unnamed x272 -> x274, local copies, waits for them, and re-layouts: 39.3 us -> 37.3 us
  transfers between devices with their start and end apart: 85 -> 85, of which waited for: 23 -> 25; matrix products, arithmetic and copies ran while one was open for 10% -> 10% of each run, Pallas kernels for 15% -> 15%
where the time goes in v3:
time: 540 us; the launch traced here: 530 us
  waiting for transfers between devices  165 us (31%)
  Pallas kernels  161 us (30%)
  starting transfers between devices  88 us (16%)
  local copies, waits for them, and re-layouts  55.9 us (10%)
  other arithmetic  37.1 us (7%)
  between operations  17.1 us (3%)
  matrix products  5.47 us (1%)
    pallas_call x36, Pallas kernels, call(): return pl.pallas_call(waiting, **where, **rest)(*operands, *wait_for)  133 us
    ppermute x51, waiting for transfers between devices, swap(): return lax.ppermute(value, 'dp', [(i, hop(i)) for i in range(count)])  82 us
    unnamed x274, local copies, waits for them, and re-layouts  37.3 us
    ppermute x12, waiting for transfers between devices, attention_gradient(): got = [lax.ppermute(v, 'fsdp', pairs) for v in moving]  37 us
    ppermute x12, waiting for transfers between devices, around(): lax.ppermute(value, 'fsdp', [(i, (i + distance) % count) for i in range(c...  34.3 us
    ppermute x51, starting transfers between devices, swap(): return lax.ppermute(value, 'dp', [(i, hop(i)) for i in range(count)])  33.9 us
    pallas_call x2, Pallas kernels, feed_forward(): pl.pallas_call(feed_forward_kernel, grid=(5,), in_specs=[whole(rows, mode...  27.8 us
    ppermute x12, starting transfers between devices, around(): lax.ppermute(value, 'fsdp', [(i, (i + distance) % count) for i in range(c...  26.4 us
  transfers between devices with their start and end apart: 85, of which 25 were waited for; matrix products, arithmetic and copies ran while one was open for 10% of the time, Pallas kernels for 15%

profile of v3, /device:TPU:0, one launch (start us, length us, event | category | flops | bytes accessed | tf_op | source)
XLA Modules:
  0.0 529.6 jit_solution(6343578420267095522)
XLA Ops:
  10.8 2.4 concatenate.29.refs_9_
  15.7 3.1 collective-permute-start.2
  18.8 2.6 collective-permute-start.1
  28.5 2.3 copy.33
  31.7 2.8 fusion.35
  42.3 8.8 %collective-permute-done.3.refs_2_ = bf16[3,128,640]{2,1,0:T(8,128)(2,1)} collective-permute-done((bf16[3,128,640]{2,1,0:T(8,128)(2,1)S(1)}, bf16[3,128,640]{2,1,0:T(8,128)(2,1)}, u32[]{:S(2)}, u32[]{:S(2)}) %collective-permute-start.3) | collective-permute-done | bytes 491552 | tf_op jit(solution)/shard_map/ppermute | solution.py:35
  53.4 2.3 copy.32
  60.3 10.3 %all-gather.3.cloned.1.call-done = bf16[1600,640]{1,0:T(8,128)(2,1)} async-done(((bf16[400,640]{1,0:T(8,128)(2,1)}), bf16[1600,640]{1,0:T(8,128)(2,1)}) %all-gather.3.cloned.1.call-update) | async-done | bytes 2048016 | tf_op jit(solution)/shard_map/all_gather | solution.py:914
  73.2 2.4 lay_out.3.refs_1_
  77.7 6.7 %collective-permute-start.10 = (bf16[640,384]{1,0:T(8,128)(2,1)S(1)}, bf16[640,384]{1,0:T(8,128)(2,1)S(1)}, u32[]{:S(2)}, u32[]{:S(2)}) collective-permute-start(bf16[640,384]{1,0:T(8,128)(2,1)S(1)} %keys_values.2.refs_4_.refs_2_.refs_5_.refs_6_), channel_id=1, source_target_pairs={{0,1},{1,2},{2,3},{4,5},{5,6},{6,7},{8,9},{9,10},{10,11},{12,13},{... | collective-permute-start | bytes 1474568 | tf_op jit(solution)/shard_map/ppermute | solution.py:40
  88.5 3.4 attend.8
  96.9 20.8 %collective-permute-done.15.refs_2_ = bf16[3,80,960]{2,1,0:T(8,128)(2,1)S(1)} collective-permute-done((bf16[3,80,960]{2,1,0:T(8,128)(2,1)S(1)}, bf16[3,80,960]{2,1,0:T(8,128)(2,1)S(1)}, u32[]{:S(2)}, u32[]{:S(2)}) %collective-permute-start.15) | collective-permute-done | bytes 460832 | tf_op jit(solution)/shard_map/ppermute | solution.py:35
  121.6 15.3 %collective-permute-done.18.refs_4_ = bf16[3,80,960]{2,1,0:T(8,128)(2,1)S(1)} collective-permute-done((bf16[3,80,960]{2,1,0:T(8,128)(2,1)S(1)}, bf16[3,80,960]{2,1,0:T(8,128)(2,1)S(1)}, u32[]{:S(2)}, u32[]{:S(2)}) %collective-permute-start.18) | collective-permute-done | bytes 460832 | tf_op jit(solution)/shard_map/ppermute | solution.py:35
  150.3 13.9 %feed_forward.2 = (f32[384,960]{1,0:T(8,128)S(1)}, f32[384,960]{1,0:T(8,128)S(1)}, bf16[384,2560]{1,0:T(8,128)(2,1)}, bf16[384,2560]{1,0:T(8,128)(2,1)}, bf16[96...) custom-call(f32[384,960]{1,0:T(8,128)} %bitcast_convert_fusion.x_ref, ...), custom_call_target="tpu_custom_call" | custom-call | flops 110399995904 | tf_op jit(solution)/shard_map/feed_forward/pallas_call | solution.py:677
  175.6 3.2 attend.12
  189.9 5.1 attend.15
  197.4 13.9 %feed_forward.3 = (f32[384,960]{1,0:T(8,128)S(1)}, f32[384,960]{1,0:T(8,128)S(1)}, bf16[384,2560]{1,0:T(8,128)(2,1)}, bf16[384,2560]{1,0:T(8,128)(2,1)}, bf16[96...) custom-call(f32[384,960]{1,0:T(8,128)} %copy-done.1, ...), custom_call_target="tpu_custom_call", output_to_operand_aliasing={{4}: (7, {}), {5}: (8, {})} | custom-call | flops 110399995904 | tf_op jit(solution)/shard_map/feed_forward/pallas_call | solution.py:677
  213.5 16.5 %feed_forward_back.2 = (bf16[2,768,2560]{2,1,0:T(8,128)(2,1)}, f32[384,960]{1,0:T(8,128)S(1)}, bf16[384,960]{1,0:T(8,128)(2,1)S(1)}, bf16[960,384]{1,0:T(8,128)(2,1)S(1)}) custom-call(f32[384,960]{1,0:T(8,128)S(1)} %copy-done.10, f32[384,960]{1,0:T(8,128)} %copy-done.87, f32[1,960]{1,0:T(1,128)S(1)} %copy-done.35, ...), custom_call_target="tpu_custom_call" | custom-call | flops 165600002048 | tf_op jit(solution)/shard_map/feed_forward_back/pallas_call | solution.py:82
  240.0 7.2 %attend_back.11 = (bf16[960,384]{1,0:T(8,128)(2,1)S(1)}, bf16[320,384]{1,0:T(8,128)(2,1)S(1)}, bf16[320,384]{1,0:T(8,128)(2,1)S(1)}) custom-call(s32[2]{0:T(128)S(1)} %copy-done.68, bf16[960,384]{1,0:T(8,128)(2,1)S(1)} %copy-done.75, bf16[960,384]{1,0:T(8,128)(2,1)S(1)} %copy-done.23, bf16[960,384]{1,0:T(8,128)(2,1)S(1)} %get-tuple-element.185.refs_3_, ...), custom_call_target="tpu_custom_call" | custom-call | flops 64399998976 | tf_op jit(solution)/shard_map/attend_back/pallas_call | solution.py:82
  247.1 32.4 %collective-permute-done.35.refs_2_ = bf16[320,384]{1,0:T(8,128)(2,1)S(1)} collective-permute-done((bf16[320,384]{1,0:T(8,128)(2,1)S(1)}, bf16[320,384]{1,0:T(8,128)(2,1)S(1)}, u32[]{:S(2)}, u32[]{:S(2)}) %collective-permute-start.35) | collective-permute-done | bytes 245792 | tf_op jit(solution)/shard_map/ppermute | solution.py:849
  279.5 4.5 collective-permute-done.38.refs_3_
  289.7 6.5 %weight_grad.6 = (bf16[4,4,80,960]{3,2,1,0:T(8,128)(2,1)}, f32[8,128]{1,0:T(8,128)}) custom-call(s32[4]{0:T(128)} %pad_add_fusion.3.refs_0_, bf16[4,8,80,768]{3,2,1,0:T(8,128)(2,1)} %bitcast.136, bf16[768,960]{1,0:T(8,128)(2,1)} %pad_maximum_fusion.1.refs_2_), custom_call_target="tpu_custom_call" | custom-call | flops 51520000000 | tf_op jit(solution)/shard_map/weight_grad/pallas_call | solution.py:82
  296.8 4.6 collective-permute-done.39.refs_3_
  301.4 7.3 %weight_grad.7 = (bf16[2,4,80,960]{3,2,1,0:T(8,128)(2,1)}, bf16[2,4,80,960]{3,2,1,0:T(8,128)(2,1)}, f32[8,128]{1,0:T(8,128)}) custom-call(s32[4]{0:T(128)} %pad_add_fusion.2.refs_0_, bf16[4,8,80,768]{3,2,1,0:T(8,128)(2,1)} %bitcast.137, bf16[768,960]{1,0:T(8,128)(2,1)} %pad_maximum_fusion.1.refs_2_, bf16[4,4,80,960]{3,2,1,0:T(8,128)(2,1)} %collective-permute-done.39.refs_3_, ...), custom_call_target="tpu_custom_call" | custom-call | flops 51520000000 | tf_op jit(solution)/shard_map/weight_grad/pallas_call | solution.py:82
  311.6 16.3 %feed_forward_back.3 = (bf16[2,768,2560]{2,1,0:T(8,128)(2,1)}, f32[384,960]{1,0:T(8,128)S(1)}, bf16[384,960]{1,0:T(8,128)(2,1)S(1)}, bf16[960,384]{1,0:T(8,128)(2,1)S(1)}) custom-call(f32[384,960]{1,0:T(8,128)S(1)} %get-tuple-element.293.refs_0_, f32[384,960]{1,0:T(8,128)} %copy-done.88, f32[1,960]{1,0:T(1,128)S(1)} %copy-done.35, ...), custom_call_target="tpu_custom_call", output_to_operand_aliasing={{0}: (9, {})} | custom-call | flops 165600002048 | tf_op jit(solution)/shard_map/feed_forward_back/pallas_call | solution.py:82
  329.1 9.4 %weight_grad.8 = (bf16[4,4,240,640]{3,2,1,0:T(8,128)(2,1)}, f32[8,128]{1,0:T(8,128)}) custom-call(s32[4]{0:T(128)} %pad_add_fusion.3.refs_0_, bf16[960,768]{1,0:T(8,128)(2,1)} %copy-done.84, bf16[2,768,2560]{2,1,0:T(8,128)(2,1)} %get-tuple-element.213.refs_2_), custom_call_target="tpu_custom_call" | custom-call | flops 80959995904 | tf_op jit(solution)/shard_map/weight_grad/pallas_call | solution.py:82
  341.6 2.6 attend_back.12
  347.1 3.6 collective-permute-done.41
  353.0 10.8 %weight_grad.9 = (bf16[2,4,240,640]{3,2,1,0:T(8,128)(2,1)}, bf16[2,4,240,640]{3,2,1,0:T(8,128)(2,1)}, f32[8,128]{1,0:T(8,128)}) custom-call(s32[4]{0:T(128)} %pad_add_fusion.2.refs_0_, bf16[960,768]{1,0:T(8,128)(2,1)} %copy-done.84, bf16[2,768,2560]{2,1,0:T(8,128)(2,1)} %get-tuple-element.213.refs_2_, ...), custom_call_target="tpu_custom_call" | custom-call | flops 80959995904 | tf_op jit(solution)/shard_map/weight_grad/pallas_call | solution.py:82
  373.5 20.4 %collective-permute-done.43 = bf16[2,4,240,640]{3,2,1,0:T(8,128)(2,1)S(1)} collective-permute-done((bf16[2,4,240,640]{3,2,1,0:T(8,128)(2,1)}, bf16[2,4,240,640]{3,2,1,0:T(8,128)(2,1)S(1)}, u32[]{:S(2)}, u32[]{:S(2)}) %collective-permute-start.43) | collective-permute-done | bytes 2457632 | tf_op jit(solution)/shard_map/ppermute | solution.py:35
  395.8 7.6 %collective-permute-start.51 = (bf16[80,960]{1,0:T(8,128)(2,1)S(1)}, bf16[80,960]{1,0:T(8,128)(2,1)S(1)}, u32[]{:S(2)}, u32[]{:S(2)}) collective-permute-start(bf16[80,960]{1,0:T(8,128)(2,1)S(1)} %copy-done.118), channel_id=1, source_target_pairs={{0,1},{1,2},{2,3},{3,0},{4,5},{5,6},{6,7},{7,4},{8,9},{9,10},{10,1... | collective-permute-start | bytes 460808 | tf_op jit(solution)/shard_map/ppermute | solution.py:57
  403.4 3.7 collective-permute-start.52
  407.5 7.2 %attend_back.15 = (bf16[960,384]{1,0:T(8,128)(2,1)S(1)}, bf16[320,384]{1,0:T(8,128)(2,1)S(1)}, bf16[320,384]{1,0:T(8,128)(2,1)S(1)}) custom-call(s32[2]{0:T(128)S(1)} %copy-done.68, bf16[960,384]{1,0:T(8,128)(2,1)S(1)} %copy-done.73, bf16[960,384]{1,0:T(8,128)(2,1)S(1)} %copy-done.20, bf16[960,384]{1,0:T(8,128)(2,1)S(1)} %copy-done.86, ...), custom_call_target="tpu_custom_call" | custom-call | flops 64399998976 | tf_op jit(solution)/shard_map/attend_back/pallas_call | solution.py:82
  415.4 2.9 collective-permute-done.52
  420.4 5.7 %weight_grad.10 = (bf16[4,4,120,640]{3,2,1,0:T(8,128)(2,1)S(1)}, f32[8,128]{1,0:T(8,128)S(1)}) custom-call(s32[4]{0:T(128)S(1)} %copy-done.37, bf16[2,4,2,128,768]{4,3,2,1,0:T(8,128)(2,1)S(1)} %copy-done, bf16[2,4,2,128,768]{4,3,2,1,0:T(8,128)(2,1)S(1)} %copy-done, bf16[384,2560]{1,0:T(8,128)(2,1)S(1)} %copy-done.4, ...), custom_call_target="tpu_custom_call" | custom-call | flops 73600000000 | tf_op jit(solution)/shard_map/weight_grad/pallas_call | solution.py:82
  428.3 6.4 %weight_grad.11 = (bf16[4,4,120,640]{3,2,1,0:T(8,128)(2,1)S(1)}, f32[8,128]{1,0:T(8,128)}) custom-call(s32[4]{0:T(128)S(1)} %copy-done.36, bf16[2,4,2,128,768]{4,3,2,1,0:T(8,128)(2,1)S(1)} %copy-done, bf16[2,4,2,128,768]{4,3,2,1,0:T(8,128)(2,1)S(1)} %copy-done, bf16[384,2560]{1,0:T(8,128)(2,1)S(1)} %copy-done.4, ...), custom_call_target="tpu_custom_call" | custom-call | flops 368000000 | tf_op jit(solution)/shard_map/weight_grad/pallas_call | solution.py:82
  436.5 3.3 collective-permute-start.58
  441.7 6.9 %collective-permute-done.58 = bf16[240,640]{1,0:T(8,128)(2,1)S(1)} collective-permute-done((bf16[240,640]{1,0:T(8,128)(2,1)S(1)}, bf16[240,640]{1,0:T(8,128)(2,1)S(1)}, u32[]{:S(2)}, u32[]{:S(2)}) %collective-permute-start.58) | collective-permute-done | bytes 307232 | tf_op jit(solution)/shard_map/ppermute | solution.py:57
  448.6 5.2 collective-permute-done.59
  457.5 2.4 copy.37
  461.5 4.1 collective-permute-done.61
  467.5 9.3 %collective-permute-done.62 = bf16[240,640]{1,0:T(8,128)(2,1)S(1)} collective-permute-done((bf16[240,640]{1,0:T(8,128)(2,1)}, bf16[240,640]{1,0:T(8,128)(2,1)S(1)}, u32[]{:S(2)}, u32[]{:S(2)}) %collective-permute-start.62) | collective-permute-done | bytes 307232 | tf_op jit(solution)/shard_map/ppermute | solution.py:57
  477.5 3.7 multiply_reduce_fusion.2
  486.3 2.6 collective-permute-done.65
  488.9 7.6 %collective-permute-done.64 = bf16[120,640]{1,0:T(8,128)(2,1)S(1)} collective-permute-done((bf16[120,640]{1,0:T(8,128)(2,1)S(1)}, bf16[120,640]{1,0:T(8,128)(2,1)S(1)}, u32[]{:S(2)}, u32[]{:S(2)}) %collective-permute-start.64) | collective-permute-done | bytes 153632 | tf_op jit(solution)/shard_map/ppermute | solution.py:57
  505.0 2.4 spread.5
  509.7 2.6 spread.3
  517.0 2.3 spread.4
  (532 shorter events, 165.6 us)
Async XLA Ops:
  7.2 63.4 %all-gather.3.cloned.1.call-start = ((), (), s32[]{:S(2)}) async-start(), calls=%async_computation | async-start | bytes 2560000 | tf_op jit(solution)/shard_map/all_gather | solution.py:914
  15.7 19.8 %collective-permute-start.2 = (bf16[144,640]{1,0:T(8,128)(2,1)S(1)}, bf16[144,640]{1,0:T(8,128)(2,1)S(1)}, u32[]{:S(2)}, u32[]{:S(2)}) collective-permute-start(bf16[144,640]{1,0:T(8,128)(2,1)S(1)} %fusion.31), channel_id=1, source_target_pairs={{0,1},{1,2},{2,3},{3,0},{4,5},{5,6},{6,7},{7,4},{8,9},{9,10},{10,1... | collective-permute-start | bytes 552968 | tf_op jit(solution)/shard_map/ppermute | solution.py:57
  18.8 16.7 %collective-permute-start.1 = (bf16[144,640]{1,0:T(8,128)(2,1)S(1)}, bf16[144,640]{1,0:T(8,128)(2,1)S(1)}, u32[]{:S(2)}, u32[]{:S(2)}) collective-permute-start(bf16[144,640]{1,0:T(8,128)(2,1)S(1)} %fusion.31), channel_id=1, source_target_pairs={{0,2},{1,3},{2,0},{3,1},{4,6},{5,7},{6,4},{7,5},{8,10},{9,11},{10,... | collective-permute-start | bytes 552968 | tf_op jit(solution)/shard_map/ppermute | solution.py:57
  21.3 13.2 %collective-permute-start = (bf16[144,640]{1,0:T(8,128)(2,1)S(1)}, bf16[144,640]{1,0:T(8,128)(2,1)}, u32[]{:S(2)}, u32[]{:S(2)}) collective-permute-start(bf16[144,640]{1,0:T(8,128)(2,1)S(1)} %fusion.31), channel_id=1, source_target_pairs={{0,3},{1,0},{2,1},{3,2},{4,7},{5,4},{6,5},{7,6},{8,11},{9,8},{10,9... | collective-permute-start | bytes 552968 | tf_op jit(solution)/shard_map/ppermute | solution.py:57
  36.9 14.2 %collective-permute-start.3 = (bf16[3,128,640]{2,1,0:T(8,128)(2,1)S(1)}, bf16[3,128,640]{2,1,0:T(8,128)(2,1)}, u32[]{:S(2)}, u32[]{:S(2)}) collective-permute-start(bf16[3,128,640]{2,1,0:T(8,128)(2,1)S(1)} %pad_maximum_fusion.3.refs_1_), channel_id=1, source_target_pairs={{0,8},{4,20},{8,0},{12,28},{16,24},{20,4},{24,16},{28,12},{1,9},{5... | collective-permute-start | bytes 1474568 | tf_op jit(solution)/shard_map/ppermute | solution.py:35
  38.5 19.5 %collective-permute-start.4 = (bf16[3,128,640]{2,1,0:T(8,128)(2,1)S(1)}, bf16[3,128,640]{2,1,0:T(8,128)(2,1)}, u32[]{:S(2)}, u32[]{:S(2)}) collective-permute-start(bf16[3,128,640]{2,1,0:T(8,128)(2,1)S(1)} %pad_maximum_fusion.3.refs_1_), channel_id=1, source_target_pairs={{0,16},{4,12},{8,24},{12,4},{16,0},{20,28},{24,8},{28,20},{1,17},{... | collective-permute-start | bytes 1474568 | tf_op jit(solution)/shard_map/ppermute | solution.py:35
  40.0 33.1 %collective-permute-start.6 = (bf16[3,128,640]{2,1,0:T(8,128)(2,1)S(1)}, bf16[3,128,640]{2,1,0:T(8,128)(2,1)}, u32[]{:S(2)}, u32[]{:S(2)}) collective-permute-start(bf16[3,128,640]{2,1,0:T(8,128)(2,1)S(1)} %pad_maximum_fusion.3.refs_1_), channel_id=1, source_target_pairs={{0,4},{4,0},{8,12},{12,8},{16,20},{20,16},{24,28},{28,24},{1,5},{5... | collective-permute-start | bytes 1474568 | tf_op jit(solution)/shard_map/ppermute | solution.py:35
  58.0 15.2 %collective-permute-start.7 = (bf16[3,128,640]{2,1,0:T(8,128)(2,1)}, bf16[3,128,640]{2,1,0:T(8,128)(2,1)}, u32[]{:S(2)}, u32[]{:S(2)}) collective-permute-start(bf16[3,128,640]{2,1,0:T(8,128)(2,1)} %collective-permute-done.3.refs_2_), channel_id=1, source_target_pairs={{0,4},{4,0},{8,12},{12,8},{16,20},{20,16},{24,28},{28,24},{1,5},{5... | collective-permute-start | bytes 1474568 | tf_op jit(solution)/shard_map/ppermute | solution.py:35
  58.0 15.2 %collective-permute-start.8 = (bf16[3,128,640]{2,1,0:T(8,128)(2,1)}, bf16[3,128,640]{2,1,0:T(8,128)(2,1)}, u32[]{:S(2)}, u32[]{:S(2)}) collective-permute-start(bf16[3,128,640]{2,1,0:T(8,128)(2,1)} %collective-permute-done.4.refs_3_), channel_id=1, source_target_pairs={{0,4},{4,0},{8,12},{12,8},{16,20},{20,16},{24,28},{28,24},{1,5},{5... | collective-permute-start | bytes 1474568 | tf_op jit(solution)/shard_map/ppermute | solution.py:35
  60.3 12.9 %collective-permute-start.9 = (bf16[3,128,640]{2,1,0:T(8,128)(2,1)}, bf16[3,128,640]{2,1,0:T(8,128)(2,1)}, u32[]{:S(2)}, u32[]{:S(2)}) collective-permute-start(bf16[3,128,640]{2,1,0:T(8,128)(2,1)} %collective-permute-done.5.refs_4_), channel_id=1, source_target_pairs={{0,4},{4,0},{8,12},{12,8},{16,20},{20,16},{24,28},{28,24},{1,5},{5... | collective-permute-start | bytes 1474568 | tf_op jit(solution)/shard_map/ppermute | solution.py:35
  77.7 17.8 %collective-permute-start.10 = (bf16[640,384]{1,0:T(8,128)(2,1)S(1)}, bf16[640,384]{1,0:T(8,128)(2,1)S(1)}, u32[]{:S(2)}, u32[]{:S(2)}) collective-permute-start(bf16[640,384]{1,0:T(8,128)(2,1)S(1)} %keys_values.2.refs_4_.refs_2_.refs_5_.refs_6_), channel_id=1, source_target_pairs={{0,1},{1,2},{2,3},{4,5},{5,6},{6,7},{8,9},{9,10},{10,11},{12,13},{... | collective-permute-start | bytes 1474568 | tf_op jit(solution)/shard_map/ppermute | solution.py:40
  84.4 33.8 %collective-permute-start.13 = (bf16[3,240,640]{2,1,0:T(8,128)(2,1)S(1)}, bf16[3,240,640]{2,1,0:T(8,128)(2,1)S(1)}, u32[]{:S(2)}, u32[]{:S(2)}) collective-permute-start(bf16[3,240,640]{2,1,0:T(8,128)(2,1)S(1)} %pad_maximum_fusion.2.refs_10_.refs_1_), channel_id=1, source_target_pairs={{0,8},{4,20},{8,0},{12,28},{16,24},{20,4},{24,16},{28,12},{1,9},{5... | collective-permute-start | bytes 2764808 | tf_op jit(solution)/shard_map/ppermute | solution.py:35
  84.7 33.5 %collective-permute-start.14 = (bf16[3,240,640]{2,1,0:T(8,128)(2,1)S(1)}, bf16[3,240,640]{2,1,0:T(8,128)(2,1)S(1)}, u32[]{:S(2)}, u32[]{:S(2)}) collective-permute-start(bf16[3,240,640]{2,1,0:T(8,128)(2,1)S(1)} %pad_maximum_fusion.2.refs_10_.refs_1_), channel_id=1, source_target_pairs={{0,16},{4,12},{8,24},{12,4},{16,0},{20,28},{24,8},{28,20},{1,17},{... | collective-permute-start | bytes 2764808 | tf_op jit(solution)/shard_map/ppermute | solution.py:35
  85.4 32.3 %collective-permute-start.15 = (bf16[3,80,960]{2,1,0:T(8,128)(2,1)S(1)}, bf16[3,80,960]{2,1,0:T(8,128)(2,1)S(1)}, u32[]{:S(2)}, u32[]{:S(2)}) collective-permute-start(bf16[3,80,960]{2,1,0:T(8,128)(2,1)S(1)} %pad_maximum_fusion.4.refs_11_.refs_1_), channel_id=1, source_target_pairs={{0,8},{4,20},{8,0},{12,28},{16,24},{20,4},{24,16},{28,12},{1,9},{5... | collective-permute-start | bytes 1382408 | tf_op jit(solution)/shard_map/ppermute | solution.py:35
  87.2 30.5 %collective-permute-start.16 = (bf16[3,80,960]{2,1,0:T(8,128)(2,1)S(1)}, bf16[3,80,960]{2,1,0:T(8,128)(2,1)S(1)}, u32[]{:S(2)}, u32[]{:S(2)}) collective-permute-start(bf16[3,80,960]{2,1,0:T(8,128)(2,1)S(1)} %pad_maximum_fusion.4.refs_11_.refs_1_), channel_id=1, source_target_pairs={{0,16},{4,12},{8,24},{12,4},{16,0},{20,28},{24,8},{28,20},{1,17},{... | collective-permute-start | bytes 1382408 | tf_op jit(solution)/shard_map/ppermute | solution.py:35
  95.5 24.7 %collective-permute-start.11 = (bf16[640,384]{1,0:T(8,128)(2,1)S(1)}, bf16[640,384]{1,0:T(8,128)(2,1)S(1)}, u32[]{:S(2)}, u32[]{:S(2)}) collective-permute-start(bf16[640,384]{1,0:T(8,128)(2,1)S(1)} %collective-permute-done.10.refs_2_.refs_5_.refs_6_), channel_id=1, source_target_pairs={{1,2},{2,3},{5,6},{6,7},{9,10},{10,11},{13,14},{14,15},{17,18},{18... | collective-permute-start | bytes 1474568 | tf_op jit(solution)/shard_map/ppermute | solution.py:40
  117.7 26.0 %collective-permute-start.19 = (bf16[3,240,640]{2,1,0:T(8,128)(2,1)S(1)}, bf16[3,240,640]{2,1,0:T(8,128)(2,1)S(1)}, u32[]{:S(2)}, u32[]{:S(2)}) collective-permute-start(bf16[3,240,640]{2,1,0:T(8,128)(2,1)S(1)} %pad_maximum_fusion.2.refs_10_.refs_1_), channel_id=1, source_target_pairs={{0,4},{4,0},{8,12},{12,8},{16,20},{20,16},{24,28},{28,24},{1,5},{5... | collective-permute-start | bytes 2764808 | tf_op jit(solution)/shard_map/ppermute | solution.py:35
  117.7 21.5 %collective-permute-start.23 = (bf16[3,80,960]{2,1,0:T(8,128)(2,1)S(1)}, bf16[3,80,960]{2,1,0:T(8,128)(2,1)S(1)}, u32[]{:S(2)}, u32[]{:S(2)}) collective-permute-start(bf16[3,80,960]{2,1,0:T(8,128)(2,1)S(1)} %pad_maximum_fusion.4.refs_11_.refs_1_), channel_id=1, source_target_pairs={{0,4},{4,0},{8,12},{12,8},{16,20},{20,16},{24,28},{28,24},{1,5},{5... | collective-permute-start | bytes 1382408 | tf_op jit(solution)/shard_map/ppermute | solution.py:35
  118.2 18.7 %collective-permute-start.17 = (bf16[3,240,640]{2,1,0:T(8,128)(2,1)S(1)}, bf16[3,240,640]{2,1,0:T(8,128)(2,1)S(1)}, u32[]{:S(2)}, u32[]{:S(2)}) collective-permute-start(bf16[3,240,640]{2,1,0:T(8,128)(2,1)S(1)} %collective-permute-done.13.refs_2_), channel_id=1, source_target_pairs={{0,16},{4,12},{8,24},{12,4},{16,0},{20,28},{24,8},{28,20},{1,17},{... | collective-permute-start | bytes 2764808 | tf_op jit(solution)/shard_map/ppermute | solution.py:35
  119.2 17.7 %collective-permute-start.18 = (bf16[3,80,960]{2,1,0:T(8,128)(2,1)S(1)}, bf16[3,80,960]{2,1,0:T(8,128)(2,1)S(1)}, u32[]{:S(2)}, u32[]{:S(2)}) collective-permute-start(bf16[3,80,960]{2,1,0:T(8,128)(2,1)S(1)} %collective-permute-done.15.refs_2_), channel_id=1, source_target_pairs={{0,16},{4,12},{8,24},{12,4},{16,0},{20,28},{24,8},{28,20},{1,17},{... | collective-permute-start | bytes 1382408 | tf_op jit(solution)/shard_map/ppermute | solution.py:35
  120.2 17.2 %collective-permute-start.12 = (bf16[640,384]{1,0:T(8,128)(2,1)S(1)}, bf16[640,384]{1,0:T(8,128)(2,1)S(1)}, u32[]{:S(2)}, u32[]{:S(2)}) collective-permute-start(bf16[640,384]{1,0:T(8,128)(2,1)S(1)} %collective-permute-done.11.refs_2_.refs_5_.refs_6_), channel_id=1, source_target_pairs={{2,3},{6,7},{10,11},{14,15},{18,19},{22,23},{26,27},{30,31}} | collective-permute-start | bytes 1474568 | tf_op jit(solution)/shard_map/ppermute | solution.py:40
  171.3 12.2 %collective-permute-start.27 = (bf16[320,384]{1,0:T(8,128)(2,1)S(1)}, bf16[320,384]{1,0:T(8,128)(2,1)S(1)}, u32[]{:S(2)}, u32[]{:S(2)}) collective-permute-start(bf16[320,384]{1,0:T(8,128)(2,1)S(1)} %get-tuple-element.168.refs_4_.refs_2_.refs_5_), channel_id=1, source_target_pairs={{0,1},{1,2},{2,3},{4,5},{5,6},{6,7},{8,9},{9,10},{10,11},{12,13},{... | collective-permute-start | bytes 737288 | tf_op jit(solution)/shard_map/ppermute | solution.py:40
  173.5 11.0 %collective-permute-start.30 = (bf16[320,384]{1,0:T(8,128)(2,1)S(1)}, bf16[320,384]{1,0:T(8,128)(2,1)S(1)}, u32[]{:S(2)}, u32[]{:S(2)}) collective-permute-start(bf16[320,384]{1,0:T(8,128)(2,1)S(1)} %get-tuple-element.169.refs_3_.refs_6_), channel_id=1, source_target_pairs={{0,1},{1,2},{2,3},{4,5},{5,6},{6,7},{8,9},{9,10},{10,11},{12,13},{... | collective-permute-start | bytes 737288 | tf_op jit(solution)/shard_map/ppermute | solution.py:40
  236.7 42.9 %collective-permute-start.35 = (bf16[320,384]{1,0:T(8,128)(2,1)S(1)}, bf16[320,384]{1,0:T(8,128)(2,1)S(1)}, u32[]{:S(2)}, u32[]{:S(2)}) collective-permute-start(bf16[320,384]{1,0:T(8,128)(2,1)S(1)} %add_convert_fusion.15), channel_id=1, source_target_pairs={{1,0},{2,1},{3,2},{5,4},{6,5},{7,6},{9,8},{10,9},{11,10},{13,12},{... | collective-permute-start | bytes 737288 | tf_op jit(solution)/shard_map/ppermute | solution.py:849
  238.2 45.9 %collective-permute-start.38 = (bf16[320,384]{1,0:T(8,128)(2,1)S(1)}, bf16[320,384]{1,0:T(8,128)(2,1)S(1)}, u32[]{:S(2)}, u32[]{:S(2)}) collective-permute-start(bf16[320,384]{1,0:T(8,128)(2,1)S(1)} %add_convert_fusion.13), channel_id=1, source_target_pairs={{1,0},{2,1},{3,2},{5,4},{6,5},{7,6},{9,8},{10,9},{11,10},{13,12},{... | collective-permute-start | bytes 737288 | tf_op jit(solution)/shard_map/ppermute | solution.py:849
  308.7 29.8 %collective-permute-start.40 = (bf16[2,4,80,960]{3,2,1,0:T(8,128)(2,1)}, bf16[2,4,80,960]{3,2,1,0:T(8,128)(2,1)}, u32[]{:S(2)}, u32[]{:S(2)}) collective-permute-start(bf16[2,4,80,960]{3,2,1,0:T(8,128)(2,1)} %get-tuple-element.202), channel_id=1, source_target_pairs={{0,8},{4,20},{8,0},{12,28},{16,24},{20,4},{24,16},{28,12},{1,9},{5... | collective-permute-start | bytes 3686408 | tf_op jit(solution)/shard_map/ppermute | solution.py:35
  338.4 14.5 %collective-permute-start.42 = (bf16[4,4,240,640]{3,2,1,0:T(8,128)(2,1)}, bf16[4,4,240,640]{3,2,1,0:T(8,128)(2,1)}, u32[]{:S(2)}, u32[]{:S(2)}) collective-permute-start(bf16[4,4,240,640]{3,2,1,0:T(8,128)(2,1)} %get-tuple-element.219), channel_id=1, source_target_pairs={{0,4},{4,0},{8,12},{12,8},{16,20},{20,16},{24,28},{28,24},{1,5},{5... | collective-permute-start | bytes 14745608 | tf_op jit(solution)/shard_map/ppermute | solution.py:35
  340.0 10.7 %collective-permute-start.41 = (bf16[4,80,960]{2,1,0:T(8,128)(2,1)S(1)}, bf16[4,80,960]{2,1,0:T(8,128)(2,1)S(1)}, u32[]{:S(2)}, u32[]{:S(2)}) collective-permute-start(bf16[4,80,960]{2,1,0:T(8,128)(2,1)S(1)} %fusion.25), channel_id=1, source_target_pairs={{0,16},{4,12},{8,24},{12,4},{16,0},{20,28},{24,8},{28,20},{1,17},{... | collective-permute-start | bytes 1843208 | tf_op jit(solution)/shard_map/ppermute | solution.py:35
  344.2 22.3 %collective-permute-start.44 = (bf16[320,384]{1,0:T(8,128)(2,1)}, bf16[320,384]{1,0:T(8,128)(2,1)}, u32[]{:S(2)}, u32[]{:S(2)}) collective-permute-start(bf16[320,384]{1,0:T(8,128)(2,1)} %get-tuple-element.233), channel_id=1, source_target_pairs={{3,2},{7,6},{11,10},{15,14},{19,18},{23,22},{27,26},{31,30}} | collective-permute-start | bytes 737288 | tf_op jit(solution)/shard_map/ppermute | solution.py:849
  345.6 22.7 %collective-permute-start.47 = (bf16[320,384]{1,0:T(8,128)(2,1)}, bf16[320,384]{1,0:T(8,128)(2,1)}, u32[]{:S(2)}, u32[]{:S(2)}) collective-permute-start(bf16[320,384]{1,0:T(8,128)(2,1)} %get-tuple-element.236), channel_id=1, source_target_pairs={{3,2},{7,6},{11,10},{15,14},{19,18},{23,22},{27,26},{31,30}} | collective-permute-start | bytes 737288 | tf_op jit(solution)/shard_map/ppermute | solution.py:849
  363.8 30.1 %collective-permute-start.43 = (bf16[2,4,240,640]{3,2,1,0:T(8,128)(2,1)}, bf16[2,4,240,640]{3,2,1,0:T(8,128)(2,1)S(1)}, u32[]{:S(2)}, u32[]{:S(2)}) collective-permute-start(bf16[2,4,240,640]{3,2,1,0:T(8,128)(2,1)} %get-tuple-element.223), channel_id=1, source_target_pairs={{0,8},{4,20},{8,0},{12,28},{16,24},{20,4},{24,16},{28,12},{1,9},{5... | collective-permute-start | bytes 7372808 | tf_op jit(solution)/shard_map/ppermute | solution.py:35
  370.9 36.2 %collective-permute-start.46 = (bf16[320,384]{1,0:T(8,128)(2,1)S(1)}, bf16[320,384]{1,0:T(8,128)(2,1)S(1)}, u32[]{:S(2)}, u32[]{:S(2)}) collective-permute-start(bf16[320,384]{1,0:T(8,128)(2,1)S(1)} %add_convert_fusion.11), channel_id=1, source_target_pairs={{1,0},{2,1},{3,2},{5,4},{6,5},{7,6},{9,8},{10,9},{11,10},{13,12},{... | collective-permute-start | bytes 737288 | tf_op jit(solution)/shard_map/ppermute | solution.py:849
  372.2 42.5 %collective-permute-start.49 = (bf16[320,384]{1,0:T(8,128)(2,1)S(1)}, bf16[320,384]{1,0:T(8,128)(2,1)S(1)}, u32[]{:S(2)}, u32[]{:S(2)}) collective-permute-start(bf16[320,384]{1,0:T(8,128)(2,1)S(1)} %add_convert_fusion.9), channel_id=1, source_target_pairs={{1,0},{2,1},{3,2},{5,4},{6,5},{7,6},{9,8},{10,9},{11,10},{13,12},{... | collective-permute-start | bytes 737288 | tf_op jit(solution)/shard_map/ppermute | solution.py:849
  394.3 24.0 %collective-permute-start.50 = (bf16[4,240,640]{2,1,0:T(8,128)(2,1)S(1)}, bf16[4,240,640]{2,1,0:T(8,128)(2,1)S(1)}, u32[]{:S(2)}, u32[]{:S(2)}) collective-permute-start(bf16[4,240,640]{2,1,0:T(8,128)(2,1)S(1)} %fusion.20), channel_id=1, source_target_pairs={{0,16},{4,12},{8,24},{12,4},{16,0},{20,28},{24,8},{28,20},{1,17},{... | collective-permute-start | bytes 3686408 | tf_op jit(solution)/shard_map/ppermute | solution.py:35
  395.8 19.5 %collective-permute-start.51 = (bf16[80,960]{1,0:T(8,128)(2,1)S(1)}, bf16[80,960]{1,0:T(8,128)(2,1)S(1)}, u32[]{:S(2)}, u32[]{:S(2)}) collective-permute-start(bf16[80,960]{1,0:T(8,128)(2,1)S(1)} %copy-done.118), channel_id=1, source_target_pairs={{0,1},{1,2},{2,3},{3,0},{4,5},{5,6},{6,7},{7,4},{8,9},{9,10},{10,1... | collective-permute-start | bytes 460808 | tf_op jit(solution)/shard_map/ppermute | solution.py:57
  403.4 14.8 %collective-permute-start.52 = (bf16[80,960]{1,0:T(8,128)(2,1)S(1)}, bf16[80,960]{1,0:T(8,128)(2,1)S(1)}, u32[]{:S(2)}, u32[]{:S(2)}) collective-permute-start(bf16[80,960]{1,0:T(8,128)(2,1)S(1)} %copy-done.117), channel_id=1, source_target_pairs={{0,2},{1,3},{2,0},{3,1},{4,6},{5,7},{6,4},{7,5},{8,10},{9,11},{10,... | collective-permute-start | bytes 460808 | tf_op jit(solution)/shard_map/ppermute | solution.py:57
  407.1 11.2 %collective-permute-start.53 = (bf16[80,960]{1,0:T(8,128)(2,1)S(1)}, bf16[80,960]{1,0:T(8,128)(2,1)S(1)}, u32[]{:S(2)}, u32[]{:S(2)}) collective-permute-start(bf16[80,960]{1,0:T(8,128)(2,1)S(1)} %copy-done.116), channel_id=1, source_target_pairs={{0,3},{1,0},{2,1},{3,2},{4,7},{5,4},{6,5},{7,6},{8,11},{9,8},{10,9... | collective-permute-start | bytes 460808 | tf_op jit(solution)/shard_map/ppermute | solution.py:57
  435.4 18.5 %collective-permute-start.57 = (bf16[2,4,120,640]{3,2,1,0:T(8,128)(2,1)S(1)}, bf16[2,4,120,640]{3,2,1,0:T(8,128)(2,1)S(1)}, u32[]{:S(2)}, u32[]{:S(2)}) collective-permute-start(bf16[2,4,120,640]{3,2,1,0:T(8,128)(2,1)S(1)} %add_convert_fusion), channel_id=1, source_target_pairs={{0,8},{4,20},{8,0},{12,28},{16,24},{20,4},{24,16},{28,12},{1,9},{5... | collective-permute-start | bytes 3686408 | tf_op jit(solution)/shard_map/ppermute | solution.py:35
  436.5 12.1 %collective-permute-start.58 = (bf16[240,640]{1,0:T(8,128)(2,1)S(1)}, bf16[240,640]{1,0:T(8,128)(2,1)S(1)}, u32[]{:S(2)}, u32[]{:S(2)}) collective-permute-start(bf16[240,640]{1,0:T(8,128)(2,1)S(1)} %get-tuple-element.305), channel_id=1, source_target_pairs={{0,1},{1,2},{2,3},{3,0},{4,5},{5,6},{6,7},{7,4},{8,9},{9,10},{10,1... | collective-permute-start | bytes 921608 | tf_op jit(solution)/shard_map/ppermute | solution.py:57
  439.7 14.0 %collective-permute-start.59 = (bf16[240,640]{1,0:T(8,128)(2,1)S(1)}, bf16[240,640]{1,0:T(8,128)(2,1)S(1)}, u32[]{:S(2)}, u32[]{:S(2)}) collective-permute-start(bf16[240,640]{1,0:T(8,128)(2,1)S(1)} %get-tuple-element.304), channel_id=1, source_target_pairs={{0,3},{1,0},{2,1},{3,2},{4,7},{5,4},{6,5},{7,6},{8,11},{9,8},{10,9... | collective-permute-start | bytes 921608 | tf_op jit(solution)/shard_map/ppermute | solution.py:57
  440.4 13.6 %collective-permute-start.60 = (bf16[80,960]{1,0:T(8,128)(2,1)S(1)}, bf16[80,960]{1,0:T(8,128)(2,1)S(1)}, u32[]{:S(2)}, u32[]{:S(2)}) collective-permute-start(bf16[80,960]{1,0:T(8,128)(2,1)S(1)} %collective-permute-done.55.refs_3_), channel_id=1, source_target_pairs={{0,8},{4,20},{8,0},{12,28},{16,24},{20,4},{24,16},{28,12},{1,9},{5... | collective-permute-start | bytes 460808 | tf_op jit(solution)/shard_map/ppermute | solution.py:35
  455.2 10.5 %collective-permute-start.61 = (bf16[4,120,640]{2,1,0:T(8,128)(2,1)}, bf16[4,120,640]{2,1,0:T(8,128)(2,1)}, u32[]{:S(2)}, u32[]{:S(2)}) collective-permute-start(bf16[4,120,640]{2,1,0:T(8,128)(2,1)} %fusion.28), channel_id=1, source_target_pairs={{0,16},{4,12},{8,24},{12,4},{16,0},{20,28},{24,8},{28,20},{1,17},{... | collective-permute-start | bytes 1843208 | tf_op jit(solution)/shard_map/ppermute | solution.py:35
  459.9 16.8 %collective-permute-start.62 = (bf16[240,640]{1,0:T(8,128)(2,1)}, bf16[240,640]{1,0:T(8,128)(2,1)S(1)}, u32[]{:S(2)}, u32[]{:S(2)}) collective-permute-start(bf16[240,640]{1,0:T(8,128)(2,1)} %get-tuple-element.303), channel_id=1, source_target_pairs={{0,2},{1,3},{2,0},{3,1},{4,6},{5,7},{6,4},{7,5},{8,10},{9,11},{10,... | collective-permute-start | bytes 921608 | tf_op jit(solution)/shard_map/ppermute | solution.py:57
  481.2 15.8 %collective-permute-start.66 = (bf16[240,640]{1,0:T(8,128)(2,1)S(1)}, bf16[240,640]{1,0:T(8,128)(2,1)S(1)}, u32[]{:S(2)}, u32[]{:S(2)}) collective-permute-start(bf16[240,640]{1,0:T(8,128)(2,1)S(1)} %add_convert_fusion.8.refs_1_), channel_id=1, source_target_pairs={{0,8},{4,20},{8,0},{12,28},{16,24},{20,4},{24,16},{28,12},{1,9},{5... | collective-permute-start | bytes 921608 | tf_op jit(solution)/shard_map/ppermute | solution.py:35
  484.1 12.4 %collective-permute-start.64 = (bf16[120,640]{1,0:T(8,128)(2,1)S(1)}, bf16[120,640]{1,0:T(8,128)(2,1)S(1)}, u32[]{:S(2)}, u32[]{:S(2)}) collective-permute-start(bf16[120,640]{1,0:T(8,128)(2,1)S(1)} %get-tuple-element.257), channel_id=1, source_target_pairs={{0,2},{1,3},{2,0},{3,1},{4,6},{5,7},{6,4},{7,5},{8,10},{9,11},{10,... | collective-permute-start | bytes 460808 | tf_op jit(solution)/shard_map/ppermute | solution.py:57
  484.1 12.4 %collective-permute-start.63 = (bf16[120,640]{1,0:T(8,128)(2,1)S(1)}, bf16[120,640]{1,0:T(8,128)(2,1)S(1)}, u32[]{:S(2)}, u32[]{:S(2)}) collective-permute-start(bf16[120,640]{1,0:T(8,128)(2,1)S(1)} %get-tuple-element.256), channel_id=1, source_target_pairs={{0,1},{1,2},{2,3},{3,0},{4,5},{5,6},{6,7},{7,4},{8,9},{9,10},{10,1... | collective-permute-start | bytes 460808 | tf_op jit(solution)/shard_map/ppermute | solution.py:57
  485.1 12.2 %collective-permute-start.68 = (bf16[240,640]{1,0:T(8,128)(2,1)S(1)}, bf16[240,640]{1,0:T(8,128)(2,1)S(1)}, u32[]{:S(2)}, u32[]{:S(2)}) collective-permute-start(bf16[240,640]{1,0:T(8,128)(2,1)S(1)} %collective-permute-done.67.refs_3_), channel_id=1, source_target_pairs={{0,8},{4,20},{8,0},{12,28},{16,24},{20,4},{24,16},{28,12},{1,9},{5... | collective-permute-start | bytes 921608 | tf_op jit(solution)/shard_map/ppermute | solution.py:35
  488.9 15.1 %collective-permute-start.80 = (bf16[80,960]{1,0:T(8,128)(2,1)S(1)}, bf16[80,960]{1,0:T(8,128)(2,1)S(1)}, u32[]{:S(2)}, u32[]{:S(2)}) collective-permute-start(bf16[80,960]{1,0:T(8,128)(2,1)S(1)} %copy-done.33), channel_id=1, source_target_pairs={{0,4},{4,0},{8,12},{12,8},{16,20},{20,16},{24,28},{28,24},{1,5},{5... | collective-permute-start | bytes 460808 | tf_op jit(solution)/shard_map/ppermute | solution.py:35
  (170 other events, 1566.4 us)
Sparse Core Ops, SparseCore 0:
  23.9 46.6 all-gather.2
